TPU v7x, 512 devices: a whole 4x4x16 slice. The times are simulated.
512 devices in a mesh: row: 16 (over z_hi, y), col: 16 (over x, z_lo), pair: 2 (over core).
Axes of the slice: x: 4, y: 4, z: 16 (z_hi: 4, z_lo: 4; z = z_hi * 4 + z_lo), core: 2. Of those that a mesh axis runs over, the one named last changes fastest.
Arguments:
- amplitudes: bfloat16 [24576, 2048], P(('row', 'col'), 'pair'), may hold values from -6 to 6
- integrals: bfloat16 [24576, 24576], P('row', 'col'), as said below
- virt_irrep: int32 [768], replicated, may hold values from 0 to 7, as said below
- pair_list: int32 [24576, 2], replicated, may hold values from 0 to 767
Outputs:
- residual: bfloat16 [24576, 2048], P(('col', 'row'), 'pair')
Inputs may be any that keep to these rules, and one draw needn't show every extreme that they name: integrals is symmetric: integrals[p, q] = integrals[q, p]. `virt_irrep`: labels of the 8 irreps; every label occurs, their counts are uneven.
All inputs are finite; a program needn't handle non-finite values.
Results may differ from a plain program's by a relative error of at most 0.018.
Values may be sent and summed in bfloat16 or wider, within the bound.
No kernel may reach another device: no remote copies, remote signals or barrier semaphores. Data moves between devices by JAX's collectives and lax.ppermute only.
A program may use at most 64 MiB of HBM per device.

v0:
```python
import jax
import jax.numpy as jnp
from jax import lax
from jax.sharding import PartitionSpec as P


def pair_symmetry(pairs, labels):
    orbital = lax.broadcasted_iota(jnp.int32, (1, labels.shape[0]), 1)
    first = jnp.sum(jnp.where(pairs[:, 0:1] == orbital, labels[None, :], 0), axis=1)
    second = jnp.sum(jnp.where(pairs[:, 1:2] == orbital, labels[None, :], 0), axis=1)
    return jnp.bitwise_xor(first, second)


def rounded_term(partial_value):
    return lax.optimization_barrier(partial_value.astype(jnp.bfloat16)).astype(jnp.float32)


def body(amplitudes, integrals, virt_irrep, pair_list):
    blk_rows, blk_cols = integrals.shape
    grid_row = lax.axis_index("row")
    grid_col = lax.axis_index("col")
    cd_pairs = lax.dynamic_slice_in_dim(pair_list, grid_row * blk_rows, blk_rows, 0)
    ab_pairs = lax.dynamic_slice_in_dim(pair_list, grid_col * blk_cols, blk_cols, 0)
    matching = (
        pair_symmetry(cd_pairs, virt_irrep)[:, None] == pair_symmetry(ab_pairs, virt_irrep)[None, :]
    )
    coupled = jnp.where(matching, integrals, jnp.zeros((), integrals.dtype))
    contract = (((0,), (0,)), ((), ()))
    block = lax.all_gather(amplitudes, "col", axis=0, tiled=True)
    return lax.psum_scatter(
        rounded_term(
            lax.dot_general(coupled, block, contract, preferred_element_type=jnp.float32)
        ).astype(jnp.bfloat16),
        "row",
        scatter_dimension=0,
        tiled=True,
    )


def solution(mesh):
    placed = (P(("row", "col"), "pair"), P("row", "col"), P(), P())
    return jax.shard_map(
        body, mesh=mesh, in_specs=placed, out_specs=P(("col", "row"), "pair"), check_vma=False
    )
```

profile of v0, /device:TPU:24, one launch (start us, length us, event | category | flops | bytes accessed | tf_op | source)
XLA Modules:
  0.0 267.9 jit_solution(4479588205238101621)
XLA Ops:
  6.5 0.0 all-gather.2.cloned.1.call-start
  6.5 0.7 all-gather.2.cloned.1.call-update
  7.3 0.0 reduce-scatter.2.cloned.1.call-start
  7.3 0.9 dynamic-slice_reduce_fusion.2
  8.2 4.3 %select_reduce_fusion.2 = (s32[1536]{0:T(1024)S(1)}, s32[1536]{0:T(1024)S(1)}, s32[1536]{0:T(1024)S(1)}, s32[1536]{0:T(1024)S(1)}) fusion(s32[1536]{0:T(1024)S(1)} %get-tuple-element.5, s32[768]{0:T(1024)} %param.6, s32[1536]{0:T(1024)S(1)} %get-tuple-element.6, s32[1536]{0:T(1024)S(1)} %get-tuple-element.8, s32[1536]{0:T(1024)S(1)} %get-tuple-element.7), kind=kLoop, calls=%fused_computation.7 | loop fusion | flops 14149632 | bytes 52224 | tf_op jit(solution)/shard_map/reduce_sum | solution.py:10
  12.5 99.4 %all-gather.2.cloned.1.call-done = bf16[1536,1024]{1,0:T(8,128)(2,1)} async-done(((bf16[96,1024]{1,0:T(8,128)(2,1)}), bf16[1536,1024]{1,0:T(8,128)(2,1)}) %all-gather.2.cloned.1.call-update) | async-done | bytes 3145744 | tf_op jit(solution)/shard_map/all_gather | solution.py:29
  112.0 9.4 %fusion.3 = bf16[1536,1024]{1,0:T(8,128)(2,1)} fusion(bf16[1536,1024]{1,0:T(8,128)(2,1)} %all-gather.2.cloned.1.call-done, bf16[1536,1536]{1,0:T(8,128)(2,1)} %param.5, s32[1536]{0:T(1024)S(1)} %xor.15, s32[1536]{0:T(1024)S(1)} %xor.14), kind=kOutput, calls=%fused_computation.12 | convolution fusion | flops 4838129664 | bytes 11022336 | tf_op jit(solution)/shard_map/dot_general | solution.py:32
  121.4 0.0 reduce-scatter.2.cloned.1.call-update
  121.4 139.7 %reduce-scatter.2.cloned.1.call-done = bf16[96,1024]{1,0:T(8,128)(2,1)} async-done(((bf16[1536,1024]{1,0:T(8,128)(2,1)}), bf16[96,1024]{1,0:T(8,128)(2,1)}) %reduce-scatter.2.cloned.1.call-update) | async-done | bytes 196624 | tf_op jit(solution)/shard_map/reduce_scatter | solution.py:30
  (2 shorter events, 0.0 us)
Async XLA Ops:
  6.5 105.4 %all-gather.2.cloned.1.call-start = ((), (), s32[]{:S(2)}) async-start(), calls=%async_computation.1 | async-start | bytes 3342336 | tf_op jit(solution)/shard_map/all_gather | solution.py:29
  7.3 253.8 %reduce-scatter.2.cloned.1.call-start = ((), (), s32[]{:S(2)}) async-start(), calls=%async_computation.2 | async-start | bytes 3342336 | tf_op jit(solution)/shard_map/reduce_scatter | solution.py:30
Sparse Core Ops, SparseCore 0:
  9.4 102.4 all-gather.1
  121.6 139.4 reduce-scatter.1
where the time goes:
time: 269 us; the launch traced here: 268 us
  waiting for transfers between devices  240 us (89%)
  between operations  13.4 us (5%)
  matrix products  9.44 us (4%)
  other arithmetic  4.31 us (2%)
    reduce_scatter x1, waiting for transfers between devices, body(): lax.psum_scatter(rounded_term(lax.dot_general(coupled, block, contract, p...  140 us
    all_gather x1, waiting for transfers between devices, body(): block = lax.all_gather(amplitudes, 'col', axis=0, tiled=True)  99.4 us
    dot_general x1, matrix products, body(): lax.dot_general(coupled, block, contract, preferred_element_type=jnp.floa...  9.44 us
  transfers between devices with their start and end apart: 2, of which 2 were waited for; matrix products, arithmetic and copies ran while one was open for 2% of the time, Pallas kernels for 0%

commit v1 on v0

v1 whole, which is shorter than its diff:
```python
import jax
import jax.numpy as jnp
from jax import lax
from jax.sharding import Mesh, PartitionSpec as P

CHUNKS = 2


def pair_symmetry(pairs, labels):
    orbital = lax.broadcasted_iota(jnp.int32, (1, labels.shape[0]), 1)
    first = jnp.sum(jnp.where(pairs[:, 0:1] == orbital, labels[None, :], 0), axis=1)
    second = jnp.sum(jnp.where(pairs[:, 1:2] == orbital, labels[None, :], 0), axis=1)
    return jnp.bitwise_xor(first, second)


def shift(block, axis, first, second):
    moves = [
        (i * 2 + core, (i + step) % 4 * 2 + core)
        for i in range(4)
        for core, step in ((0, first), (1, second))
    ]
    return lax.ppermute(block, (axis, "core"), moves)


def pick(blocks, index):
    return lax.dynamic_index_in_dim(blocks, index % 4, 0, keepdims=False)


def total(*terms):
    return sum(t.astype(jnp.float32) for t in terms)


def gather_x(own):
    return jnp.concatenate(
        [own, shift(own, "x", 1, 1), shift(own, "x", -1, -1), shift(own, "x", 2, -2)], axis=0
    )


def scatter_y(partial, y):
    part = lambda d: lax.dynamic_index_in_dim(partial, (y + d) % 4, 1, keepdims=False)
    up = shift(part(1), "y", 1, 1)
    down = shift(part(3), "y", -1, -1)
    far = shift(part(2), "y", 2, -2)
    return total(part(0), up, down, far).astype(partial.dtype)


def scatter_zh(partial, zh, core):
    relayed = shift(pick(partial, zh + 2), "zh", 1, -1)
    add = lambda block, mine: jnp.where(mine, total(block, relayed), total(block)).astype(partial.dtype)
    up = shift(add(pick(partial, zh + 1), core == 0), "zh", 1, 1)
    down = shift(add(pick(partial, zh + 3), core == 1), "zh", -1, -1)
    return total(pick(partial, zh), up, down).astype(partial.dtype)


def body(amplitudes, integrals, virt_irrep, pair_list):
    blk = integrals.shape[0]
    zh, y, x, zl, core = (lax.axis_index(a) for a in ("zh", "y", "x", "zl", "core"))
    cd_pairs = lax.dynamic_slice_in_dim(pair_list, (zh * 4 + y) * blk, blk, 0)
    ab_pairs = lax.dynamic_slice_in_dim(pair_list, (x * 4 + zl) * blk, blk, 0)
    matching = (
        pair_symmetry(cd_pairs, virt_irrep)[:, None] == pair_symmetry(ab_pairs, virt_irrep)[None, :]
    )
    coupled = jnp.where(matching, integrals, jnp.zeros((), integrals.dtype)).reshape(4, -1, blk)
    coupled = lax.optimization_barrier(
        jnp.concatenate([pick(coupled, x + d) for d in (0, 3, 1, 2)], axis=0)
    )
    near = lax.all_gather(amplitudes, "zl", axis=0, tiled=True)
    width = amplitudes.shape[1] // CHUNKS
    done = []
    for k in range(CHUNKS):
        block = gather_x(near[:, k * width : (k + 1) * width])
        product = lax.dot_general(
            coupled, block, (((0,), (0,)), ((), ())), preferred_element_type=jnp.float32
        ).astype(jnp.bfloat16)
        product = lax.optimization_barrier(product).reshape(4, 4, -1, width)
        done.append(scatter_zh(scatter_y(product, y), zh, core))
    return jnp.concatenate(done, axis=1)


def solution(mesh):
    fine = Mesh(mesh.devices.reshape(4, 4, 4, 4, 2), ("zh", "y", "x", "zl", "core"))
    row, col = ("zh", "y"), ("x", "zl")
    placed = (P(row + col, "core"), P(row, col), P(), P())
    return jax.shard_map(
        body, mesh=fine, in_specs=placed, out_specs=P(col + row, "core"), check_vma=False
    )
```

time: 269 us -> 138 us (0.51)
  waiting for transfers between devices: 240 us -> 9.93 us
  starting transfers between devices: 0.04 us -> 76.4 us
  blocking collectives: 0 us -> 21.1 us
  between operations: 13.4 us -> 0.57 us
  other arithmetic: 4.31 us -> 14.1 us
  local copies, waits for them, and re-layouts: 0.9 us -> 4.24 us
    reduce_scatter x1 -> x0, waiting for transfers between devices: 140 us -> none  [body(): lax.psum_scatter(rounded_term(lax.dot_general(coupled, block, contract, p...]
    all_gather x1 -> x0, waiting for transfers between devices: 99.4 us -> none  [body(): block = lax.all_gather(amplitudes, 'col', axis=0, tiled=True)]
    ppermute x0 -> x18, starting transfers between devices: none -> 76.4 us  [shift(): return lax.ppermute(block, (axis, 'core'), moves)]
    all_gather x0 -> x1, blocking collectives: none -> 21.1 us  [body(): near = lax.all_gather(amplitudes, 'zl', axis=0, tiled=True)]
    ppermute x0 -> x18, waiting for transfers between devices: none -> 9.93 us  [shift(): return lax.ppermute(block, (axis, 'core'), moves)]
    select_n x0 -> x1, other arithmetic: none -> 3.47 us  [body(): jnp.where(matching, integrals, jnp.zeros((), integrals.dtype))]
    convert_element_type x0 -> x6, other arithmetic: none -> 3.22 us  [the longest x2 3 us: scatter_y(): return total(part(0), up, down, far).astype(partial.dtype)]
    concatenate x0 -> x2, other arithmetic: none -> 3.1 us  [the longest x1 2.4 us: body(): jnp.concatenate([pick(coupled, x + d) for d in (0, 3, 1, 2)], axis=0)]
  transfers between devices with their start and end apart: 2 -> 18, of which waited for: 2 -> 4; matrix products, arithmetic and copies ran while one was open for 2% -> 20% of each run, Pallas kernels for 0% -> 0%
where the time goes in v1:
time: 138 us; the launch traced here: 136 us
  starting transfers between devices  76.4 us (55%)
  blocking collectives  21.1 us (15%)
  other arithmetic  14.1 us (10%)
  matrix products  10.2 us (7%)
  waiting for transfers between devices  9.93 us (7%)
  local copies, waits for them, and re-layouts  4.24 us (3%)
    ppermute x18, starting transfers between devices, shift(): return lax.ppermute(block, (axis, 'core'), moves)  76.4 us
    all_gather x1, blocking collectives, body(): near = lax.all_gather(amplitudes, 'zl', axis=0, tiled=True)  21.1 us
    dot_general x2, matrix products, body(): lax.dot_general(coupled, block, (((0,), (0,)), ((), ())), preferred_eleme...  10.2 us
    ppermute x18, waiting for transfers between devices, shift(): return lax.ppermute(block, (axis, 'core'), moves)  9.93 us
    reduce_sum x1, other arithmetic, pair_symmetry(): jnp.sum(jnp.where(pairs[:, 1:2] == orbital, labels[None, :], 0), axis=1)  4.3 us
    select_n x1, other arithmetic, body(): jnp.where(matching, integrals, jnp.zeros((), integrals.dtype))  3.47 us
    convert_element_type x2, other arithmetic, scatter_y(): return total(part(0), up, down, far).astype(partial.dtype)  3 us
  transfers between devices with their start and end apart: 18, of which 4 were waited for; matrix products, arithmetic and copies ran while one was open for 20% of the time, Pallas kernels for 0%

profile of v1, /device:TPU:24, one launch (start us, length us, event | category | flops | bytes accessed | tf_op | source)
XLA Modules:
  0.0 136.5 jit_solution(1136448385585627056)
XLA Ops:
  0.0 21.1 %all_gather.3 = bf16[384,1024]{1,0:T(8,128)(2,1)S(1)} all-gather(bf16[96,1024]{1,0:T(8,128)(2,1)} %param.4), channel_id=1, replica_groups=mesh['zh'=4,'y'=4,'x'=4,'zl'=4,'core'=2] {'zl'}, dimensions={0}, use_global_device_ids=true | all-gather | bytes 983040 | tf_op jit(solution)/shard_map/all_gather | solution.py:67
  21.1 0.1 fusion.30
  21.1 3.4 %collective-permute-start = (bf16[384,512]{1,0:T(8,128)(2,1)S(1)}, bf16[384,512]{1,0:T(8,128)(2,1)S(1)}, u32[]{:S(2)}, u32[]{:S(2)}) collective-permute-start(bf16[384,512]{1,0:T(8,128)(2,1)S(1)} %get-tuple-element.23), channel_id=1, source_target_pairs={{0,8},{1,9},{8,16},{9,17},{16,24},{17,25},{24,0},{25,1},{2,10},{3,... | collective-permute-start | bytes 1179656 | tf_op jit(solution)/shard_map/ppermute | solution.py:22
  24.5 3.7 %collective-permute-start.1 = (bf16[384,512]{1,0:T(8,128)(2,1)S(1)}, bf16[384,512]{1,0:T(8,128)(2,1)S(1)}, u32[]{:S(2)}, u32[]{:S(2)}) collective-permute-start(bf16[384,512]{1,0:T(8,128)(2,1)S(1)} %get-tuple-element.23), channel_id=1, source_target_pairs={{0,24},{1,25},{8,0},{9,1},{16,8},{17,9},{24,16},{25,17},{2,26},{3,... | collective-permute-start | bytes 1179656 | tf_op jit(solution)/shard_map/ppermute | solution.py:22
  28.2 3.7 %collective-permute-start.2 = (bf16[384,512]{1,0:T(8,128)(2,1)S(1)}, bf16[384,512]{1,0:T(8,128)(2,1)}, u32[]{:S(2)}, u32[]{:S(2)}) collective-permute-start(bf16[384,512]{1,0:T(8,128)(2,1)S(1)} %get-tuple-element.23), channel_id=1, source_target_pairs={{0,16},{1,17},{8,24},{9,25},{16,0},{17,1},{24,8},{25,9},{2,18},{3,... | collective-permute-start | bytes 1179656 | tf_op jit(solution)/shard_map/ppermute | solution.py:22
  31.9 3.0 %collective-permute-start.10 = (bf16[384,512]{1,0:T(8,128)(2,1)S(1)}, bf16[384,512]{1,0:T(8,128)(2,1)}, u32[]{:S(2)}, u32[]{:S(2)}) collective-permute-start(bf16[384,512]{1,0:T(8,128)(2,1)S(1)} %get-tuple-element.24), channel_id=1, source_target_pairs={{0,24},{1,25},{8,0},{9,1},{16,8},{17,9},{24,16},{25,17},{2,26},{3,... | collective-permute-start | bytes 1179656 | tf_op jit(solution)/shard_map/ppermute | solution.py:22
  35.0 3.4 %collective-permute-start.11 = (bf16[384,512]{1,0:T(8,128)(2,1)S(1)}, bf16[384,512]{1,0:T(8,128)(2,1)}, u32[]{:S(2)}, u32[]{:S(2)}) collective-permute-start(bf16[384,512]{1,0:T(8,128)(2,1)S(1)} %get-tuple-element.24), channel_id=1, source_target_pairs={{0,16},{1,17},{8,24},{9,25},{16,0},{17,1},{24,8},{25,9},{2,18},{3,... | collective-permute-start | bytes 1179656 | tf_op jit(solution)/shard_map/ppermute | solution.py:22
  38.5 0.9 dynamic-slice_reduce_fusion.2
  39.4 4.3 %select_reduce_fusion.2 = (s32[1536]{0:T(1024)S(1)}, s32[1536]{0:T(1024)S(1)}, s32[1536]{0:T(1024)S(1)}, s32[1536]{0:T(1024)S(1)}) fusion(s32[1536]{0:T(1024)S(1)} %get-tuple-element.5, s32[768]{0:T(1024)} %param.6, s32[1536]{0:T(1024)S(1)} %get-tuple-element.6, s32[1536]{0:T(1024)S(1)} %get-tuple-element.8, s32[1536]{0:T(1024)S(1)} %get-tuple-element.7), kind=kLoop, calls=%fused_computation.6 | loop fusion | flops 14149632 | bytes 52224 | tf_op jit(solution)/shard_map/reduce_sum | solution.py:12
  43.8 3.5 %compare_select_fusion = bf16[1536,1536]{1,0:T(8,128)(2,1)S(1)} fusion(bf16[1536,1536]{1,0:T(8,128)(2,1)} %param.5, s32[1536]{0:T(1024)S(1)} %xor.15, s32[1536]{0:T(1024)S(1)} %xor.14), kind=kLoop, calls=%fused_computation | loop fusion | flops 4718592 | bytes 9449472 | tf_op jit(solution)/shard_map/jit(_where)/select_n | solution.py:63
  47.2 0.3 dynamic-slice_bitcast_fusion.3
  47.6 2.4 %pad_maximum_fusion = bf16[1536,1536]{1,0:T(8,128)(2,1)} fusion(bf16[384,1536]{1,0:T(8,128)(2,1)S(1)} %get-tuple-element.14, bf16[384,1536]{1,0:T(8,128)(2,1)S(1)} %get-tuple-element.15, bf16[384,1536]{1,0:T(8,128)(2,1)S(1)} %get-tuple-element.16, bf16[384,1536]{1,0:T(8,128)(2,1)S(1)} %get-tuple-element.13), kind=kLoop, calls=%fused_computation.1 | loop fusion | flops 18874368 | bytes 9437184 | tf_op jit(solution)/shard_map/concatenate | solution.py:65
  50.0 0.0 collective-permute-done
  50.0 2.6 %collective-permute-start.9 = (bf16[384,512]{1,0:T(8,128)(2,1)S(1)}, bf16[384,512]{1,0:T(8,128)(2,1)S(1)}, u32[]{:S(2)}, u32[]{:S(2)}) collective-permute-start(bf16[384,512]{1,0:T(8,128)(2,1)S(1)} %get-tuple-element.24), channel_id=1, source_target_pairs={{0,8},{1,9},{8,16},{9,17},{16,24},{17,25},{24,0},{25,1},{2,10},{3,... | collective-permute-start | bytes 1179656 | tf_op jit(solution)/shard_map/ppermute | solution.py:22
  52.6 0.0 collective-permute-done.1
  52.7 0.7 copy-done.1
  53.4 0.0 collective-permute-done.2
  53.4 5.3 %convolution_convert_fusion.1 = bf16[1536,512]{1,0:T(8,128)(2,1)S(1)} fusion(bf16[1536,1536]{1,0:T(8,128)(2,1)} %pad_maximum_fusion, bf16[384,512]{1,0:T(8,128)(2,1)} %collective-permute-done.2, bf16[384,512]{1,0:T(8,128)(2,1)} %copy-done.1, bf16[384,512]{1,0:T(8,128)(2,1)} %copy-done, bf16[384,512]{1,0:T(8,128)(2,1)S(1)} %get-tuple-element.23), kind=kOutput, calls=%fused_computation.11 | convolution fusion | flops 2422996992 | bytes 7864320 | tf_op jit(solution)/shard_map/dot_general | solution.py:72
  58.7 0.1 dynamic-slice_bitcast_fusion.9
  58.8 4.1 %collective-permute-start.3 = (bf16[4,96,512]{2,1,0:T(8,128)(2,1)S(1)}, bf16[4,96,512]{2,1,0:T(8,128)(2,1)}, u32[]{:S(2)}, u32[]{:S(2)}) collective-permute-start(bf16[4,96,512]{2,1,0:T(8,128)(2,1)S(1)} %get-tuple-element.17), channel_id=1, source_target_pairs={{0,32},{1,33},{32,64},{33,65},{64,96},{65,97},{96,0},{97,1},{2,34}... | collective-permute-start | bytes 1179656 | tf_op jit(solution)/shard_map/ppermute | solution.py:22
  62.9 1.9 %collective-permute-start.4 = (bf16[4,96,512]{2,1,0:T(8,128)(2,1)S(1)}, bf16[4,96,512]{2,1,0:T(8,128)(2,1)}, u32[]{:S(2)}, u32[]{:S(2)}) collective-permute-start(bf16[4,96,512]{2,1,0:T(8,128)(2,1)S(1)} %get-tuple-element.19), channel_id=1, source_target_pairs={{0,96},{1,97},{32,0},{33,1},{64,32},{65,33},{96,64},{97,65},{2,98}... | collective-permute-start | bytes 1179656 | tf_op jit(solution)/shard_map/ppermute | solution.py:22
  64.9 0.0 collective-permute-done.10
  64.9 3.4 %collective-permute-start.5 = (bf16[4,96,512]{2,1,0:T(8,128)(2,1)S(1)}, bf16[4,96,512]{2,1,0:T(8,128)(2,1)}, u32[]{:S(2)}, u32[]{:S(2)}) collective-permute-start(bf16[4,96,512]{2,1,0:T(8,128)(2,1)S(1)} %get-tuple-element.18), channel_id=1, source_target_pairs={{0,64},{1,65},{32,96},{33,97},{64,0},{65,1},{96,32},{97,33},{2,66}... | collective-permute-start | bytes 1179656 | tf_op jit(solution)/shard_map/ppermute | solution.py:22
  68.3 0.0 collective-permute-done.11
  68.3 0.0 collective-permute-done.9
  68.3 4.9 %convolution_convert_fusion = bf16[1536,512]{1,0:T(8,128)(2,1)} fusion(bf16[1536,1536]{1,0:T(8,128)(2,1)S(1)} %bitcast.59, bf16[384,512]{1,0:T(8,128)(2,1)} %collective-permute-done.11, bf16[384,512]{1,0:T(8,128)(2,1)} %collective-permute-done.10, bf16[384,512]{1,0:T(8,128)(2,1)S(1)} %collective-permute-done.9, bf16[384,512]{1,0:T(8,128)(2,1)S(1)} %get-tuple-element.24), kind=kOutput, calls=%fused_computation.10 | convolution fusion | flops 2422996992 | bytes 7864320 | tf_op jit(solution)/shard_map/dot_general | solution.py:72
  73.2 2.1 %dynamic-slice_bitcast_fusion.6 = (bf16[4,96,512]{2,1,0:T(8,128)(2,1)}, bf16[4,96,512]{2,1,0:T(8,128)(2,1)S(1)}, bf16[4,96,512]{2,1,0:T(8,128)(2,1)S(1)}) fusion(bf16[4,4,96,512]{3,2,1,0:T(8,128)(2,1)} %bitcast.14, s32[]{:T(128)S(6)} %select_n.177, s32[]{:T(128)S(6)} %select_n.181, s32[]{:T(128)S(6)} %select_n.179), kind=kLoop, calls=%fused_computation.40 | loop fusion | bytes 2359308 | tf_op jit(solution)/shard_map/jit(dynamic_index_in_dim)/squeeze | solution.py:40
  75.3 3.7 %collective-permute-start.12 = (bf16[4,96,512]{2,1,0:T(8,128)(2,1)}, bf16[4,96,512]{2,1,0:T(8,128)(2,1)}, u32[]{:S(2)}, u32[]{:S(2)}) collective-permute-start(bf16[4,96,512]{2,1,0:T(8,128)(2,1)} %get-tuple-element.20), channel_id=1, source_target_pairs={{0,32},{1,33},{32,64},{33,65},{64,96},{65,97},{96,0},{97,1},{2,34}... | collective-permute-start | bytes 1179656 | tf_op jit(solution)/shard_map/ppermute | solution.py:22
  79.0 2.8 %collective-permute-start.13 = (bf16[4,96,512]{2,1,0:T(8,128)(2,1)S(1)}, bf16[4,96,512]{2,1,0:T(8,128)(2,1)}, u32[]{:S(2)}, u32[]{:S(2)}) collective-permute-start(bf16[4,96,512]{2,1,0:T(8,128)(2,1)S(1)} %get-tuple-element.22), channel_id=1, source_target_pairs={{0,96},{1,97},{32,0},{33,1},{64,32},{65,33},{96,64},{97,65},{2,98}... | collective-permute-start | bytes 1179656 | tf_op jit(solution)/shard_map/ppermute | solution.py:22
  81.8 0.0 collective-permute-done.3
  81.8 4.0 %collective-permute-start.14 = (bf16[4,96,512]{2,1,0:T(8,128)(2,1)S(1)}, bf16[4,96,512]{2,1,0:T(8,128)(2,1)}, u32[]{:S(2)}, u32[]{:S(2)}) collective-permute-start(bf16[4,96,512]{2,1,0:T(8,128)(2,1)S(1)} %get-tuple-element.21), channel_id=1, source_target_pairs={{0,64},{1,65},{32,96},{33,97},{64,0},{65,1},{96,32},{97,33},{2,66}... | collective-permute-start | bytes 1179656 | tf_op jit(solution)/shard_map/ppermute | solution.py:22
  85.9 1.4 %fusion.19 = bf16[4,96,512]{2,1,0:T(8,128)(2,1)S(1)} fusion(bf16[4,96,512]{2,1,0:T(8,128)(2,1)} %collective-permute-done.5, bf16[4,96,512]{2,1,0:T(8,128)(2,1)} %collective-permute-done.4, bf16[4,96,512]{2,1,0:T(8,128)(2,1)} %collective-permute-done.3, bf16[4,4,96,512]{3,2,1,0:T(8,128)(2,1)S(1)} %bitcast.61, s32[]{:T(128)S(6)} %select_n.175), kind=kLoop, calls=%fused_computation.37 | loop fusion | flops 1572864 | bytes 1966084 | tf_op jit(solution)/shard_map/convert_element_type | solution.py:44
  87.3 8.3 %collective-permute-start.6 = (bf16[96,512]{1,0:T(8,128)(2,1)S(1)}, bf16[96,512]{1,0:T(8,128)(2,1)S(1)}, u32[]{:S(2)}, u32[]{:S(2)}) collective-permute-start(bf16[96,512]{1,0:T(8,128)(2,1)S(1)} %dynamic-slice_bitcast_fusion.11), channel_id=1, source_target_pairs={{0,128},{1,385},{128,256},{129,1},{256,384},{257,129},{384,0},{385... | collective-permute-start | bytes 294920 | tf_op jit(solution)/shard_map/ppermute | solution.py:22
  95.6 0.0 collective-permute-done.12
  95.6 0.8 collective-permute-done.13
  96.4 0.0 collective-permute-done.14
  96.4 1.6 %fusion.16 = bf16[4,96,512]{2,1,0:T(8,128)(2,1)S(1)} fusion(bf16[4,96,512]{2,1,0:T(8,128)(2,1)} %collective-permute-done.14, bf16[4,96,512]{2,1,0:T(8,128)(2,1)} %collective-permute-done.13, bf16[4,96,512]{2,1,0:T(8,128)(2,1)} %collective-permute-done.12, bf16[4,4,96,512]{3,2,1,0:T(8,128)(2,1)} %bitcast.14, s32[]{:T(128)S(6)} %select_n.175), kind=kLoop, calls=%fused_computation.33 | loop fusion | flops 1572864 | bytes 1966084 | tf_op jit(solution)/shard_map/convert_element_type | solution.py:44
  98.0 8.8 %collective-permute-start.15 = (bf16[96,512]{1,0:T(8,128)(2,1)S(1)}, bf16[96,512]{1,0:T(8,128)(2,1)S(1)}, u32[]{:S(2)}, u32[]{:S(2)}) collective-permute-start(bf16[96,512]{1,0:T(8,128)(2,1)S(1)} %dynamic-slice_bitcast_fusion.10), channel_id=1, source_target_pairs={{0,128},{1,385},{128,256},{129,1},{256,384},{257,129},{384,0},{385... | collective-permute-start | bytes 294920 | tf_op jit(solution)/shard_map/ppermute | solution.py:22
  106.9 0.1 fusion.20
  106.9 6.4 %collective-permute-start.7 = (bf16[96,512]{1,0:T(8,128)(2,1)S(1)}, bf16[96,512]{1,0:T(8,128)(2,1)S(1)}, u32[]{:S(2)}, u32[]{:S(2)}) collective-permute-start(bf16[96,512]{1,0:T(8,128)(2,1)S(1)} %get-tuple-element.25), channel_id=1, source_target_pairs={{0,128},{1,129},{128,256},{129,257},{256,384},{257,385},{384,0},{3... | collective-permute-start | bytes 294920 | tf_op jit(solution)/shard_map/ppermute | solution.py:22
  113.4 3.3 %collective-permute-start.8 = (bf16[96,512]{1,0:T(8,128)(2,1)S(1)}, bf16[96,512]{1,0:T(8,128)(2,1)S(1)}, u32[]{:S(2)}, u32[]{:S(2)}) collective-permute-start(bf16[96,512]{1,0:T(8,128)(2,1)S(1)} %get-tuple-element.26), channel_id=1, source_target_pairs={{0,384},{1,385},{128,0},{129,1},{256,128},{257,129},{384,256},{385... | collective-permute-start | bytes 294920 | tf_op jit(solution)/shard_map/ppermute | solution.py:22
  116.7 0.1 fusion.22
  116.8 6.4 %collective-permute-start.16 = (bf16[96,512]{1,0:T(8,128)(2,1)S(1)}, bf16[96,512]{1,0:T(8,128)(2,1)S(1)}, u32[]{:S(2)}, u32[]{:S(2)}) collective-permute-start(bf16[96,512]{1,0:T(8,128)(2,1)S(1)} %get-tuple-element.27), channel_id=1, source_target_pairs={{0,128},{1,129},{128,256},{129,257},{256,384},{257,385},{384,0},{3... | collective-permute-start | bytes 294920 | tf_op jit(solution)/shard_map/ppermute | solution.py:22
  123.2 3.3 %collective-permute-start.17 = (bf16[96,512]{1,0:T(8,128)(2,1)S(1)}, bf16[96,512]{1,0:T(8,128)(2,1)S(1)}, u32[]{:S(2)}, u32[]{:S(2)}) collective-permute-start(bf16[96,512]{1,0:T(8,128)(2,1)S(1)} %get-tuple-element.28), channel_id=1, source_target_pairs={{0,384},{1,385},{128,0},{129,1},{256,128},{257,129},{384,256},{385... | collective-permute-start | bytes 294920 | tf_op jit(solution)/shard_map/ppermute | solution.py:22
  126.6 2.1 %collective-permute-done.8 = bf16[96,512]{1,0:T(8,128)(2,1)S(1)} collective-permute-done((bf16[96,512]{1,0:T(8,128)(2,1)S(1)}, bf16[96,512]{1,0:T(8,128)(2,1)S(1)}, u32[]{:S(2)}, u32[]{:S(2)}) %collective-permute-start.8) | collective-permute-done | bytes 98336 | tf_op jit(solution)/shard_map/ppermute | solution.py:22
  128.7 0.6 collective-permute-done.16
  129.4 6.4 %collective-permute-done.17 = bf16[96,512]{1,0:T(8,128)(2,1)S(1)} collective-permute-done((bf16[96,512]{1,0:T(8,128)(2,1)S(1)}, bf16[96,512]{1,0:T(8,128)(2,1)S(1)}, u32[]{:S(2)}, u32[]{:S(2)}) %collective-permute-start.17) | collective-permute-done | bytes 98336 | tf_op jit(solution)/shard_map/ppermute | solution.py:22
  135.8 0.7 pad_maximum_fusion.1
  (19 shorter events, 0.2 us)
Async XLA Ops:
  21.1 28.9 %collective-permute-start = (bf16[384,512]{1,0:T(8,128)(2,1)S(1)}, bf16[384,512]{1,0:T(8,128)(2,1)S(1)}, u32[]{:S(2)}, u32[]{:S(2)}) collective-permute-start(bf16[384,512]{1,0:T(8,128)(2,1)S(1)} %get-tuple-element.23), channel_id=1, source_target_pairs={{0,8},{1,9},{8,16},{9,17},{16,24},{17,25},{24,0},{25,1},{2,10},{3,... | collective-permute-start | bytes 1179656 | tf_op jit(solution)/shard_map/ppermute | solution.py:22
  24.5 28.1 %collective-permute-start.1 = (bf16[384,512]{1,0:T(8,128)(2,1)S(1)}, bf16[384,512]{1,0:T(8,128)(2,1)S(1)}, u32[]{:S(2)}, u32[]{:S(2)}) collective-permute-start(bf16[384,512]{1,0:T(8,128)(2,1)S(1)} %get-tuple-element.23), channel_id=1, source_target_pairs={{0,24},{1,25},{8,0},{9,1},{16,8},{17,9},{24,16},{25,17},{2,26},{3,... | collective-permute-start | bytes 1179656 | tf_op jit(solution)/shard_map/ppermute | solution.py:22
  28.2 25.2 %collective-permute-start.2 = (bf16[384,512]{1,0:T(8,128)(2,1)S(1)}, bf16[384,512]{1,0:T(8,128)(2,1)}, u32[]{:S(2)}, u32[]{:S(2)}) collective-permute-start(bf16[384,512]{1,0:T(8,128)(2,1)S(1)} %get-tuple-element.23), channel_id=1, source_target_pairs={{0,16},{1,17},{8,24},{9,25},{16,0},{17,1},{24,8},{25,9},{2,18},{3,... | collective-permute-start | bytes 1179656 | tf_op jit(solution)/shard_map/ppermute | solution.py:22
  31.9 32.9 %collective-permute-start.10 = (bf16[384,512]{1,0:T(8,128)(2,1)S(1)}, bf16[384,512]{1,0:T(8,128)(2,1)}, u32[]{:S(2)}, u32[]{:S(2)}) collective-permute-start(bf16[384,512]{1,0:T(8,128)(2,1)S(1)} %get-tuple-element.24), channel_id=1, source_target_pairs={{0,24},{1,25},{8,0},{9,1},{16,8},{17,9},{24,16},{25,17},{2,26},{3,... | collective-permute-start | bytes 1179656 | tf_op jit(solution)/shard_map/ppermute | solution.py:22
  35.0 33.3 %collective-permute-start.11 = (bf16[384,512]{1,0:T(8,128)(2,1)S(1)}, bf16[384,512]{1,0:T(8,128)(2,1)}, u32[]{:S(2)}, u32[]{:S(2)}) collective-permute-start(bf16[384,512]{1,0:T(8,128)(2,1)S(1)} %get-tuple-element.24), channel_id=1, source_target_pairs={{0,16},{1,17},{8,24},{9,25},{16,0},{17,1},{24,8},{25,9},{2,18},{3,... | collective-permute-start | bytes 1179656 | tf_op jit(solution)/shard_map/ppermute | solution.py:22
  50.0 18.3 %slice-start = ((s8[4718592]{0:T(1024)(128)(4,1)}), s8[524288]{0:T(1024)(128)(4,1)S(1)}, s32[]{:S(2)}) async-start(s8[4718592]{0:T(1024)(128)(4,1)} %bitcast.58), calls=%async_computation | async-start | bytes 1048576
  50.0 18.3 %slice-start.1 = ((s8[4718592]{0:T(1024)(128)(4,1)}), s8[4194304]{0:T(1024)(128)(4,1)S(1)}, s32[]{:S(2)}) async-start(s8[4718592]{0:T(1024)(128)(4,1)} %bitcast.58), calls=%async_computation.1 | async-start | bytes 8388608
  50.0 2.7 %copy-start = (bf16[384,512]{1,0:T(8,128)(2,1)}, bf16[384,512]{1,0:T(8,128)(2,1)S(1)}, u32[]{:S(2)}) copy-start(bf16[384,512]{1,0:T(8,128)(2,1)S(1)} %collective-permute-done) | copy-start | bytes 1179652
  50.0 18.3 %collective-permute-start.9 = (bf16[384,512]{1,0:T(8,128)(2,1)S(1)}, bf16[384,512]{1,0:T(8,128)(2,1)S(1)}, u32[]{:S(2)}, u32[]{:S(2)}) collective-permute-start(bf16[384,512]{1,0:T(8,128)(2,1)S(1)} %get-tuple-element.24), channel_id=1, source_target_pairs={{0,8},{1,9},{8,16},{9,17},{16,24},{17,25},{24,0},{25,1},{2,10},{3,... | collective-permute-start | bytes 1179656 | tf_op jit(solution)/shard_map/ppermute | solution.py:22
  52.7 0.7 copy-start.1
  58.8 23.0 %collective-permute-start.3 = (bf16[4,96,512]{2,1,0:T(8,128)(2,1)S(1)}, bf16[4,96,512]{2,1,0:T(8,128)(2,1)}, u32[]{:S(2)}, u32[]{:S(2)}) collective-permute-start(bf16[4,96,512]{2,1,0:T(8,128)(2,1)S(1)} %get-tuple-element.17), channel_id=1, source_target_pairs={{0,32},{1,33},{32,64},{33,65},{64,96},{65,97},{96,0},{97,1},{2,34}... | collective-permute-start | bytes 1179656 | tf_op jit(solution)/shard_map/ppermute | solution.py:22
  62.9 22.9 %collective-permute-start.4 = (bf16[4,96,512]{2,1,0:T(8,128)(2,1)S(1)}, bf16[4,96,512]{2,1,0:T(8,128)(2,1)}, u32[]{:S(2)}, u32[]{:S(2)}) collective-permute-start(bf16[4,96,512]{2,1,0:T(8,128)(2,1)S(1)} %get-tuple-element.19), channel_id=1, source_target_pairs={{0,96},{1,97},{32,0},{33,1},{64,32},{65,33},{96,64},{97,65},{2,98}... | collective-permute-start | bytes 1179656 | tf_op jit(solution)/shard_map/ppermute | solution.py:22
  64.9 21.0 %collective-permute-start.5 = (bf16[4,96,512]{2,1,0:T(8,128)(2,1)S(1)}, bf16[4,96,512]{2,1,0:T(8,128)(2,1)}, u32[]{:S(2)}, u32[]{:S(2)}) collective-permute-start(bf16[4,96,512]{2,1,0:T(8,128)(2,1)S(1)} %get-tuple-element.18), channel_id=1, source_target_pairs={{0,64},{1,65},{32,96},{33,97},{64,0},{65,1},{96,32},{97,33},{2,66}... | collective-permute-start | bytes 1179656 | tf_op jit(solution)/shard_map/ppermute | solution.py:22
  75.3 20.3 %collective-permute-start.12 = (bf16[4,96,512]{2,1,0:T(8,128)(2,1)}, bf16[4,96,512]{2,1,0:T(8,128)(2,1)}, u32[]{:S(2)}, u32[]{:S(2)}) collective-permute-start(bf16[4,96,512]{2,1,0:T(8,128)(2,1)} %get-tuple-element.20), channel_id=1, source_target_pairs={{0,32},{1,33},{32,64},{33,65},{64,96},{65,97},{96,0},{97,1},{2,34}... | collective-permute-start | bytes 1179656 | tf_op jit(solution)/shard_map/ppermute | solution.py:22
  79.0 17.4 %collective-permute-start.13 = (bf16[4,96,512]{2,1,0:T(8,128)(2,1)S(1)}, bf16[4,96,512]{2,1,0:T(8,128)(2,1)}, u32[]{:S(2)}, u32[]{:S(2)}) collective-permute-start(bf16[4,96,512]{2,1,0:T(8,128)(2,1)S(1)} %get-tuple-element.22), channel_id=1, source_target_pairs={{0,96},{1,97},{32,0},{33,1},{64,32},{65,33},{96,64},{97,65},{2,98}... | collective-permute-start | bytes 1179656 | tf_op jit(solution)/shard_map/ppermute | solution.py:22
  81.8 14.6 %collective-permute-start.14 = (bf16[4,96,512]{2,1,0:T(8,128)(2,1)S(1)}, bf16[4,96,512]{2,1,0:T(8,128)(2,1)}, u32[]{:S(2)}, u32[]{:S(2)}) collective-permute-start(bf16[4,96,512]{2,1,0:T(8,128)(2,1)S(1)} %get-tuple-element.21), channel_id=1, source_target_pairs={{0,64},{1,65},{32,96},{33,97},{64,0},{65,1},{96,32},{97,33},{2,66}... | collective-permute-start | bytes 1179656 | tf_op jit(solution)/shard_map/ppermute | solution.py:22
  87.3 19.5 %collective-permute-start.6 = (bf16[96,512]{1,0:T(8,128)(2,1)S(1)}, bf16[96,512]{1,0:T(8,128)(2,1)S(1)}, u32[]{:S(2)}, u32[]{:S(2)}) collective-permute-start(bf16[96,512]{1,0:T(8,128)(2,1)S(1)} %dynamic-slice_bitcast_fusion.11), channel_id=1, source_target_pairs={{0,128},{1,385},{128,256},{129,1},{256,384},{257,129},{384,0},{385... | collective-permute-start | bytes 294920 | tf_op jit(solution)/shard_map/ppermute | solution.py:22
  98.0 18.7 %collective-permute-start.15 = (bf16[96,512]{1,0:T(8,128)(2,1)S(1)}, bf16[96,512]{1,0:T(8,128)(2,1)S(1)}, u32[]{:S(2)}, u32[]{:S(2)}) collective-permute-start(bf16[96,512]{1,0:T(8,128)(2,1)S(1)} %dynamic-slice_bitcast_fusion.10), channel_id=1, source_target_pairs={{0,128},{1,385},{128,256},{129,1},{256,384},{257,129},{384,0},{385... | collective-permute-start | bytes 294920 | tf_op jit(solution)/shard_map/ppermute | solution.py:22
  106.9 19.6 %collective-permute-start.7 = (bf16[96,512]{1,0:T(8,128)(2,1)S(1)}, bf16[96,512]{1,0:T(8,128)(2,1)S(1)}, u32[]{:S(2)}, u32[]{:S(2)}) collective-permute-start(bf16[96,512]{1,0:T(8,128)(2,1)S(1)} %get-tuple-element.25), channel_id=1, source_target_pairs={{0,128},{1,129},{128,256},{129,257},{256,384},{257,385},{384,0},{3... | collective-permute-start | bytes 294920 | tf_op jit(solution)/shard_map/ppermute | solution.py:22
  113.4 15.3 %collective-permute-start.8 = (bf16[96,512]{1,0:T(8,128)(2,1)S(1)}, bf16[96,512]{1,0:T(8,128)(2,1)S(1)}, u32[]{:S(2)}, u32[]{:S(2)}) collective-permute-start(bf16[96,512]{1,0:T(8,128)(2,1)S(1)} %get-tuple-element.26), channel_id=1, source_target_pairs={{0,384},{1,385},{128,0},{129,1},{256,128},{257,129},{384,256},{385... | collective-permute-start | bytes 294920 | tf_op jit(solution)/shard_map/ppermute | solution.py:22
  116.8 12.6 %collective-permute-start.16 = (bf16[96,512]{1,0:T(8,128)(2,1)S(1)}, bf16[96,512]{1,0:T(8,128)(2,1)S(1)}, u32[]{:S(2)}, u32[]{:S(2)}) collective-permute-start(bf16[96,512]{1,0:T(8,128)(2,1)S(1)} %get-tuple-element.27), channel_id=1, source_target_pairs={{0,128},{1,129},{128,256},{129,257},{256,384},{257,385},{384,0},{3... | collective-permute-start | bytes 294920 | tf_op jit(solution)/shard_map/ppermute | solution.py:22
  123.2 12.5 %collective-permute-start.17 = (bf16[96,512]{1,0:T(8,128)(2,1)S(1)}, bf16[96,512]{1,0:T(8,128)(2,1)S(1)}, u32[]{:S(2)}, u32[]{:S(2)}) collective-permute-start(bf16[96,512]{1,0:T(8,128)(2,1)S(1)} %get-tuple-element.28), channel_id=1, source_target_pairs={{0,384},{1,385},{128,0},{129,1},{256,128},{257,129},{384,256},{385... | collective-permute-start | bytes 294920 | tf_op jit(solution)/shard_map/ppermute | solution.py:22

commit v2 on v0

v2 whole, which is shorter than its diff:
```python
import functools

import jax
import jax.numpy as jnp
from jax import lax
from jax.experimental import pallas as pl
from jax.experimental.pallas import tpu as pltpu
from jax.sharding import Mesh, PartitionSpec as P

WIDTHS = (512, 512)
GATHER_X = ("dir", "dir")
SCATTER_Y = "dir"
SCATTER_Z = ('rl', 'rl')
TIE = True
COST = 100
VMEM = 24
PREP_FIRST = True
MERGE_Z = False


def permute(block, axis, target):
    moves = [(i * 2 + core, target(i, core) % 4 * 2 + core) for i in range(4) for core in (0, 1)]
    return lax.ppermute(block, (axis, "core"), moves)


def shift(block, axis, first, second):
    return permute(block, axis, lambda i, core: i + (second if core else first))


def swap(block, axis, first, second):
    return permute(block, axis, lambda i, core: i ^ (second if core else first))


def total(*terms):
    return sum(t.astype(jnp.float32) for t in terms)


def places(kind, me, core):
    if kind in ("dir", "rl"):
        return [(me + d) % 4 for d in range(4)]
    if kind == "rh":
        near = jnp.where(core == 0, 3, 1)
        return [me, me ^ near, me ^ near ^ 2, me ^ 2]
    return list(range(4))


def gather(kind, own, axis):
    if kind == "dir":
        far = shift(own, axis, 2, -2)
        after = shift(own, axis, -1, -1)
        return [own, after, far, shift(own, axis, 1, 1)]
    if kind == "rl":
        before, after = shift(own, axis, 1, 1), shift(own, axis, -1, -1)
        onward = jnp.where(lax.axis_index("core") == 0, before, after)
        return [own, after, shift(onward, axis, 1, -1), before]
    if kind == "rh":
        first = swap(own, axis, 1, 3)
        pair = swap(jnp.stack([own, first]), axis, 3, 1)
        return [own, pair[0], first, pair[1]]
    whole = lax.all_to_all(jnp.broadcast_to(own[None], (4,) + own.shape), axis, 0, 0)
    return [whole[i] for i in range(4)]


def scatter(kind, blocks, axis):
    dtype = blocks.dtype
    if kind == "dir":
        far = shift(blocks[2], axis, 2, -2)
        up = shift(blocks[1], axis, 1, 1)
        down = shift(blocks[3], axis, -1, -1)
        return total(blocks[0], far, up, down).astype(dtype)
    there = swap(blocks[2:], axis, 1, 3)
    kept = total(blocks[0], there[0])
    onward = total(blocks[1], there[1]).astype(dtype)
    return (kept + swap(onward, axis, 3, 1).astype(jnp.float32)).astype(dtype)


def pieces(blocks, order):
    return jnp.stack([lax.dynamic_index_in_dim(blocks, i, 0, keepdims=False) for i in order])


def lookup(table, index):
    found = jnp.zeros(index.shape, table.dtype)
    for row in range(table.shape[0]):
        line = jnp.broadcast_to(table[row : row + 1, :], index.shape)
        value = jnp.take_along_axis(line, index & 127, axis=1)
        found = jnp.where(index >> 7 == row, value, found)
    return found


def couple_kernel(rows_to, block, table, orbitals, out, labels):
    step = pl.program_id(0)
    tile, blk = block.shape[1], block.shape[0]
    lines = blk // 128

    @pl.when(step == 0)
    def _():
        symmetry = lookup(table[...], orbitals[...]).astype(jnp.float32)
        first, second = symmetry[: 2 * lines].astype(jnp.int32), symmetry[2 * lines :].astype(jnp.int32)
        labels[...] = jnp.bitwise_xor(first, second).astype(jnp.float32)

    mine = []
    for k in range(tile // 128):
        line = labels[pl.ds(step * (tile // 128) + k, 1), :]
        mine.append(jnp.broadcast_to(line, (128, 128)).T.astype(block.dtype))
    mine = jnp.concatenate(mine, axis=0)
    turned = block[...].T
    size = tile // 4
    for j in range(lines):
        across = slice(j * 128, (j + 1) * 128)
        other = labels[lines + j : lines + j + 1, :].astype(block.dtype)
        masked = jnp.where(mine == other, turned[:, across], jnp.zeros((), block.dtype))
        for k in range(4):
            out[rows_to[k], 0, :, across] = masked[k * size : (k + 1) * size]


def couple(integrals, labels, ab_pairs, cd_pairs, rows_to):
    blk = integrals.shape[0]
    tile = blk // 4
    table = labels.reshape(-1, 128)
    orbitals = jnp.concatenate([p.T.reshape(2, -1, 128) for p in (ab_pairs, cd_pairs)], axis=1)
    orbitals = orbitals.reshape(-1, 128)
    return pl.pallas_call(
        couple_kernel,
        grid_spec=pltpu.PrefetchScalarGridSpec(
            num_scalar_prefetch=1,
            grid=(4,),
            in_specs=[
                pl.BlockSpec((blk, tile), lambda i, *s: (0, i)),
                pl.BlockSpec(table.shape, lambda i, *s: (0, 0)),
                pl.BlockSpec(orbitals.shape, lambda i, *s: (0, 0)),
            ],
            out_specs=pl.BlockSpec((4, 1, tile // 4, blk), lambda i, *s: (0, i, 0, 0)),
            scratch_shapes=[pltpu.VMEM((2 * blk // 128, 128), jnp.float32)],
        ),
        out_shape=jax.ShapeDtypeStruct((4, 4, tile // 4, blk), integrals.dtype),
        compiler_params=pltpu.CompilerParams(vmem_limit_bytes=VMEM * 2**20),
        cost_estimate=pl.CostEstimate(flops=0, bytes_accessed=4 * blk * blk, transcendentals=0),
    )(rows_to, pltpu.with_memory_space_constraint(integrals, pltpu.HBM), table, orbitals)


def multiply_kernel(order_x, order_zl, coupled, *refs):
    blocks, outs, whole = refs[:4], refs[4:8], refs[8]
    depth = blocks[0].shape[0]
    size = depth // 4
    for k, ref in enumerate(blocks):
        for j in range(4):
            place = pl.multiple_of((order_x[k] * 4 + order_zl[j]) * size, 32)
            whole[pl.ds(place, size), :] = ref[j * size : (j + 1) * size, :]
    for k, out in enumerate(outs):
        rows = coupled[k * depth : (k + 1) * depth, :]
        out[...] = jnp.dot(rows, whole[...], preferred_element_type=jnp.float32).astype(out.dtype)


def multiply(coupled, blocks, order_x, order_zl):
    rows, depth = coupled.shape
    width = blocks[0].shape[1]
    part = jax.ShapeDtypeStruct((rows // 4, width), blocks[0].dtype)
    here = pl.BlockSpec(memory_space=pltpu.VMEM)
    return pl.pallas_call(
        multiply_kernel,
        in_specs=[pl.BlockSpec(memory_space=pltpu.SMEM)] * 2 + [here] * 5,
        out_specs=[here] * 4,
        scratch_shapes=[pltpu.VMEM((depth, width), blocks[0].dtype)],
        out_shape=[part] * 4,
        compiler_params=pltpu.CompilerParams(vmem_limit_bytes=VMEM * 2**20),
        cost_estimate=pl.CostEstimate(
            flops=2 * COST * rows * depth * width, bytes_accessed=rows * depth * 2, transcendentals=0
        ),
    )(as_ints(order_x), as_ints(order_zl), coupled, *blocks)


def as_ints(order):
    return jnp.stack([jnp.asarray(i, jnp.int32) for i in order])


def body(amplitudes, integrals, virt_irrep, pair_list):
    blk = integrals.shape[0]
    zh, y, x, zl, core = (lax.axis_index(a) for a in ("zh", "y", "x", "zl", "core"))

    near = gather("dir", amplitudes, "zl")
    near = jnp.concatenate(near, axis=0)

    cd_pairs = lax.dynamic_slice_in_dim(pair_list, (zh * 4 + y) * blk, blk, 0)
    ab_pairs = lax.dynamic_slice_in_dim(pair_list, (x * 4 + zl) * blk, blk, 0)
    order_zl = places("dir", zl, core)
    place_y = (jnp.arange(4, dtype=jnp.int32) - y) % 4
    coupled = couple(integrals, virt_irrep, ab_pairs, cd_pairs, place_y).reshape(blk, blk)

    if PREP_FIRST:
        near, coupled = lax.optimization_barrier((near, coupled))
    starts = [sum(WIDTHS[:k]) for k in range(len(WIDTHS))]
    product = []
    for start, width, kind in zip(starts, WIDTHS, GATHER_X):
        blocks = gather(kind, near[:, start : start + width], "x")
        product.append(multiply(coupled, blocks, places(kind, x, core), order_zl))
    done, over_ys = [], []
    earlier = None
    for part, kind in zip(product, SCATTER_Z):
        width = part[0].shape[-1]
        arrived = send(SCATTER_Y, part, "y")
        if earlier is not None and TIE:
            arrived, held = lax.optimization_barrier((arrived, earlier[1:]))
            earlier = (earlier[0], *held)
        over_y = finish(SCATTER_Y, *arrived, "y").reshape(4, -1, width)
        over_ys.append(over_y)
        if not MERGE_Z:
            blocks = pieces(over_y, places(kind, zh, core))
            if earlier is not None:
                done.append(finish(*earlier, "zh"))
            earlier = (kind, *send(kind, blocks, "zh"))
    if MERGE_Z:
        kind = SCATTER_Z[0]
        blocks = pieces(jnp.concatenate(over_ys, axis=-1), places(kind, zh, core))
        return finish(kind, *send(kind, blocks, "zh"), "zh")
    done.append(finish(*earlier, "zh"))
    return jnp.concatenate(done, axis=1)


def send(kind, blocks, axis):
    if kind == "dir":
        far = shift(blocks[2], axis, 2, -2)
        up = shift(blocks[1], axis, 1, 1)
        down = shift(blocks[3], axis, -1, -1)
        return blocks[0], far, up, down
    if kind == "rh":
        return blocks, swap(blocks[2:], axis, 1, 3)
    if kind == "rl":
        return blocks, shift(blocks[2], axis, 1, -1)
    return (lax.all_to_all(blocks, axis, 0, 0),)


def finish(kind, *arrived_axis):
    *arrived, axis = arrived_axis
    dtype = arrived[0].dtype
    if kind == "dir":
        return total(*arrived).astype(dtype)
    if kind == "rl":
        blocks, relayed = arrived
        core = lax.axis_index("core")
        add = lambda block, mine: jnp.where(mine, total(block, relayed), total(block)).astype(dtype)
        up = shift(add(blocks[1], core == 0), axis, 1, 1)
        down = shift(add(blocks[3], core == 1), axis, -1, -1)
        return total(blocks[0], up, down).astype(dtype)
    if kind == "rh":
        blocks, there = arrived
        kept = total(blocks[0], there[0])
        onward = total(blocks[1], there[1]).astype(dtype)
        return (kept + swap(onward, axis, 3, 1).astype(jnp.float32)).astype(dtype)
    return jnp.sum(arrived[0].astype(jnp.float32), axis=0).astype(dtype)


def solution(mesh):
    fine = Mesh(mesh.devices.reshape(4, 4, 4, 4, 2), ("zh", "y", "x", "zl", "core"))
    row, col = ("zh", "y"), ("x", "zl")
    placed = (P(row + col, "core"), P(row, col), P(), P())
    return jax.shard_map(
        body, mesh=fine, in_specs=placed, out_specs=P(col + row, "core"), check_vma=False
    )
```

time: 269 us -> 136 us (0.51)
  waiting for transfers between devices: 240 us -> 24.2 us
  starting transfers between devices: 0.04 us -> 87.5 us
  Pallas kernels: 0 us -> 12.9 us
  between operations: 13.4 us -> 0.53 us
  matrix products: 9.44 us -> 0 us
  local copies, waits for them, and re-layouts: 0.9 us -> 6.8 us
    reduce_scatter x1 -> x0, waiting for transfers between devices: 140 us -> none  [body(): lax.psum_scatter(rounded_term(lax.dot_general(coupled, block, contract, p...]
    all_gather x1 -> x0, waiting for transfers between devices: 99.4 us -> none  [body(): block = lax.all_gather(amplitudes, 'col', axis=0, tiled=True)]
    ppermute x0 -> x21, starting transfers between devices: none -> 87.5 us  [permute(): return lax.ppermute(block, (axis, 'core'), moves)]
    ppermute x0 -> x21, waiting for transfers between devices: none -> 24.2 us  [permute(): return lax.ppermute(block, (axis, 'core'), moves)]
    pallas_call x0 -> x3, Pallas kernels: none -> 12.9 us  [the longest x2 8.07 us: multiply(): pl.pallas_call(multiply_kernel, in_specs=[pl.BlockSpec(memory_space=pltpu...]
    dot_general x1 -> x0, matrix products: 9.44 us -> none  [body(): lax.dot_general(coupled, block, contract, preferred_element_type=jnp.floa...]
    unnamed x0 -> x8, local copies, waits for them, and re-layouts: none -> 5.17 us
    reduce_sum x1 -> x0, other arithmetic: 4.3 us -> none  [pair_symmetry(): jnp.sum(jnp.where(pairs[:, 1:2] == orbital, labels[None, :], 0), axis=1)]
  transfers between devices with their start and end apart: 2 -> 21, of which waited for: 2 -> 7; matrix products, arithmetic and copies ran while one was open for 2% -> 2% of each run, Pallas kernels for 0% -> 10%
where the time goes in v2:
time: 136 us; the launch traced here: 135 us
  starting transfers between devices  87.5 us (64%)
  waiting for transfers between devices  24.2 us (18%)
  Pallas kernels  12.9 us (9%)
  local copies, waits for them, and re-layouts  6.8 us (5%)
  other arithmetic  2.74 us (2%)
    ppermute x21, starting transfers between devices, permute(): return lax.ppermute(block, (axis, 'core'), moves)  87.5 us
    ppermute x21, waiting for transfers between devices, permute(): return lax.ppermute(block, (axis, 'core'), moves)  24.2 us
    pallas_call x2, Pallas kernels, multiply(): pl.pallas_call(multiply_kernel, in_specs=[pl.BlockSpec(memory_space=pltpu...  8.07 us
    unnamed x8, local copies, waits for them, and re-layouts  5.17 us
    pallas_call x1, Pallas kernels, couple(): pl.pallas_call(couple_kernel, grid_spec=pltpu.PrefetchScalarGridSpec(num_...  4.86 us
  transfers between devices with their start and end apart: 21, of which 7 were waited for; matrix products, arithmetic and copies ran while one was open for 2% of the time, Pallas kernels for 10%

profile of v2, /device:TPU:24, one launch (start us, length us, event | category | flops | bytes accessed | tf_op | source)
XLA Modules:
  0.0 134.7 jit_solution(13432463807848483635)
XLA Ops:
  0.0 6.5 %collective-permute-start = (bf16[96,1024]{1,0:T(8,128)(2,1)}, bf16[96,1024]{1,0:T(8,128)(2,1)S(1)}, u32[]{:S(2)}, u32[]{:S(2)}) collective-permute-start(bf16[96,1024]{1,0:T(8,128)(2,1)} %param.4), channel_id=1, source_target_pairs={{0,6},{1,7},{2,0},{3,1},{4,2},{5,3},{6,4},{7,5},{8,14},{9,15},{10,... | collective-permute-start | bytes 589832 | tf_op jit(solution)/shard_map/ppermute | solution.py:23
  6.5 1.9 %collective-permute-start.1 = (bf16[96,1024]{1,0:T(8,128)(2,1)}, bf16[96,1024]{1,0:T(8,128)(2,1)S(1)}, u32[]{:S(2)}, u32[]{:S(2)}) collective-permute-start(bf16[96,1024]{1,0:T(8,128)(2,1)} %param.4), channel_id=1, source_target_pairs={{0,4},{1,5},{2,6},{3,7},{4,0},{5,1},{6,2},{7,3},{8,12},{9,13},{10,... | collective-permute-start | bytes 589832 | tf_op jit(solution)/shard_map/ppermute | solution.py:23
  8.5 2.6 %collective-permute-start.2 = (bf16[96,1024]{1,0:T(8,128)(2,1)}, bf16[96,1024]{1,0:T(8,128)(2,1)S(1)}, u32[]{:S(2)}, u32[]{:S(2)}) collective-permute-start(bf16[96,1024]{1,0:T(8,128)(2,1)} %param.4), channel_id=1, source_target_pairs={{0,2},{1,3},{2,4},{3,5},{4,6},{5,7},{6,0},{7,1},{8,10},{9,11},{10,... | collective-permute-start | bytes 589832 | tf_op jit(solution)/shard_map/ppermute | solution.py:23
  11.1 0.7 dynamic-slice_bitcast_fusion.2
  11.9 0.0 copy-start.2
  11.9 0.7 copy-done.2
  12.5 4.9 %shard_map.46 = bf16[4,4,96,1536]{3,2,1,0:T(8,128)(2,1)S(1)} custom-call(s32[4]{0:T(128)S(1)} %and_select_fusion.rows_to, bf16[1536,1536]{1,0:T(8,128)(2,1)} %block.1, s32[6,128]{1,0:T(8,128)S(1)} %bitcast.41, s32[48,128]{1,0:T(8,128)S(1)} %bitcast.40), custom_call_target="tpu_custom_call" | custom-call | bytes 9437184 | tf_op jit(solution)/shard_map/pallas_call | solution.py:122
  17.4 2.1 %copy-done = bf16[4,4,96,1536]{3,2,1,0:T(8,128)(2,1)} copy-done((bf16[4,4,96,1536]{3,2,1,0:T(8,128)(2,1)}, bf16[4,4,96,1536]{3,2,1,0:T(8,128)(2,1)S(1)}, u32[]{:S(2)}) %copy-start) | copy-done | bytes 4718616
  19.6 4.3 %collective-permute-done.1 = bf16[96,1024]{1,0:T(8,128)(2,1)S(1)} collective-permute-done((bf16[96,1024]{1,0:T(8,128)(2,1)}, bf16[96,1024]{1,0:T(8,128)(2,1)S(1)}, u32[]{:S(2)}, u32[]{:S(2)}) %collective-permute-start.1) | collective-permute-done | bytes 196640 | tf_op jit(solution)/shard_map/ppermute | solution.py:23
  23.8 0.0 collective-permute-done.2
  23.8 0.1 pad_maximum_fusion
  23.9 0.8 fusion.9
  24.7 4.9 %collective-permute-start.10 = (bf16[384,512]{1,0:T(8,128)(2,1)S(1)}, bf16[384,512]{1,0:T(8,128)(2,1)S(1)}, u32[]{:S(2)}, u32[]{:S(2)}) collective-permute-start(bf16[384,512]{1,0:T(8,128)(2,1)S(1)} %get-tuple-element.37.refs_0_), channel_id=1, source_target_pairs={{0,16},{1,17},{8,24},{9,25},{16,0},{17,1},{24,8},{25,9},{2,18},{3,... | collective-permute-start | bytes 1179656 | tf_op jit(solution)/shard_map/ppermute | solution.py:23
  29.6 2.5 %collective-permute-start.11 = (bf16[384,512]{1,0:T(8,128)(2,1)S(1)}, bf16[384,512]{1,0:T(8,128)(2,1)S(1)}, u32[]{:S(2)}, u32[]{:S(2)}) collective-permute-start(bf16[384,512]{1,0:T(8,128)(2,1)S(1)} %get-tuple-element.37.refs_0_), channel_id=1, source_target_pairs={{0,8},{1,9},{8,16},{9,17},{16,24},{17,25},{24,0},{25,1},{2,10},{3,... | collective-permute-start | bytes 1179656 | tf_op jit(solution)/shard_map/ppermute | solution.py:23
  32.1 4.6 %collective-permute-start.9 = (bf16[384,512]{1,0:T(8,128)(2,1)S(1)}, bf16[384,512]{1,0:T(8,128)(2,1)S(1)}, u32[]{:S(2)}, u32[]{:S(2)}) collective-permute-start(bf16[384,512]{1,0:T(8,128)(2,1)S(1)} %get-tuple-element.37.refs_0_), channel_id=1, source_target_pairs={{0,24},{1,25},{8,0},{9,1},{16,8},{17,9},{24,16},{25,17},{2,26},{3,... | collective-permute-start | bytes 1179656 | tf_op jit(solution)/shard_map/ppermute | solution.py:23
  36.9 0.1 pad_add_fusion.1
  36.9 1.9 %collective-permute-start.3 = (bf16[384,512]{1,0:T(8,128)(2,1)}, bf16[384,512]{1,0:T(8,128)(2,1)}, u32[]{:S(2)}, u32[]{:S(2)}) collective-permute-start(bf16[384,512]{1,0:T(8,128)(2,1)} %get-tuple-element.38.refs_0_), channel_id=1, source_target_pairs={{0,24},{1,25},{8,0},{9,1},{16,8},{17,9},{24,16},{25,17},{2,26},{3,... | collective-permute-start | bytes 1179656 | tf_op jit(solution)/shard_map/ppermute | solution.py:23
  38.9 3.3 %collective-permute-start.4 = (bf16[384,512]{1,0:T(8,128)(2,1)}, bf16[384,512]{1,0:T(8,128)(2,1)}, u32[]{:S(2)}, u32[]{:S(2)}) collective-permute-start(bf16[384,512]{1,0:T(8,128)(2,1)} %get-tuple-element.38.refs_0_), channel_id=1, source_target_pairs={{0,16},{1,17},{8,24},{9,25},{16,0},{17,1},{24,8},{25,9},{2,18},{3,... | collective-permute-start | bytes 1179656 | tf_op jit(solution)/shard_map/ppermute | solution.py:23
  42.2 0.0 collective-permute-done.10.refs_2_
  42.2 2.5 %collective-permute-start.5 = (bf16[384,512]{1,0:T(8,128)(2,1)}, bf16[384,512]{1,0:T(8,128)(2,1)}, u32[]{:S(2)}, u32[]{:S(2)}) collective-permute-start(bf16[384,512]{1,0:T(8,128)(2,1)} %get-tuple-element.38.refs_0_), channel_id=1, source_target_pairs={{0,8},{1,9},{8,16},{9,17},{16,24},{17,25},{24,0},{25,1},{2,10},{3,... | collective-permute-start | bytes 1179656 | tf_op jit(solution)/shard_map/ppermute | solution.py:23
  44.7 3.9 %collective-permute-done.11.refs_3_ = bf16[384,512]{1,0:T(8,128)(2,1)S(1)} collective-permute-done((bf16[384,512]{1,0:T(8,128)(2,1)S(1)}, bf16[384,512]{1,0:T(8,128)(2,1)S(1)}, u32[]{:S(2)}, u32[]{:S(2)}) %collective-permute-start.11) | collective-permute-done | bytes 393248 | tf_op jit(solution)/shard_map/ppermute | solution.py:23
  48.7 0.0 collective-permute-done.9.refs_1_
  48.7 2.3 %copy-done.1 = bf16[4,4,96,1536]{3,2,1,0:T(8,128)(2,1)S(1)} copy-done((bf16[4,4,96,1536]{3,2,1,0:T(8,128)(2,1)S(1)}, bf16[4,4,96,1536]{3,2,1,0:T(8,128)(2,1)}, u32[]{:S(2)}) %copy-start.1) | copy-done | bytes 4718616
  51.0 4.0 %shard_map.48 = (bf16[384,512]{1,0:T(8,128)(2,1)S(1)}, bf16[384,512]{1,0:T(8,128)(2,1)}, bf16[384,512]{1,0:T(8,128)(2,1)}, bf16[384,512]{1,0:T(8,128)(2,1)}) custom-call(s32[4]{0:T(128)S(1)} %get-tuple-element.49.order_x, s32[4]{0:T(128)S(1)} %get-tuple-element.50.order_zl, bf16[1536,1536]{1,0:T(8,128)(2,1)S(1)} %bitcast.38, ...), custom_call_target="tpu_custom_call" | custom-call | flops 241591910400 | bytes 4718592 | tf_op jit(solution)/shard_map/pallas_call | solution.py:159
  55.0 3.1 %collective-permute-start.12 = (bf16[384,512]{1,0:T(8,128)(2,1)}, bf16[384,512]{1,0:T(8,128)(2,1)}, u32[]{:S(2)}, u32[]{:S(2)}) collective-permute-start(bf16[384,512]{1,0:T(8,128)(2,1)} %get-tuple-element.28), channel_id=1, source_target_pairs={{0,64},{1,65},{32,96},{33,97},{64,0},{65,1},{96,32},{97,33},{2,66}... | collective-permute-start | bytes 1179656 | tf_op jit(solution)/shard_map/ppermute | solution.py:23
  58.2 4.1 %collective-permute-start.13 = (bf16[384,512]{1,0:T(8,128)(2,1)}, bf16[384,512]{1,0:T(8,128)(2,1)}, u32[]{:S(2)}, u32[]{:S(2)}) collective-permute-start(bf16[384,512]{1,0:T(8,128)(2,1)} %get-tuple-element.29), channel_id=1, source_target_pairs={{0,32},{1,33},{32,64},{33,65},{64,96},{65,97},{96,0},{97,1},{2,34}... | collective-permute-start | bytes 1179656 | tf_op jit(solution)/shard_map/ppermute | solution.py:23
  62.3 1.9 %collective-permute-start.14 = (bf16[384,512]{1,0:T(8,128)(2,1)}, bf16[384,512]{1,0:T(8,128)(2,1)}, u32[]{:S(2)}, u32[]{:S(2)}) collective-permute-start(bf16[384,512]{1,0:T(8,128)(2,1)} %get-tuple-element.30), channel_id=1, source_target_pairs={{0,96},{1,97},{32,0},{33,1},{64,32},{65,33},{96,64},{97,65},{2,98}... | collective-permute-start | bytes 1179656 | tf_op jit(solution)/shard_map/ppermute | solution.py:23
  64.2 4.1 %shard_map.47 = (bf16[384,512]{1,0:T(8,128)(2,1)S(1)}, bf16[384,512]{1,0:T(8,128)(2,1)S(1)}, bf16[384,512]{1,0:T(8,128)(2,1)S(1)}, bf16[384,512]{1,0:T(8,128)(2,1)S(1)}) custom-call(s32[4]{0:T(128)S(1)} %get-tuple-element.49.order_x, s32[4]{0:T(128)S(1)} %get-tuple-element.50.order_zl, bf16[1536,1536]{1,0:T(8,128)(2,1)S(1)} %bitcast.39, ...), custom_call_target="tpu_custom_call" | custom-call | flops 241591910400 | bytes 4718592 | tf_op jit(solution)/shard_map/pallas_call | solution.py:159
  68.3 4.0 %collective-permute-start.6 = (bf16[384,512]{1,0:T(8,128)(2,1)S(1)}, bf16[384,512]{1,0:T(8,128)(2,1)S(1)}, u32[]{:S(2)}, u32[]{:S(2)}) collective-permute-start(bf16[384,512]{1,0:T(8,128)(2,1)S(1)} %get-tuple-element.24), channel_id=1, source_target_pairs={{0,64},{1,65},{32,96},{33,97},{64,0},{65,1},{96,32},{97,33},{2,66}... | collective-permute-start | bytes 1179656 | tf_op jit(solution)/shard_map/ppermute | solution.py:23
  72.3 3.0 %collective-permute-start.7 = (bf16[384,512]{1,0:T(8,128)(2,1)S(1)}, bf16[384,512]{1,0:T(8,128)(2,1)S(1)}, u32[]{:S(2)}, u32[]{:S(2)}) collective-permute-start(bf16[384,512]{1,0:T(8,128)(2,1)S(1)} %get-tuple-element.25), channel_id=1, source_target_pairs={{0,32},{1,33},{32,64},{33,65},{64,96},{65,97},{96,0},{97,1},{2,34}... | collective-permute-start | bytes 1179656 | tf_op jit(solution)/shard_map/ppermute | solution.py:23
  75.4 2.8 %collective-permute-start.8 = (bf16[384,512]{1,0:T(8,128)(2,1)S(1)}, bf16[384,512]{1,0:T(8,128)(2,1)S(1)}, u32[]{:S(2)}, u32[]{:S(2)}) collective-permute-start(bf16[384,512]{1,0:T(8,128)(2,1)S(1)} %get-tuple-element.26), channel_id=1, source_target_pairs={{0,96},{1,97},{32,0},{33,1},{64,32},{65,33},{96,64},{97,65},{2,98}... | collective-permute-start | bytes 1179656 | tf_op jit(solution)/shard_map/ppermute | solution.py:23
  78.2 0.9 collective-permute-done.14
  79.2 1.4 %add_convert_fusion.1 = bf16[384,512]{1,0:T(8,128)(2,1)S(1)} fusion(bf16[384,512]{1,0:T(8,128)(2,1)} %collective-permute-done.14, bf16[384,512]{1,0:T(8,128)(2,1)} %collective-permute-done.13, bf16[384,512]{1,0:T(8,128)(2,1)} %collective-permute-done.12, bf16[384,512]{1,0:T(8,128)(2,1)S(1)} %get-tuple-element.27), kind=kLoop, calls=%fused_computation.2 | loop fusion | flops 1572864 | bytes 1966080 | tf_op jit(solution)/shard_map/convert_element_type | solution.py:236
  80.6 9.1 %collective-permute-start.15 = (bf16[96,512]{1,0:T(8,128)(2,1)S(1)}, bf16[96,512]{1,0:T(8,128)(2,1)S(1)}, u32[]{:S(2)}, u32[]{:S(2)}) collective-permute-start(bf16[96,512]{1,0:T(8,128)(2,1)S(1)} %bitcast.46), channel_id=1, source_target_pairs={{0,128},{1,385},{128,256},{129,1},{256,384},{257,129},{384,0},{385... | collective-permute-start | bytes 294920 | tf_op jit(solution)/shard_map/ppermute | solution.py:23
  89.8 0.1 pad_maximum_fusion.1
  89.8 2.5 %collective-permute-done.7 = bf16[384,512]{1,0:T(8,128)(2,1)S(1)} collective-permute-done((bf16[384,512]{1,0:T(8,128)(2,1)S(1)}, bf16[384,512]{1,0:T(8,128)(2,1)S(1)}, u32[]{:S(2)}, u32[]{:S(2)}) %collective-permute-start.7) | collective-permute-done | bytes 393248 | tf_op jit(solution)/shard_map/ppermute | solution.py:23
  92.3 2.4 %collective-permute-done.8 = bf16[384,512]{1,0:T(8,128)(2,1)S(1)} collective-permute-done((bf16[384,512]{1,0:T(8,128)(2,1)S(1)}, bf16[384,512]{1,0:T(8,128)(2,1)S(1)}, u32[]{:S(2)}, u32[]{:S(2)}) %collective-permute-start.8) | collective-permute-done | bytes 393248 | tf_op jit(solution)/shard_map/ppermute | solution.py:23
  94.7 0.2 add_convert_fusion
  94.9 9.1 %collective-permute-start.18 = (bf16[96,512]{1,0:T(8,128)(2,1)S(1)}, bf16[96,512]{1,0:T(8,128)(2,1)S(1)}, u32[]{:S(2)}, u32[]{:S(2)}) collective-permute-start(bf16[96,512]{1,0:T(8,128)(2,1)S(1)} %dynamic-slice_bitcast_fusion), channel_id=1, source_target_pairs={{0,128},{1,385},{128,256},{129,1},{256,384},{257,129},{384,0},{385... | collective-permute-start | bytes 294920 | tf_op jit(solution)/shard_map/ppermute | solution.py:23
  104.0 0.1 fusion
  104.1 7.1 %collective-permute-start.16 = (bf16[96,512]{1,0:T(8,128)(2,1)S(1)}, bf16[96,512]{1,0:T(8,128)(2,1)S(1)}, u32[]{:S(2)}, u32[]{:S(2)}) collective-permute-start(bf16[96,512]{1,0:T(8,128)(2,1)S(1)} %get-tuple-element.39), channel_id=1, source_target_pairs={{0,128},{1,129},{128,256},{129,257},{256,384},{257,385},{384,0},{3... | collective-permute-start | bytes 294920 | tf_op jit(solution)/shard_map/ppermute | solution.py:23
  111.2 2.7 %collective-permute-start.17 = (bf16[96,512]{1,0:T(8,128)(2,1)S(1)}, bf16[96,512]{1,0:T(8,128)(2,1)S(1)}, u32[]{:S(2)}, u32[]{:S(2)}) collective-permute-start(bf16[96,512]{1,0:T(8,128)(2,1)S(1)} %get-tuple-element.40), channel_id=1, source_target_pairs={{0,384},{1,385},{128,0},{129,1},{256,128},{257,129},{384,256},{385... | collective-permute-start | bytes 294920 | tf_op jit(solution)/shard_map/ppermute | solution.py:23
  113.9 0.1 fusion.2
  113.9 7.1 %collective-permute-start.19 = (bf16[96,512]{1,0:T(8,128)(2,1)S(1)}, bf16[96,512]{1,0:T(8,128)(2,1)S(1)}, u32[]{:S(2)}, u32[]{:S(2)}) collective-permute-start(bf16[96,512]{1,0:T(8,128)(2,1)S(1)} %get-tuple-element.41), channel_id=1, source_target_pairs={{0,128},{1,129},{128,256},{129,257},{256,384},{257,385},{384,0},{3... | collective-permute-start | bytes 294920 | tf_op jit(solution)/shard_map/ppermute | solution.py:23
  121.0 2.7 %collective-permute-start.20 = (bf16[96,512]{1,0:T(8,128)(2,1)S(1)}, bf16[96,512]{1,0:T(8,128)(2,1)S(1)}, u32[]{:S(2)}, u32[]{:S(2)}) collective-permute-start(bf16[96,512]{1,0:T(8,128)(2,1)S(1)} %get-tuple-element.42), channel_id=1, source_target_pairs={{0,384},{1,385},{128,0},{129,1},{256,128},{257,129},{384,256},{385... | collective-permute-start | bytes 294920 | tf_op jit(solution)/shard_map/ppermute | solution.py:23
  123.8 6.3 %collective-permute-done.19 = bf16[96,512]{1,0:T(8,128)(2,1)S(1)} collective-permute-done((bf16[96,512]{1,0:T(8,128)(2,1)S(1)}, bf16[96,512]{1,0:T(8,128)(2,1)S(1)}, u32[]{:S(2)}, u32[]{:S(2)}) %collective-permute-start.19) | collective-permute-done | bytes 98336 | tf_op jit(solution)/shard_map/ppermute | solution.py:23
  130.1 3.8 %collective-permute-done.20 = bf16[96,512]{1,0:T(8,128)(2,1)S(1)} collective-permute-done((bf16[96,512]{1,0:T(8,128)(2,1)S(1)}, bf16[96,512]{1,0:T(8,128)(2,1)S(1)}, u32[]{:S(2)}, u32[]{:S(2)}) %collective-permute-start.20) | collective-permute-done | bytes 98336 | tf_op jit(solution)/shard_map/ppermute | solution.py:23
  134.0 0.7 pad_maximum_fusion.2
  (23 shorter events, 0.2 us)
Async XLA Ops:
  0.0 19.6 %collective-permute-start = (bf16[96,1024]{1,0:T(8,128)(2,1)}, bf16[96,1024]{1,0:T(8,128)(2,1)S(1)}, u32[]{:S(2)}, u32[]{:S(2)}) collective-permute-start(bf16[96,1024]{1,0:T(8,128)(2,1)} %param.4), channel_id=1, source_target_pairs={{0,6},{1,7},{2,0},{3,1},{4,2},{5,3},{6,4},{7,5},{8,14},{9,15},{10,... | collective-permute-start | bytes 589832 | tf_op jit(solution)/shard_map/ppermute | solution.py:23
  6.5 17.3 %collective-permute-start.1 = (bf16[96,1024]{1,0:T(8,128)(2,1)}, bf16[96,1024]{1,0:T(8,128)(2,1)S(1)}, u32[]{:S(2)}, u32[]{:S(2)}) collective-permute-start(bf16[96,1024]{1,0:T(8,128)(2,1)} %param.4), channel_id=1, source_target_pairs={{0,4},{1,5},{2,6},{3,7},{4,0},{5,1},{6,2},{7,3},{8,12},{9,13},{10,... | collective-permute-start | bytes 589832 | tf_op jit(solution)/shard_map/ppermute | solution.py:23
  8.5 15.4 %collective-permute-start.2 = (bf16[96,1024]{1,0:T(8,128)(2,1)}, bf16[96,1024]{1,0:T(8,128)(2,1)S(1)}, u32[]{:S(2)}, u32[]{:S(2)}) collective-permute-start(bf16[96,1024]{1,0:T(8,128)(2,1)} %param.4), channel_id=1, source_target_pairs={{0,2},{1,3},{2,4},{3,5},{4,6},{5,7},{6,0},{7,1},{8,10},{9,11},{10,... | collective-permute-start | bytes 589832 | tf_op jit(solution)/shard_map/ppermute | solution.py:23
  11.9 0.7 copy-start.2
  12.5 11.3 %copy-start.3 = (bf16[96,1024]{1,0:T(8,128)(2,1)S(1)}, bf16[96,1024]{1,0:T(8,128)(2,1)}, u32[]{:S(2)}) copy-start(bf16[96,1024]{1,0:T(8,128)(2,1)} %param.4) | copy-start | bytes 589828
  17.4 2.2 %copy-start = (bf16[4,4,96,1536]{3,2,1,0:T(8,128)(2,1)}, bf16[4,4,96,1536]{3,2,1,0:T(8,128)(2,1)S(1)}, u32[]{:S(2)}) copy-start(bf16[4,4,96,1536]{3,2,1,0:T(8,128)(2,1)S(1)} %shard_map.46) | copy-start | bytes 14155780
  24.7 17.5 %collective-permute-start.10 = (bf16[384,512]{1,0:T(8,128)(2,1)S(1)}, bf16[384,512]{1,0:T(8,128)(2,1)S(1)}, u32[]{:S(2)}, u32[]{:S(2)}) collective-permute-start(bf16[384,512]{1,0:T(8,128)(2,1)S(1)} %get-tuple-element.37.refs_0_), channel_id=1, source_target_pairs={{0,16},{1,17},{8,24},{9,25},{16,0},{17,1},{24,8},{25,9},{2,18},{3,... | collective-permute-start | bytes 1179656 | tf_op jit(solution)/shard_map/ppermute | solution.py:23
  29.6 19.0 %collective-permute-start.11 = (bf16[384,512]{1,0:T(8,128)(2,1)S(1)}, bf16[384,512]{1,0:T(8,128)(2,1)S(1)}, u32[]{:S(2)}, u32[]{:S(2)}) collective-permute-start(bf16[384,512]{1,0:T(8,128)(2,1)S(1)} %get-tuple-element.37.refs_0_), channel_id=1, source_target_pairs={{0,8},{1,9},{8,16},{9,17},{16,24},{17,25},{24,0},{25,1},{2,10},{3,... | collective-permute-start | bytes 1179656 | tf_op jit(solution)/shard_map/ppermute | solution.py:23
  32.1 16.5 %collective-permute-start.9 = (bf16[384,512]{1,0:T(8,128)(2,1)S(1)}, bf16[384,512]{1,0:T(8,128)(2,1)S(1)}, u32[]{:S(2)}, u32[]{:S(2)}) collective-permute-start(bf16[384,512]{1,0:T(8,128)(2,1)S(1)} %get-tuple-element.37.refs_0_), channel_id=1, source_target_pairs={{0,24},{1,25},{8,0},{9,1},{16,8},{17,9},{24,16},{25,17},{2,26},{3,... | collective-permute-start | bytes 1179656 | tf_op jit(solution)/shard_map/ppermute | solution.py:23
  36.9 25.3 %collective-permute-start.3 = (bf16[384,512]{1,0:T(8,128)(2,1)}, bf16[384,512]{1,0:T(8,128)(2,1)}, u32[]{:S(2)}, u32[]{:S(2)}) collective-permute-start(bf16[384,512]{1,0:T(8,128)(2,1)} %get-tuple-element.38.refs_0_), channel_id=1, source_target_pairs={{0,24},{1,25},{8,0},{9,1},{16,8},{17,9},{24,16},{25,17},{2,26},{3,... | collective-permute-start | bytes 1179656 | tf_op jit(solution)/shard_map/ppermute | solution.py:23
  38.9 25.3 %collective-permute-start.4 = (bf16[384,512]{1,0:T(8,128)(2,1)}, bf16[384,512]{1,0:T(8,128)(2,1)}, u32[]{:S(2)}, u32[]{:S(2)}) collective-permute-start(bf16[384,512]{1,0:T(8,128)(2,1)} %get-tuple-element.38.refs_0_), channel_id=1, source_target_pairs={{0,16},{1,17},{8,24},{9,25},{16,0},{17,1},{24,8},{25,9},{2,18},{3,... | collective-permute-start | bytes 1179656 | tf_op jit(solution)/shard_map/ppermute | solution.py:23
  42.2 22.0 %collective-permute-start.5 = (bf16[384,512]{1,0:T(8,128)(2,1)}, bf16[384,512]{1,0:T(8,128)(2,1)}, u32[]{:S(2)}, u32[]{:S(2)}) collective-permute-start(bf16[384,512]{1,0:T(8,128)(2,1)} %get-tuple-element.38.refs_0_), channel_id=1, source_target_pairs={{0,8},{1,9},{8,16},{9,17},{16,24},{17,25},{24,0},{25,1},{2,10},{3,... | collective-permute-start | bytes 1179656 | tf_op jit(solution)/shard_map/ppermute | solution.py:23
  48.7 2.3 %copy-start.1 = (bf16[4,4,96,1536]{3,2,1,0:T(8,128)(2,1)S(1)}, bf16[4,4,96,1536]{3,2,1,0:T(8,128)(2,1)}, u32[]{:S(2)}) copy-start(bf16[4,4,96,1536]{3,2,1,0:T(8,128)(2,1)} %copy-done) | copy-start | bytes 14155780
  55.0 20.3 %collective-permute-start.12 = (bf16[384,512]{1,0:T(8,128)(2,1)}, bf16[384,512]{1,0:T(8,128)(2,1)}, u32[]{:S(2)}, u32[]{:S(2)}) collective-permute-start(bf16[384,512]{1,0:T(8,128)(2,1)} %get-tuple-element.28), channel_id=1, source_target_pairs={{0,64},{1,65},{32,96},{33,97},{64,0},{65,1},{96,32},{97,33},{2,66}... | collective-permute-start | bytes 1179656 | tf_op jit(solution)/shard_map/ppermute | solution.py:23
  58.2 20.0 %collective-permute-start.13 = (bf16[384,512]{1,0:T(8,128)(2,1)}, bf16[384,512]{1,0:T(8,128)(2,1)}, u32[]{:S(2)}, u32[]{:S(2)}) collective-permute-start(bf16[384,512]{1,0:T(8,128)(2,1)} %get-tuple-element.29), channel_id=1, source_target_pairs={{0,32},{1,33},{32,64},{33,65},{64,96},{65,97},{96,0},{97,1},{2,34}... | collective-permute-start | bytes 1179656 | tf_op jit(solution)/shard_map/ppermute | solution.py:23
  62.3 16.9 %collective-permute-start.14 = (bf16[384,512]{1,0:T(8,128)(2,1)}, bf16[384,512]{1,0:T(8,128)(2,1)}, u32[]{:S(2)}, u32[]{:S(2)}) collective-permute-start(bf16[384,512]{1,0:T(8,128)(2,1)} %get-tuple-element.30), channel_id=1, source_target_pairs={{0,96},{1,97},{32,0},{33,1},{64,32},{65,33},{96,64},{97,65},{2,98}... | collective-permute-start | bytes 1179656 | tf_op jit(solution)/shard_map/ppermute | solution.py:23
  68.3 21.5 %collective-permute-start.6 = (bf16[384,512]{1,0:T(8,128)(2,1)S(1)}, bf16[384,512]{1,0:T(8,128)(2,1)S(1)}, u32[]{:S(2)}, u32[]{:S(2)}) collective-permute-start(bf16[384,512]{1,0:T(8,128)(2,1)S(1)} %get-tuple-element.24), channel_id=1, source_target_pairs={{0,64},{1,65},{32,96},{33,97},{64,0},{65,1},{96,32},{97,33},{2,66}... | collective-permute-start | bytes 1179656 | tf_op jit(solution)/shard_map/ppermute | solution.py:23
  72.3 20.0 %collective-permute-start.7 = (bf16[384,512]{1,0:T(8,128)(2,1)S(1)}, bf16[384,512]{1,0:T(8,128)(2,1)S(1)}, u32[]{:S(2)}, u32[]{:S(2)}) collective-permute-start(bf16[384,512]{1,0:T(8,128)(2,1)S(1)} %get-tuple-element.25), channel_id=1, source_target_pairs={{0,32},{1,33},{32,64},{33,65},{64,96},{65,97},{96,0},{97,1},{2,34}... | collective-permute-start | bytes 1179656 | tf_op jit(solution)/shard_map/ppermute | solution.py:23
  75.4 19.3 %collective-permute-start.8 = (bf16[384,512]{1,0:T(8,128)(2,1)S(1)}, bf16[384,512]{1,0:T(8,128)(2,1)S(1)}, u32[]{:S(2)}, u32[]{:S(2)}) collective-permute-start(bf16[384,512]{1,0:T(8,128)(2,1)S(1)} %get-tuple-element.26), channel_id=1, source_target_pairs={{0,96},{1,97},{32,0},{33,1},{64,32},{65,33},{96,64},{97,65},{2,98}... | collective-permute-start | bytes 1179656 | tf_op jit(solution)/shard_map/ppermute | solution.py:23
  80.6 14.0 %collective-permute-start.15 = (bf16[96,512]{1,0:T(8,128)(2,1)S(1)}, bf16[96,512]{1,0:T(8,128)(2,1)S(1)}, u32[]{:S(2)}, u32[]{:S(2)}) collective-permute-start(bf16[96,512]{1,0:T(8,128)(2,1)S(1)} %bitcast.46), channel_id=1, source_target_pairs={{0,128},{1,385},{128,256},{129,1},{256,384},{257,129},{384,0},{385... | collective-permute-start | bytes 294920 | tf_op jit(solution)/shard_map/ppermute | solution.py:23
  94.9 18.9 %collective-permute-start.18 = (bf16[96,512]{1,0:T(8,128)(2,1)S(1)}, bf16[96,512]{1,0:T(8,128)(2,1)S(1)}, u32[]{:S(2)}, u32[]{:S(2)}) collective-permute-start(bf16[96,512]{1,0:T(8,128)(2,1)S(1)} %dynamic-slice_bitcast_fusion), channel_id=1, source_target_pairs={{0,128},{1,385},{128,256},{129,1},{256,384},{257,129},{384,0},{385... | collective-permute-start | bytes 294920 | tf_op jit(solution)/shard_map/ppermute | solution.py:23
  104.1 19.6 %collective-permute-start.16 = (bf16[96,512]{1,0:T(8,128)(2,1)S(1)}, bf16[96,512]{1,0:T(8,128)(2,1)S(1)}, u32[]{:S(2)}, u32[]{:S(2)}) collective-permute-start(bf16[96,512]{1,0:T(8,128)(2,1)S(1)} %get-tuple-element.39), channel_id=1, source_target_pairs={{0,128},{1,129},{128,256},{129,257},{256,384},{257,385},{384,0},{3... | collective-permute-start | bytes 294920 | tf_op jit(solution)/shard_map/ppermute | solution.py:23
  111.2 12.6 %collective-permute-start.17 = (bf16[96,512]{1,0:T(8,128)(2,1)S(1)}, bf16[96,512]{1,0:T(8,128)(2,1)S(1)}, u32[]{:S(2)}, u32[]{:S(2)}) collective-permute-start(bf16[96,512]{1,0:T(8,128)(2,1)S(1)} %get-tuple-element.40), channel_id=1, source_target_pairs={{0,384},{1,385},{128,0},{129,1},{256,128},{257,129},{384,256},{385... | collective-permute-start | bytes 294920 | tf_op jit(solution)/shard_map/ppermute | solution.py:23
  113.9 16.1 %collective-permute-start.19 = (bf16[96,512]{1,0:T(8,128)(2,1)S(1)}, bf16[96,512]{1,0:T(8,128)(2,1)S(1)}, u32[]{:S(2)}, u32[]{:S(2)}) collective-permute-start(bf16[96,512]{1,0:T(8,128)(2,1)S(1)} %get-tuple-element.41), channel_id=1, source_target_pairs={{0,128},{1,129},{128,256},{129,257},{256,384},{257,385},{384,0},{3... | collective-permute-start | bytes 294920 | tf_op jit(solution)/shard_map/ppermute | solution.py:23
  121.0 12.9 %collective-permute-start.20 = (bf16[96,512]{1,0:T(8,128)(2,1)S(1)}, bf16[96,512]{1,0:T(8,128)(2,1)S(1)}, u32[]{:S(2)}, u32[]{:S(2)}) collective-permute-start(bf16[96,512]{1,0:T(8,128)(2,1)S(1)} %get-tuple-element.42), channel_id=1, source_target_pairs={{0,384},{1,385},{128,0},{129,1},{256,128},{257,129},{384,256},{385... | collective-permute-start | bytes 294920 | tf_op jit(solution)/shard_map/ppermute | solution.py:23

commit v3 on v2

v3 whole, which is shorter than its diff:
```python
import jax
import jax.numpy as jnp
from jax import lax
from jax.experimental import pallas as pl
from jax.experimental.pallas import tpu as pltpu
from jax.sharding import Mesh, PartitionSpec as P

WIDTHS = (384, 640)
SCATTER_Z = ("rl", "rh")
VMEM = 32


def permute(block, axis, target):
    moves = [(i * 2 + core, target(i, core) % 4 * 2 + core) for i in range(4) for core in (0, 1)]
    return lax.ppermute(block, (axis, "core"), moves)


def shift(block, axis, first, second):
    return permute(block, axis, lambda i, core: i + (second if core else first))


def swap(block, axis, first, second):
    return permute(block, axis, lambda i, core: i ^ (second if core else first))


def total(*terms):
    return sum(t.astype(jnp.float32) for t in terms)


def places(kind, me, core):
    if kind in ("dir", "rl"):
        return [(me + d) % 4 for d in range(4)]
    near = jnp.where(core == 0, 3, 1)
    return [me, me ^ near, me ^ near ^ 2, me ^ 2]


def gather(own, axis):
    far = shift(own, axis, 2, -2)
    after = shift(own, axis, -1, -1)
    return [own, after, far, shift(own, axis, 1, 1)]


def pieces(blocks, order):
    return jnp.stack([lax.dynamic_index_in_dim(blocks, i, 0, keepdims=False) for i in order])


def lookup(table, index):
    found = jnp.zeros(index.shape, table.dtype)
    for row in range(table.shape[0]):
        line = jnp.broadcast_to(table[row : row + 1, :], index.shape)
        value = jnp.take_along_axis(line, index & 127, axis=1)
        found = jnp.where(index >> 7 == row, value, found)
    return found


def couple_kernel(rows_to, block, table, orbitals, out, done, labels):
    step = pl.program_id(0)
    tile, blk = block.shape[1], block.shape[0]
    lines = blk // 128

    @pl.when(step == 0)
    def _():
        symmetry = lookup(table[...], orbitals[...]).astype(jnp.float32)
        first, second = symmetry[: 2 * lines].astype(jnp.int32), symmetry[2 * lines :].astype(jnp.int32)
        labels[...] = jnp.bitwise_xor(first, second).astype(jnp.float32)

    done[...] = jnp.zeros(done.shape, done.dtype)
    mine = []
    for k in range(tile // 128):
        line = labels[pl.ds(step * (tile // 128) + k, 1), :]
        mine.append(jnp.broadcast_to(line, (128, 128)).T.astype(block.dtype))
    mine = jnp.concatenate(mine, axis=0)
    turned = block[...].T
    size = tile // 4
    for j in range(lines):
        across = slice(j * 128, (j + 1) * 128)
        other = labels[lines + j : lines + j + 1, :].astype(block.dtype)
        masked = jnp.where(mine == other, turned[:, across], jnp.zeros((), block.dtype))
        for k in range(4):
            out[rows_to[k], 0, :, across] = masked[k * size : (k + 1) * size]


def couple(integrals, labels, ab_pairs, cd_pairs, rows_to):
    blk = integrals.shape[0]
    tile = blk // 4
    table = labels.reshape(-1, 128)
    orbitals = jnp.concatenate([p.T.reshape(2, -1, 128) for p in (ab_pairs, cd_pairs)], axis=1)
    orbitals = orbitals.reshape(-1, 128)
    return pl.pallas_call(
        couple_kernel,
        grid_spec=pltpu.PrefetchScalarGridSpec(
            num_scalar_prefetch=1,
            grid=(4,),
            in_specs=[
                pl.BlockSpec((blk, tile), lambda i, *s: (0, i)),
                pl.BlockSpec(table.shape, lambda i, *s: (0, 0)),
                pl.BlockSpec(orbitals.shape, lambda i, *s: (0, 0)),
            ],
            out_specs=[
                pl.BlockSpec((4, 1, tile // 4, blk), lambda i, *s: (0, i, 0, 0)),
                pl.BlockSpec((8, 128), lambda i, *s: (0, 0)),
            ],
            scratch_shapes=[pltpu.VMEM((2 * blk // 128, 128), jnp.float32)],
        ),
        out_shape=[
            jax.ShapeDtypeStruct((4, 4, tile // 4, blk), integrals.dtype),
            jax.ShapeDtypeStruct((8, 128), jnp.float32),
        ],
        compiler_params=pltpu.CompilerParams(vmem_limit_bytes=VMEM * 2**20),
        cost_estimate=pl.CostEstimate(flops=0, bytes_accessed=4 * blk * blk, transcendentals=0),
    )(rows_to, pltpu.with_memory_space_constraint(integrals, pltpu.HBM), table, orbitals)


def multiply_kernel(order, coupled, *refs):
    *blocks, out, whole = refs
    depth = blocks[0].shape[0]

    @pl.when(pl.program_id(0) == 0)
    def _():
        for k, ref in enumerate(blocks):
            whole[pl.ds(pl.multiple_of(order[k] * depth, 128), depth), :] = ref[...]

    out[...] = jnp.dot(coupled[...], whole[...], preferred_element_type=jnp.float32).astype(out.dtype)[None]


def multiply(coupled, blocks, order):
    rows, depth = coupled.shape
    width = blocks[0].shape[1]
    tile = rows // 4
    one = pl.BlockSpec(blocks[0].shape, lambda i, s: (0, 0))
    return pl.pallas_call(
        multiply_kernel,
        grid_spec=pltpu.PrefetchScalarGridSpec(
            num_scalar_prefetch=1,
            grid=(4,),
            in_specs=[pl.BlockSpec((tile, depth), lambda i, s: (i, 0))] + [one] * 4,
            out_specs=pl.BlockSpec((1, tile, width), lambda i, s: (i, 0, 0)),
            scratch_shapes=[pltpu.VMEM((depth, width), blocks[0].dtype)],
        ),
        out_shape=jax.ShapeDtypeStruct((4, tile, width), blocks[0].dtype),
        compiler_params=pltpu.CompilerParams(vmem_limit_bytes=VMEM * 2**20),
        cost_estimate=pl.CostEstimate(
            flops=2 * rows * depth * width, bytes_accessed=rows * depth * 2, transcendentals=0
        ),
    )(as_ints(order), coupled, *blocks)


def as_ints(order):
    return jnp.stack([jnp.asarray(i).astype(jnp.int32) for i in order])


def body(amplitudes, integrals, virt_irrep, pair_list):
    blk = integrals.shape[0]
    zh, y, x, zl, core = (lax.axis_index(a) for a in ("zh", "y", "x", "zl", "core"))

    near = lax.all_gather(amplitudes, "zl", axis=0, tiled=True)

    cd_pairs = lax.dynamic_slice_in_dim(pair_list, (zh * 4 + y) * blk, blk, 0)
    ab_pairs = lax.dynamic_slice_in_dim(pair_list, (x * 4 + zl) * blk, blk, 0)
    order_y = places("dir", y, core)
    place_y = as_ints([sum(k * (order_y[k] == to) for k in range(4)) for to in range(4)])
    coupled, masked = couple(integrals, virt_irrep, ab_pairs, cd_pairs, place_y)
    coupled = coupled.reshape(blk, blk)

    product, start = [], 0
    for width in WIDTHS:
        part = near[:, start : start + width]
        if start:
            part, masked = lax.optimization_barrier((part, masked))
        start += width
        product.append(multiply(coupled, gather(part, "x"), places("dir", x, core)))

    done, earlier = [], None
    for part, kind in zip(product, SCATTER_Z):
        arrived = send("dir", part, "y")
        if earlier is not None:
            arrived, held = lax.optimization_barrier((arrived, earlier[1:]))
            earlier = (earlier[0], *held)
        over_y = finish("dir", *arrived, "y").reshape(4, -1, part.shape[-1])
        blocks = pieces(over_y, places(kind, zh, core))
        if earlier is not None:
            done.append(finish(*earlier, "zh"))
        earlier = (kind, *send(kind, blocks, "zh"))
    done.append(finish(*earlier, "zh"))
    return jnp.concatenate(done, axis=1)


def send(kind, blocks, axis):
    if kind == "dir":
        far = shift(blocks[2], axis, 2, -2)
        up = shift(blocks[1], axis, 1, 1)
        down = shift(blocks[3], axis, -1, -1)
        return blocks[0], far, up, down
    if kind == "rh":
        return blocks, swap(blocks[2:], axis, 1, 3)
    return blocks, shift(blocks[2], axis, 1, -1)


def finish(kind, *arrived_axis):
    *arrived, axis = arrived_axis
    dtype = arrived[0].dtype
    if kind == "dir":
        return total(*arrived).astype(dtype)
    if kind == "rl":
        blocks, relayed = arrived
        core = lax.axis_index("core")
        add = lambda block, mine: jnp.where(mine, total(block, relayed), total(block)).astype(dtype)
        up = shift(add(blocks[1], core == 0), axis, 1, 1)
        down = shift(add(blocks[3], core == 1), axis, -1, -1)
        return total(blocks[0], up, down).astype(dtype)
    blocks, there = arrived
    kept = total(blocks[0], there[0])
    onward = total(blocks[1], there[1]).astype(dtype)
    return (kept + swap(onward, axis, 3, 1).astype(jnp.float32)).astype(dtype)


def solution(mesh):
    fine = Mesh(mesh.devices.reshape(4, 4, 4, 4, 2), ("zh", "y", "x", "zl", "core"))
    row, col = ("zh", "y"), ("x", "zl")
    placed = (P(row + col, "core"), P(row, col), P(), P())
    return jax.shard_map(
        body, mesh=fine, in_specs=placed, out_specs=P(col + row, "core"), check_vma=False
    )
```

time: 136 us -> 135 us (level)
  blocking collectives: 0 us -> 21.2 us
  starting transfers between devices: 87.5 us -> 68.7 us
  local copies, waits for them, and re-layouts: 6.8 us -> 1.2 us
  waiting for transfers between devices: 24.2 us -> 26.7 us
  Pallas kernels: 12.9 us -> 14.4 us
    all_gather x0 -> x1, blocking collectives: none -> 21.2 us  [body(): near = lax.all_gather(amplitudes, 'zl', axis=0, tiled=True)]
    ppermute x21 -> x17, starting transfers between devices: 87.5 us -> 68.7 us  [permute(): return lax.ppermute(block, (axis, 'core'), moves)]
    unnamed x8 -> x2, local copies, waits for them, and re-layouts: 5.17 us -> 0.01 us
    ppermute x21 -> x17, waiting for transfers between devices: 24.2 us -> 26.7 us  [permute(): return lax.ppermute(block, (axis, 'core'), moves)]
  transfers between devices with their start and end apart: 21 -> 17, of which waited for: 7 -> 6; matrix products, arithmetic and copies ran while one was open for 2% -> 1% of each run, Pallas kernels for 10% -> 11%
where the time goes in v3:
time: 135 us; the launch traced here: 134 us
  starting transfers between devices  68.7 us (51%)
  waiting for transfers between devices  26.7 us (20%)
  blocking collectives  21.2 us (16%)
  Pallas kernels  14.4 us (11%)
  other arithmetic  1.51 us (1%)
    ppermute x17, starting transfers between devices, permute(): return lax.ppermute(block, (axis, 'core'), moves)  68.7 us
    ppermute x17, waiting for transfers between devices, permute(): return lax.ppermute(block, (axis, 'core'), moves)  26.7 us
    all_gather x1, blocking collectives, body(): near = lax.all_gather(amplitudes, 'zl', axis=0, tiled=True)  21.2 us
    pallas_call x2, Pallas kernels, multiply(): pl.pallas_call(multiply_kernel, grid_spec=pltpu.PrefetchScalarGridSpec(nu...  8.94 us
    pallas_call x1, Pallas kernels, couple(): pl.pallas_call(couple_kernel, grid_spec=pltpu.PrefetchScalarGridSpec(num_...  5.44 us
  transfers between devices with their start and end apart: 17, of which 6 were waited for; matrix products, arithmetic and copies ran while one was open for 1% of the time, Pallas kernels for 11%

profile of v3, /device:TPU:24, one launch (start us, length us, event | category | flops | bytes accessed | tf_op | source)
XLA Modules:
  0.0 134.2 jit_solution(11314748733489683456)
XLA Ops:
  0.0 21.2 %all_gather.3 = bf16[384,1024]{1,0:T(8,128)(2,1)S(1)} all-gather(bf16[96,1024]{1,0:T(8,128)(2,1)} %param.4), channel_id=1, replica_groups=mesh['zh'=4,'y'=4,'x'=4,'zl'=4,'core'=2] {'zl'}, dimensions={0}, use_global_device_ids=true | all-gather | bytes 983040 | tf_op jit(solution)/shard_map/all_gather | solution.py:156
  21.2 4.7 %collective-permute-start.6 = (bf16[384,384]{1,0:T(8,128)(2,1)S(1)}, bf16[384,384]{1,0:T(8,128)(2,1)S(1)}, u32[]{:S(2)}, u32[]{:S(2)}) collective-permute-start(bf16[384,384]{1,0:T(8,128)(2,1)S(1)} %slice.65.refs_0_), channel_id=1, source_target_pairs={{0,24},{1,25},{8,0},{9,1},{16,8},{17,9},{24,16},{25,17},{2,26},{3,... | collective-permute-start | bytes 884744 | tf_op jit(solution)/shard_map/ppermute | solution.py:15
  25.9 2.7 %collective-permute-start.7 = (bf16[384,384]{1,0:T(8,128)(2,1)S(1)}, bf16[384,384]{1,0:T(8,128)(2,1)S(1)}, u32[]{:S(2)}, u32[]{:S(2)}) collective-permute-start(bf16[384,384]{1,0:T(8,128)(2,1)S(1)} %slice.65.refs_0_), channel_id=1, source_target_pairs={{0,16},{1,17},{8,24},{9,25},{16,0},{17,1},{24,8},{25,9},{2,18},{3,... | collective-permute-start | bytes 884744 | tf_op jit(solution)/shard_map/ppermute | solution.py:15
  28.6 2.8 %collective-permute-start.8 = (bf16[384,384]{1,0:T(8,128)(2,1)S(1)}, bf16[384,384]{1,0:T(8,128)(2,1)S(1)}, u32[]{:S(2)}, u32[]{:S(2)}) collective-permute-start(bf16[384,384]{1,0:T(8,128)(2,1)S(1)} %slice.65.refs_0_), channel_id=1, source_target_pairs={{0,8},{1,9},{8,16},{9,17},{16,24},{17,25},{24,0},{25,1},{2,10},{3,... | collective-permute-start | bytes 884744 | tf_op jit(solution)/shard_map/ppermute | solution.py:15
  31.4 0.1 slice.60.refs_0_
  31.5 4.3 %collective-permute-start = (bf16[384,640]{1,0:T(8,128)(2,1)S(1)}, bf16[384,640]{1,0:T(8,128)(2,1)S(1)}, u32[]{:S(2)}, u32[]{:S(2)}) collective-permute-start(bf16[384,640]{1,0:T(8,128)(2,1)S(1)} %slice.60.refs_0_), channel_id=1, source_target_pairs={{0,24},{1,25},{8,0},{9,1},{16,8},{17,9},{24,16},{25,17},{2,26},{3,... | collective-permute-start | bytes 1474568 | tf_op jit(solution)/shard_map/ppermute | solution.py:15
  35.8 3.4 %collective-permute-start.1 = (bf16[384,640]{1,0:T(8,128)(2,1)S(1)}, bf16[384,640]{1,0:T(8,128)(2,1)S(1)}, u32[]{:S(2)}, u32[]{:S(2)}) collective-permute-start(bf16[384,640]{1,0:T(8,128)(2,1)S(1)} %slice.60.refs_0_), channel_id=1, source_target_pairs={{0,16},{1,17},{8,24},{9,25},{16,0},{17,1},{24,8},{25,9},{2,18},{3,... | collective-permute-start | bytes 1474568 | tf_op jit(solution)/shard_map/ppermute | solution.py:15
  39.2 0.7 dynamic-slice_bitcast_fusion.1
  40.1 0.1 pad_add_fusion.2.rows_to
  40.2 5.4 %shard_map.46 = (bf16[4,4,96,1536]{3,2,1,0:T(8,128)(2,1)S(1)}, f32[8,128]{1,0:T(8,128)}) custom-call(s32[4]{0:T(128)S(1)} %pad_add_fusion.2.rows_to, bf16[1536,1536]{1,0:T(8,128)(2,1)} %block.1, s32[6,128]{1,0:T(8,128)S(1)} %bitcast.55, s32[48,128]{1,0:T(8,128)S(1)} %bitcast.54), custom_call_target="tpu_custom_call" | custom-call | bytes 9437184 | tf_op jit(solution)/shard_map/pallas_call | solution.py:89
  45.6 0.0 collective-permute-done.6.refs_1_
  45.6 1.9 %collective-permute-start.2 = (bf16[384,640]{1,0:T(8,128)(2,1)S(1)}, bf16[384,640]{1,0:T(8,128)(2,1)S(1)}, u32[]{:S(2)}, u32[]{:S(2)}) collective-permute-start(bf16[384,640]{1,0:T(8,128)(2,1)S(1)} %slice.60.refs_0_), channel_id=1, source_target_pairs={{0,8},{1,9},{8,16},{9,17},{16,24},{17,25},{24,0},{25,1},{2,10},{3,... | collective-permute-start | bytes 1474568 | tf_op jit(solution)/shard_map/ppermute | solution.py:15
  47.6 0.1 pad_add_fusion.1.order
  47.6 0.0 collective-permute-done.7.refs_2_
  47.6 0.0 collective-permute-done.8.refs_3_
  47.6 3.8 %shard_map.48 = bf16[4,384,384]{2,1,0:T(8,128)(2,1)S(1)} custom-call(s32[4]{0:T(128)S(1)} %pad_add_fusion.1.order, bf16[1536,1536]{1,0:T(8,128)(2,1)S(1)} %bitcast.52, bf16[384,384]{1,0:T(8,128)(2,1)S(1)} %slice.65.refs_0_, bf16[384,384]{1,0:T(8,128)(2,1)S(1)} %collective-permute-done.6.refs_1_, bf16[384,384]{1,0:T(8,128)(2,1)S(1)} %collective-permute-done.7.refs_2_, ...), custom_call_target="tpu_custom_call" | custom-call | flops 1811939328 | bytes 4718592 | tf_op jit(solution)/shard_map/pallas_call | solution.py:131
  51.5 0.1 slice_bitcast_fusion.6
  51.6 3.4 %collective-permute-start.10 = (bf16[384,384]{1,0:T(8,128)(2,1)S(1)}, bf16[384,384]{1,0:T(8,128)(2,1)S(1)}, u32[]{:S(2)}, u32[]{:S(2)}) collective-permute-start(bf16[384,384]{1,0:T(8,128)(2,1)S(1)} %get-tuple-element.25), channel_id=1, source_target_pairs={{0,32},{1,33},{32,64},{33,65},{64,96},{65,97},{96,0},{97,1},{2,34}... | collective-permute-start | bytes 884744 | tf_op jit(solution)/shard_map/ppermute | solution.py:15
  54.9 2.5 %collective-permute-start.11 = (bf16[384,384]{1,0:T(8,128)(2,1)S(1)}, bf16[384,384]{1,0:T(8,128)(2,1)S(1)}, u32[]{:S(2)}, u32[]{:S(2)}) collective-permute-start(bf16[384,384]{1,0:T(8,128)(2,1)S(1)} %get-tuple-element.24), channel_id=1, source_target_pairs={{0,96},{1,97},{32,0},{33,1},{64,32},{65,33},{96,64},{97,65},{2,98}... | collective-permute-start | bytes 884744 | tf_op jit(solution)/shard_map/ppermute | solution.py:15
  57.4 0.0 collective-permute-done.refs_1_
  57.4 3.1 %collective-permute-start.9 = (bf16[384,384]{1,0:T(8,128)(2,1)S(1)}, bf16[384,384]{1,0:T(8,128)(2,1)S(1)}, u32[]{:S(2)}, u32[]{:S(2)}) collective-permute-start(bf16[384,384]{1,0:T(8,128)(2,1)S(1)} %get-tuple-element.23), channel_id=1, source_target_pairs={{0,64},{1,65},{32,96},{33,97},{64,0},{65,1},{96,32},{97,33},{2,66}... | collective-permute-start | bytes 884744 | tf_op jit(solution)/shard_map/ppermute | solution.py:15
  60.6 0.0 collective-permute-done.1.refs_2_
  60.6 1.9 %collective-permute-done.2.refs_3_ = bf16[384,640]{1,0:T(8,128)(2,1)S(1)} collective-permute-done((bf16[384,640]{1,0:T(8,128)(2,1)S(1)}, bf16[384,640]{1,0:T(8,128)(2,1)S(1)}, u32[]{:S(2)}, u32[]{:S(2)}) %collective-permute-start.2) | collective-permute-done | bytes 491552 | tf_op jit(solution)/shard_map/ppermute | solution.py:15
  62.5 5.1 %shard_map.47 = bf16[4,384,640]{2,1,0:T(8,128)(2,1)S(1)} custom-call(s32[4]{0:T(128)S(1)} %pad_add_fusion.1.order, bf16[1536,1536]{1,0:T(8,128)(2,1)S(1)} %bitcast.53, bf16[384,640]{1,0:T(8,128)(2,1)S(1)} %slice.60.refs_0_, bf16[384,640]{1,0:T(8,128)(2,1)S(1)} %collective-permute-done.refs_1_, bf16[384,640]{1,0:T(8,128)(2,1)S(1)} %collective-permute-done.1.refs_2_, ...), custom_call_target="tpu_custom_call" | custom-call | flops 3019898880 | bytes 4718592 | tf_op jit(solution)/shard_map/pallas_call | solution.py:131
  67.7 0.2 slice_bitcast_fusion
  67.8 3.1 %collective-permute-start.3 = (bf16[384,640]{1,0:T(8,128)(2,1)S(1)}, bf16[384,640]{1,0:T(8,128)(2,1)S(1)}, u32[]{:S(2)}, u32[]{:S(2)}) collective-permute-start(bf16[384,640]{1,0:T(8,128)(2,1)S(1)} %get-tuple-element.21), channel_id=1, source_target_pairs={{0,64},{1,65},{32,96},{33,97},{64,0},{65,1},{96,32},{97,33},{2,66}... | collective-permute-start | bytes 1474568 | tf_op jit(solution)/shard_map/ppermute | solution.py:15
  71.0 4.1 %collective-permute-start.4 = (bf16[384,640]{1,0:T(8,128)(2,1)S(1)}, bf16[384,640]{1,0:T(8,128)(2,1)S(1)}, u32[]{:S(2)}, u32[]{:S(2)}) collective-permute-start(bf16[384,640]{1,0:T(8,128)(2,1)S(1)} %get-tuple-element.20), channel_id=1, source_target_pairs={{0,32},{1,33},{32,64},{33,65},{64,96},{65,97},{96,0},{97,1},{2,34}... | collective-permute-start | bytes 1474568 | tf_op jit(solution)/shard_map/ppermute | solution.py:15
  75.1 0.0 collective-permute-done.10
  75.1 1.9 %collective-permute-start.5 = (bf16[384,640]{1,0:T(8,128)(2,1)S(1)}, bf16[384,640]{1,0:T(8,128)(2,1)S(1)}, u32[]{:S(2)}, u32[]{:S(2)}) collective-permute-start(bf16[384,640]{1,0:T(8,128)(2,1)S(1)} %get-tuple-element.19), channel_id=1, source_target_pairs={{0,96},{1,97},{32,0},{33,1},{64,32},{65,33},{96,64},{97,65},{2,98}... | collective-permute-start | bytes 1474568 | tf_op jit(solution)/shard_map/ppermute | solution.py:15
  77.0 0.0 collective-permute-done.11
  77.0 0.0 collective-permute-done.9
  77.1 0.2 fusion.2
  77.3 9.1 %collective-permute-start.12 = (bf16[96,384]{1,0:T(8,128)(2,1)S(1)}, bf16[96,384]{1,0:T(8,128)(2,1)S(1)}, u32[]{:S(2)}, u32[]{:S(2)}) collective-permute-start(bf16[96,384]{1,0:T(8,128)(2,1)S(1)} %bitcast.60), channel_id=1, source_target_pairs={{0,128},{1,385},{128,256},{129,1},{256,384},{257,129},{384,0},{385... | collective-permute-start | bytes 221192 | tf_op jit(solution)/shard_map/ppermute | solution.py:15
  86.4 0.1 pad_maximum_fusion
  86.4 3.3 %collective-permute-done.12 = bf16[96,384]{1,0:T(8,128)(2,1)S(1)} collective-permute-done((bf16[96,384]{1,0:T(8,128)(2,1)S(1)}, bf16[96,384]{1,0:T(8,128)(2,1)S(1)}, u32[]{:S(2)}, u32[]{:S(2)}) %collective-permute-start.12) | collective-permute-done | bytes 73760 | tf_op jit(solution)/shard_map/ppermute | solution.py:15
  89.7 0.0 collective-permute-done.3
  89.7 0.8 collective-permute-done.4
  90.6 2.4 %collective-permute-done.5 = bf16[384,640]{1,0:T(8,128)(2,1)S(1)} collective-permute-done((bf16[384,640]{1,0:T(8,128)(2,1)S(1)}, bf16[384,640]{1,0:T(8,128)(2,1)S(1)}, u32[]{:S(2)}, u32[]{:S(2)}) %collective-permute-start.5) | collective-permute-done | bytes 491552 | tf_op jit(solution)/shard_map/ppermute | solution.py:15
  93.0 0.2 add_convert_fusion
  93.4 9.1 %collective-permute-start.15 = (bf16[2,96,640]{2,1,0:T(8,128)(2,1)S(1)}, bf16[2,96,640]{2,1,0:T(8,128)(2,1)S(1)}, u32[]{:S(2)}, u32[]{:S(2)}) collective-permute-start(bf16[2,96,640]{2,1,0:T(8,128)(2,1)S(1)} %pad_maximum_fusion.1), channel_id=1, source_target_pairs={{0,128},{1,385},{128,0},{129,257},{256,384},{257,129},{384,256},{3... | collective-permute-start | bytes 737288 | tf_op jit(solution)/shard_map/ppermute | solution.py:15
  102.5 1.9 %collective-permute-start.13 = (bf16[96,384]{1,0:T(8,128)(2,1)S(1)}, bf16[96,384]{1,0:T(8,128)(2,1)S(1)}, u32[]{:S(2)}, u32[]{:S(2)}) collective-permute-start(bf16[96,384]{1,0:T(8,128)(2,1)S(1)} %get-tuple-element.28), channel_id=1, source_target_pairs={{0,128},{1,129},{128,256},{129,257},{256,384},{257,385},{384,0},{3... | collective-permute-start | bytes 221192 | tf_op jit(solution)/shard_map/ppermute | solution.py:15
  104.5 7.8 %collective-permute-start.14 = (bf16[96,384]{1,0:T(8,128)(2,1)S(1)}, bf16[96,384]{1,0:T(8,128)(2,1)S(1)}, u32[]{:S(2)}, u32[]{:S(2)}) collective-permute-start(bf16[96,384]{1,0:T(8,128)(2,1)S(1)} %get-tuple-element.29), channel_id=1, source_target_pairs={{0,384},{1,385},{128,0},{129,1},{256,128},{257,129},{384,256},{385... | collective-permute-start | bytes 221192 | tf_op jit(solution)/shard_map/ppermute | solution.py:15
  112.3 6.7 %collective-permute-done.15 = bf16[2,96,640]{2,1,0:T(8,128)(2,1)S(1)} collective-permute-done((bf16[2,96,640]{2,1,0:T(8,128)(2,1)S(1)}, bf16[2,96,640]{2,1,0:T(8,128)(2,1)S(1)}, u32[]{:S(2)}, u32[]{:S(2)}) %collective-permute-start.15) | collective-permute-done | bytes 245792 | tf_op jit(solution)/shard_map/ppermute | solution.py:15
  119.0 2.9 %collective-permute-start.16 = (bf16[96,640]{1,0:T(8,128)(2,1)S(1)}, bf16[96,640]{1,0:T(8,128)(2,1)S(1)}, u32[]{:S(2)}, u32[]{:S(2)}) collective-permute-start(bf16[96,640]{1,0:T(8,128)(2,1)S(1)} %fusion.8), channel_id=1, source_target_pairs={{0,384},{1,129},{128,256},{129,1},{256,128},{257,385},{384,0},{385... | collective-permute-start | bytes 368648 | tf_op jit(solution)/shard_map/ppermute | solution.py:15
  121.9 0.0 collective-permute-done.13
  121.9 0.0 collective-permute-done.14
  121.9 11.5 %collective-permute-done.16 = bf16[96,640]{1,0:T(8,128)(2,1)S(1)} collective-permute-done((bf16[96,640]{1,0:T(8,128)(2,1)S(1)}, bf16[96,640]{1,0:T(8,128)(2,1)S(1)}, u32[]{:S(2)}, u32[]{:S(2)}) %collective-permute-start.16) | collective-permute-done | bytes 122912 | tf_op jit(solution)/shard_map/ppermute | solution.py:15
  133.5 0.7 pad_maximum_fusion.2
  (13 shorter events, 0.4 us)
Async XLA Ops:
  0.0 40.2 %copy-start = (s32[768]{0:T(1024)S(1)}, s32[768]{0:T(1024)}, u32[]{:S(2)}) copy-start(s32[768]{0:T(1024)} %param.6) | copy-start | bytes 9220
  21.2 24.4 %collective-permute-start.6 = (bf16[384,384]{1,0:T(8,128)(2,1)S(1)}, bf16[384,384]{1,0:T(8,128)(2,1)S(1)}, u32[]{:S(2)}, u32[]{:S(2)}) collective-permute-start(bf16[384,384]{1,0:T(8,128)(2,1)S(1)} %slice.65.refs_0_), channel_id=1, source_target_pairs={{0,24},{1,25},{8,0},{9,1},{16,8},{17,9},{24,16},{25,17},{2,26},{3,... | collective-permute-start | bytes 884744 | tf_op jit(solution)/shard_map/ppermute | solution.py:15
  25.9 21.7 %collective-permute-start.7 = (bf16[384,384]{1,0:T(8,128)(2,1)S(1)}, bf16[384,384]{1,0:T(8,128)(2,1)S(1)}, u32[]{:S(2)}, u32[]{:S(2)}) collective-permute-start(bf16[384,384]{1,0:T(8,128)(2,1)S(1)} %slice.65.refs_0_), channel_id=1, source_target_pairs={{0,16},{1,17},{8,24},{9,25},{16,0},{17,1},{24,8},{25,9},{2,18},{3,... | collective-permute-start | bytes 884744 | tf_op jit(solution)/shard_map/ppermute | solution.py:15
  28.6 19.0 %collective-permute-start.8 = (bf16[384,384]{1,0:T(8,128)(2,1)S(1)}, bf16[384,384]{1,0:T(8,128)(2,1)S(1)}, u32[]{:S(2)}, u32[]{:S(2)}) collective-permute-start(bf16[384,384]{1,0:T(8,128)(2,1)S(1)} %slice.65.refs_0_), channel_id=1, source_target_pairs={{0,8},{1,9},{8,16},{9,17},{16,24},{17,25},{24,0},{25,1},{2,10},{3,... | collective-permute-start | bytes 884744 | tf_op jit(solution)/shard_map/ppermute | solution.py:15
  31.5 25.9 %collective-permute-start = (bf16[384,640]{1,0:T(8,128)(2,1)S(1)}, bf16[384,640]{1,0:T(8,128)(2,1)S(1)}, u32[]{:S(2)}, u32[]{:S(2)}) collective-permute-start(bf16[384,640]{1,0:T(8,128)(2,1)S(1)} %slice.60.refs_0_), channel_id=1, source_target_pairs={{0,24},{1,25},{8,0},{9,1},{16,8},{17,9},{24,16},{25,17},{2,26},{3,... | collective-permute-start | bytes 1474568 | tf_op jit(solution)/shard_map/ppermute | solution.py:15
  35.8 24.8 %collective-permute-start.1 = (bf16[384,640]{1,0:T(8,128)(2,1)S(1)}, bf16[384,640]{1,0:T(8,128)(2,1)S(1)}, u32[]{:S(2)}, u32[]{:S(2)}) collective-permute-start(bf16[384,640]{1,0:T(8,128)(2,1)S(1)} %slice.60.refs_0_), channel_id=1, source_target_pairs={{0,16},{1,17},{8,24},{9,25},{16,0},{17,1},{24,8},{25,9},{2,18},{3,... | collective-permute-start | bytes 1474568 | tf_op jit(solution)/shard_map/ppermute | solution.py:15
  45.6 16.9 %collective-permute-start.2 = (bf16[384,640]{1,0:T(8,128)(2,1)S(1)}, bf16[384,640]{1,0:T(8,128)(2,1)S(1)}, u32[]{:S(2)}, u32[]{:S(2)}) collective-permute-start(bf16[384,640]{1,0:T(8,128)(2,1)S(1)} %slice.60.refs_0_), channel_id=1, source_target_pairs={{0,8},{1,9},{8,16},{9,17},{16,24},{17,25},{24,0},{25,1},{2,10},{3,... | collective-permute-start | bytes 1474568 | tf_op jit(solution)/shard_map/ppermute | solution.py:15
  51.6 23.5 %collective-permute-start.10 = (bf16[384,384]{1,0:T(8,128)(2,1)S(1)}, bf16[384,384]{1,0:T(8,128)(2,1)S(1)}, u32[]{:S(2)}, u32[]{:S(2)}) collective-permute-start(bf16[384,384]{1,0:T(8,128)(2,1)S(1)} %get-tuple-element.25), channel_id=1, source_target_pairs={{0,32},{1,33},{32,64},{33,65},{64,96},{65,97},{96,0},{97,1},{2,34}... | collective-permute-start | bytes 884744 | tf_op jit(solution)/shard_map/ppermute | solution.py:15
  54.9 22.1 %collective-permute-start.11 = (bf16[384,384]{1,0:T(8,128)(2,1)S(1)}, bf16[384,384]{1,0:T(8,128)(2,1)S(1)}, u32[]{:S(2)}, u32[]{:S(2)}) collective-permute-start(bf16[384,384]{1,0:T(8,128)(2,1)S(1)} %get-tuple-element.24), channel_id=1, source_target_pairs={{0,96},{1,97},{32,0},{33,1},{64,32},{65,33},{96,64},{97,65},{2,98}... | collective-permute-start | bytes 884744 | tf_op jit(solution)/shard_map/ppermute | solution.py:15
  57.4 19.6 %collective-permute-start.9 = (bf16[384,384]{1,0:T(8,128)(2,1)S(1)}, bf16[384,384]{1,0:T(8,128)(2,1)S(1)}, u32[]{:S(2)}, u32[]{:S(2)}) collective-permute-start(bf16[384,384]{1,0:T(8,128)(2,1)S(1)} %get-tuple-element.23), channel_id=1, source_target_pairs={{0,64},{1,65},{32,96},{33,97},{64,0},{65,1},{96,32},{97,33},{2,66}... | collective-permute-start | bytes 884744 | tf_op jit(solution)/shard_map/ppermute | solution.py:15
  67.8 21.9 %collective-permute-start.3 = (bf16[384,640]{1,0:T(8,128)(2,1)S(1)}, bf16[384,640]{1,0:T(8,128)(2,1)S(1)}, u32[]{:S(2)}, u32[]{:S(2)}) collective-permute-start(bf16[384,640]{1,0:T(8,128)(2,1)S(1)} %get-tuple-element.21), channel_id=1, source_target_pairs={{0,64},{1,65},{32,96},{33,97},{64,0},{65,1},{96,32},{97,33},{2,66}... | collective-permute-start | bytes 1474568 | tf_op jit(solution)/shard_map/ppermute | solution.py:15
  71.0 19.6 %collective-permute-start.4 = (bf16[384,640]{1,0:T(8,128)(2,1)S(1)}, bf16[384,640]{1,0:T(8,128)(2,1)S(1)}, u32[]{:S(2)}, u32[]{:S(2)}) collective-permute-start(bf16[384,640]{1,0:T(8,128)(2,1)S(1)} %get-tuple-element.20), channel_id=1, source_target_pairs={{0,32},{1,33},{32,64},{33,65},{64,96},{65,97},{96,0},{97,1},{2,34}... | collective-permute-start | bytes 1474568 | tf_op jit(solution)/shard_map/ppermute | solution.py:15
  75.1 17.9 %collective-permute-start.5 = (bf16[384,640]{1,0:T(8,128)(2,1)S(1)}, bf16[384,640]{1,0:T(8,128)(2,1)S(1)}, u32[]{:S(2)}, u32[]{:S(2)}) collective-permute-start(bf16[384,640]{1,0:T(8,128)(2,1)S(1)} %get-tuple-element.19), channel_id=1, source_target_pairs={{0,96},{1,97},{32,0},{33,1},{64,32},{65,33},{96,64},{97,65},{2,98}... | collective-permute-start | bytes 1474568 | tf_op jit(solution)/shard_map/ppermute | solution.py:15
  77.3 12.5 %collective-permute-start.12 = (bf16[96,384]{1,0:T(8,128)(2,1)S(1)}, bf16[96,384]{1,0:T(8,128)(2,1)S(1)}, u32[]{:S(2)}, u32[]{:S(2)}) collective-permute-start(bf16[96,384]{1,0:T(8,128)(2,1)S(1)} %bitcast.60), channel_id=1, source_target_pairs={{0,128},{1,385},{128,256},{129,1},{256,384},{257,129},{384,0},{385... | collective-permute-start | bytes 221192 | tf_op jit(solution)/shard_map/ppermute | solution.py:15
  93.4 25.6 %collective-permute-start.15 = (bf16[2,96,640]{2,1,0:T(8,128)(2,1)S(1)}, bf16[2,96,640]{2,1,0:T(8,128)(2,1)S(1)}, u32[]{:S(2)}, u32[]{:S(2)}) collective-permute-start(bf16[2,96,640]{2,1,0:T(8,128)(2,1)S(1)} %pad_maximum_fusion.1), channel_id=1, source_target_pairs={{0,128},{1,385},{128,0},{129,257},{256,384},{257,129},{384,256},{3... | collective-permute-start | bytes 737288 | tf_op jit(solution)/shard_map/ppermute | solution.py:15
  102.5 19.3 %collective-permute-start.13 = (bf16[96,384]{1,0:T(8,128)(2,1)S(1)}, bf16[96,384]{1,0:T(8,128)(2,1)S(1)}, u32[]{:S(2)}, u32[]{:S(2)}) collective-permute-start(bf16[96,384]{1,0:T(8,128)(2,1)S(1)} %get-tuple-element.28), channel_id=1, source_target_pairs={{0,128},{1,129},{128,256},{129,257},{256,384},{257,385},{384,0},{3... | collective-permute-start | bytes 221192 | tf_op jit(solution)/shard_map/ppermute | solution.py:15
  104.5 17.4 %collective-permute-start.14 = (bf16[96,384]{1,0:T(8,128)(2,1)S(1)}, bf16[96,384]{1,0:T(8,128)(2,1)S(1)}, u32[]{:S(2)}, u32[]{:S(2)}) collective-permute-start(bf16[96,384]{1,0:T(8,128)(2,1)S(1)} %get-tuple-element.29), channel_id=1, source_target_pairs={{0,384},{1,385},{128,0},{129,1},{256,128},{257,129},{384,256},{385... | collective-permute-start | bytes 221192 | tf_op jit(solution)/shard_map/ppermute | solution.py:15
  119.0 14.4 %collective-permute-start.16 = (bf16[96,640]{1,0:T(8,128)(2,1)S(1)}, bf16[96,640]{1,0:T(8,128)(2,1)S(1)}, u32[]{:S(2)}, u32[]{:S(2)}) collective-permute-start(bf16[96,640]{1,0:T(8,128)(2,1)S(1)} %fusion.8), channel_id=1, source_target_pairs={{0,384},{1,129},{128,256},{129,1},{256,128},{257,385},{384,0},{385... | collective-permute-start | bytes 368648 | tf_op jit(solution)/shard_map/ppermute | solution.py:15

commit v4 on v3

--- a/solution.py
+++ b/solution.py
@@ -6,7 +6,7 @@
 from jax.sharding import Mesh, PartitionSpec as P
 
 WIDTHS = (384, 640)
-SCATTER_Z = ("rl", "rh")
+SCATTER_Z = ("rh", "rh")
 VMEM = 32
 
 

time: 135 us -> 134 us (level)
  the two profiles are of different devices: /device:TPU:24 before, /device:TPU:128 now
where the time goes in v4:
time: 134 us; the launch traced here: 133 us
  starting transfers between devices  66.4 us (50%)
  waiting for transfers between devices  28 us (21%)
  blocking collectives  21.2 us (16%)
  Pallas kernels  14.4 us (11%)
  other arithmetic  1.53 us (1%)
    ppermute x16, starting transfers between devices, permute(): return lax.ppermute(block, (axis, 'core'), moves)  66.4 us
    ppermute x16, waiting for transfers between devices, permute(): return lax.ppermute(block, (axis, 'core'), moves)  28 us
    all_gather x1, blocking collectives, body(): near = lax.all_gather(amplitudes, 'zl', axis=0, tiled=True)  21.2 us
    pallas_call x2, Pallas kernels, multiply(): pl.pallas_call(multiply_kernel, grid_spec=pltpu.PrefetchScalarGridSpec(nu...  8.95 us
    pallas_call x1, Pallas kernels, couple(): pl.pallas_call(couple_kernel, grid_spec=pltpu.PrefetchScalarGridSpec(num_...  5.44 us
  transfers between devices with their start and end apart: 16, of which 3 were waited for; matrix products, arithmetic and copies ran while one was open for 1% of the time, Pallas kernels for 11%

profile of v4, /device:TPU:128, one launch (start us, length us, event | category | flops | bytes accessed | tf_op | source)
XLA Modules:
  0.0 133.2 jit_solution(1403335101100970217)
XLA Ops:
  0.0 21.2 %all_gather.3 = bf16[384,1024]{1,0:T(8,128)(2,1)S(1)} all-gather(bf16[96,1024]{1,0:T(8,128)(2,1)} %param.4), channel_id=1, replica_groups=mesh['zh'=4,'y'=4,'x'=4,'zl'=4,'core'=2] {'zl'}, dimensions={0}, use_global_device_ids=true | all-gather | bytes 983040 | tf_op jit(solution)/shard_map/all_gather | solution.py:156
  21.2 4.7 %collective-permute-start.6 = (bf16[384,384]{1,0:T(8,128)(2,1)S(1)}, bf16[384,384]{1,0:T(8,128)(2,1)S(1)}, u32[]{:S(2)}, u32[]{:S(2)}) collective-permute-start(bf16[384,384]{1,0:T(8,128)(2,1)S(1)} %slice.71.refs_0_), channel_id=1, source_target_pairs={{0,24},{1,25},{8,0},{9,1},{16,8},{17,9},{24,16},{25,17},{2,26},{3,... | collective-permute-start | bytes 884744 | tf_op jit(solution)/shard_map/ppermute | solution.py:15
  25.9 2.7 %collective-permute-start.7 = (bf16[384,384]{1,0:T(8,128)(2,1)S(1)}, bf16[384,384]{1,0:T(8,128)(2,1)S(1)}, u32[]{:S(2)}, u32[]{:S(2)}) collective-permute-start(bf16[384,384]{1,0:T(8,128)(2,1)S(1)} %slice.71.refs_0_), channel_id=1, source_target_pairs={{0,16},{1,17},{8,24},{9,25},{16,0},{17,1},{24,8},{25,9},{2,18},{3,... | collective-permute-start | bytes 884744 | tf_op jit(solution)/shard_map/ppermute | solution.py:15
  28.6 2.8 %collective-permute-start.8 = (bf16[384,384]{1,0:T(8,128)(2,1)S(1)}, bf16[384,384]{1,0:T(8,128)(2,1)S(1)}, u32[]{:S(2)}, u32[]{:S(2)}) collective-permute-start(bf16[384,384]{1,0:T(8,128)(2,1)S(1)} %slice.71.refs_0_), channel_id=1, source_target_pairs={{0,8},{1,9},{8,16},{9,17},{16,24},{17,25},{24,0},{25,1},{2,10},{3,... | collective-permute-start | bytes 884744 | tf_op jit(solution)/shard_map/ppermute | solution.py:15
  31.4 0.1 slice.66.refs_0_
  31.5 4.3 %collective-permute-start = (bf16[384,640]{1,0:T(8,128)(2,1)S(1)}, bf16[384,640]{1,0:T(8,128)(2,1)S(1)}, u32[]{:S(2)}, u32[]{:S(2)}) collective-permute-start(bf16[384,640]{1,0:T(8,128)(2,1)S(1)} %slice.66.refs_0_), channel_id=1, source_target_pairs={{0,24},{1,25},{8,0},{9,1},{16,8},{17,9},{24,16},{25,17},{2,26},{3,... | collective-permute-start | bytes 1474568 | tf_op jit(solution)/shard_map/ppermute | solution.py:15
  35.8 3.4 %collective-permute-start.1 = (bf16[384,640]{1,0:T(8,128)(2,1)S(1)}, bf16[384,640]{1,0:T(8,128)(2,1)S(1)}, u32[]{:S(2)}, u32[]{:S(2)}) collective-permute-start(bf16[384,640]{1,0:T(8,128)(2,1)S(1)} %slice.66.refs_0_), channel_id=1, source_target_pairs={{0,16},{1,17},{8,24},{9,25},{16,0},{17,1},{24,8},{25,9},{2,18},{3,... | collective-permute-start | bytes 1474568 | tf_op jit(solution)/shard_map/ppermute | solution.py:15
  39.2 0.7 dynamic-slice_bitcast_fusion.1
  40.1 0.1 pad_add_fusion.2.rows_to
  40.2 0.0 copy-done
  40.2 5.4 %shard_map.46 = (bf16[4,4,96,1536]{3,2,1,0:T(8,128)(2,1)S(1)}, f32[8,128]{1,0:T(8,128)}) custom-call(s32[4]{0:T(128)S(1)} %pad_add_fusion.2.rows_to, bf16[1536,1536]{1,0:T(8,128)(2,1)} %block.1, s32[6,128]{1,0:T(8,128)S(1)} %bitcast.51, s32[48,128]{1,0:T(8,128)S(1)} %bitcast.50), custom_call_target="tpu_custom_call" | custom-call | bytes 9437184 | tf_op jit(solution)/shard_map/pallas_call | solution.py:89
  45.6 0.0 collective-permute-done.6.refs_1_
  45.6 1.9 %collective-permute-start.2 = (bf16[384,640]{1,0:T(8,128)(2,1)S(1)}, bf16[384,640]{1,0:T(8,128)(2,1)S(1)}, u32[]{:S(2)}, u32[]{:S(2)}) collective-permute-start(bf16[384,640]{1,0:T(8,128)(2,1)S(1)} %slice.66.refs_0_), channel_id=1, source_target_pairs={{0,8},{1,9},{8,16},{9,17},{16,24},{17,25},{24,0},{25,1},{2,10},{3,... | collective-permute-start | bytes 1474568 | tf_op jit(solution)/shard_map/ppermute | solution.py:15
  47.5 0.1 pad_add_fusion.1.order
  47.6 0.0 collective-permute-done.7.refs_2_
  47.6 0.0 collective-permute-done.8.refs_3_
  47.6 3.8 %shard_map.48 = bf16[4,384,384]{2,1,0:T(8,128)(2,1)S(1)} custom-call(s32[4]{0:T(128)S(1)} %pad_add_fusion.1.order, bf16[1536,1536]{1,0:T(8,128)(2,1)S(1)} %bitcast.48, bf16[384,384]{1,0:T(8,128)(2,1)S(1)} %slice.71.refs_0_, bf16[384,384]{1,0:T(8,128)(2,1)S(1)} %collective-permute-done.6.refs_1_, bf16[384,384]{1,0:T(8,128)(2,1)S(1)} %collective-permute-done.7.refs_2_, ...), custom_call_target="tpu_custom_call" | custom-call | flops 1811939328 | bytes 4718592 | tf_op jit(solution)/shard_map/pallas_call | solution.py:131
  51.5 0.1 slice_bitcast_fusion.6
  51.6 3.5 %collective-permute-start.10 = (bf16[384,384]{1,0:T(8,128)(2,1)S(1)}, bf16[384,384]{1,0:T(8,128)(2,1)S(1)}, u32[]{:S(2)}, u32[]{:S(2)}) collective-permute-start(bf16[384,384]{1,0:T(8,128)(2,1)S(1)} %get-tuple-element.25), channel_id=1, source_target_pairs={{0,32},{1,33},{32,64},{33,65},{64,96},{65,97},{96,0},{97,1},{2,34}... | collective-permute-start | bytes 884744 | tf_op jit(solution)/shard_map/ppermute | solution.py:15
  55.0 3.6 %collective-permute-start.11 = (bf16[384,384]{1,0:T(8,128)(2,1)S(1)}, bf16[384,384]{1,0:T(8,128)(2,1)S(1)}, u32[]{:S(2)}, u32[]{:S(2)}) collective-permute-start(bf16[384,384]{1,0:T(8,128)(2,1)S(1)} %get-tuple-element.24), channel_id=1, source_target_pairs={{0,96},{1,97},{32,0},{33,1},{64,32},{65,33},{96,64},{97,65},{2,98}... | collective-permute-start | bytes 884744 | tf_op jit(solution)/shard_map/ppermute | solution.py:15
  58.6 0.0 collective-permute-done.refs_1_
  58.6 3.9 %collective-permute-start.9 = (bf16[384,384]{1,0:T(8,128)(2,1)S(1)}, bf16[384,384]{1,0:T(8,128)(2,1)S(1)}, u32[]{:S(2)}, u32[]{:S(2)}) collective-permute-start(bf16[384,384]{1,0:T(8,128)(2,1)S(1)} %get-tuple-element.23), channel_id=1, source_target_pairs={{0,64},{1,65},{32,96},{33,97},{64,0},{65,1},{96,32},{97,33},{2,66}... | collective-permute-start | bytes 884744 | tf_op jit(solution)/shard_map/ppermute | solution.py:15
  62.5 0.0 collective-permute-done.1.refs_2_
  62.5 0.0 collective-permute-done.2.refs_3_
  62.6 5.1 %shard_map.47 = bf16[4,384,640]{2,1,0:T(8,128)(2,1)S(1)} custom-call(s32[4]{0:T(128)S(1)} %pad_add_fusion.1.order, bf16[1536,1536]{1,0:T(8,128)(2,1)S(1)} %bitcast.49, bf16[384,640]{1,0:T(8,128)(2,1)S(1)} %slice.66.refs_0_, bf16[384,640]{1,0:T(8,128)(2,1)S(1)} %collective-permute-done.refs_1_, bf16[384,640]{1,0:T(8,128)(2,1)S(1)} %collective-permute-done.1.refs_2_, ...), custom_call_target="tpu_custom_call" | custom-call | flops 3019898880 | bytes 4718592 | tf_op jit(solution)/shard_map/pallas_call | solution.py:131
  67.7 0.2 slice_bitcast_fusion
  67.9 5.1 %collective-permute-start.3 = (bf16[384,640]{1,0:T(8,128)(2,1)S(1)}, bf16[384,640]{1,0:T(8,128)(2,1)S(1)}, u32[]{:S(2)}, u32[]{:S(2)}) collective-permute-start(bf16[384,640]{1,0:T(8,128)(2,1)S(1)} %get-tuple-element.21), channel_id=1, source_target_pairs={{0,64},{1,65},{32,96},{33,97},{64,0},{65,1},{96,32},{97,33},{2,66}... | collective-permute-start | bytes 1474568 | tf_op jit(solution)/shard_map/ppermute | solution.py:15
  73.0 2.6 %collective-permute-start.4 = (bf16[384,640]{1,0:T(8,128)(2,1)S(1)}, bf16[384,640]{1,0:T(8,128)(2,1)S(1)}, u32[]{:S(2)}, u32[]{:S(2)}) collective-permute-start(bf16[384,640]{1,0:T(8,128)(2,1)S(1)} %get-tuple-element.20), channel_id=1, source_target_pairs={{0,32},{1,33},{32,64},{33,65},{64,96},{65,97},{96,0},{97,1},{2,34}... | collective-permute-start | bytes 1474568 | tf_op jit(solution)/shard_map/ppermute | solution.py:15
  75.6 0.0 collective-permute-done.10
  75.6 4.5 %collective-permute-start.5 = (bf16[384,640]{1,0:T(8,128)(2,1)S(1)}, bf16[384,640]{1,0:T(8,128)(2,1)S(1)}, u32[]{:S(2)}, u32[]{:S(2)}) collective-permute-start(bf16[384,640]{1,0:T(8,128)(2,1)S(1)} %get-tuple-element.19), channel_id=1, source_target_pairs={{0,96},{1,97},{32,0},{33,1},{64,32},{65,33},{96,64},{97,65},{2,98}... | collective-permute-start | bytes 1474568 | tf_op jit(solution)/shard_map/ppermute | solution.py:15
  80.0 0.0 collective-permute-done.11
  80.0 0.0 collective-permute-done.9
  80.1 0.2 fusion.2
  80.2 0.1 constant_dynamic-slice_fusion.5
  80.3 1.9 %collective-permute-start.12 = (bf16[2,96,384]{2,1,0:T(8,128)(2,1)S(1)}, bf16[2,96,384]{2,1,0:T(8,128)(2,1)S(1)}, u32[]{:S(2)}, u32[]{:S(2)}) collective-permute-start(bf16[2,96,384]{2,1,0:T(8,128)(2,1)S(1)} %pad_maximum_fusion.3), channel_id=1, source_target_pairs={{0,128},{1,385},{128,0},{129,257},{256,384},{257,129},{384,256},{3... | collective-permute-start | bytes 442376 | tf_op jit(solution)/shard_map/ppermute | solution.py:15
  82.3 11.7 %collective-permute-done.12 = bf16[2,96,384]{2,1,0:T(8,128)(2,1)S(1)} collective-permute-done((bf16[2,96,384]{2,1,0:T(8,128)(2,1)S(1)}, bf16[2,96,384]{2,1,0:T(8,128)(2,1)S(1)}, u32[]{:S(2)}, u32[]{:S(2)}) %collective-permute-start.12) | collective-permute-done | bytes 147488 | tf_op jit(solution)/shard_map/ppermute | solution.py:15
  93.9 0.0 collective-permute-done.3
  94.0 0.0 collective-permute-done.4
  94.0 0.0 collective-permute-done.5
  94.0 0.3 add_convert_fusion
  94.3 2.5 %collective-permute-start.14 = (bf16[2,96,640]{2,1,0:T(8,128)(2,1)S(1)}, bf16[2,96,640]{2,1,0:T(8,128)(2,1)S(1)}, u32[]{:S(2)}, u32[]{:S(2)}) collective-permute-start(bf16[2,96,640]{2,1,0:T(8,128)(2,1)S(1)} %pad_maximum_fusion.1), channel_id=1, source_target_pairs={{0,128},{1,385},{128,0},{129,257},{256,384},{257,129},{384,256},{3... | collective-permute-start | bytes 737288 | tf_op jit(solution)/shard_map/ppermute | solution.py:15
  96.8 9.2 %collective-permute-start.13 = (bf16[96,384]{1,0:T(8,128)(2,1)S(1)}, bf16[96,384]{1,0:T(8,128)(2,1)S(1)}, u32[]{:S(2)}, u32[]{:S(2)}) collective-permute-start(bf16[96,384]{1,0:T(8,128)(2,1)S(1)} %fusion.6), channel_id=1, source_target_pairs={{0,384},{1,129},{128,256},{129,1},{256,128},{257,385},{384,0},{385... | collective-permute-start | bytes 221192 | tf_op jit(solution)/shard_map/ppermute | solution.py:15
  106.1 10.3 %collective-permute-done.14 = bf16[2,96,640]{2,1,0:T(8,128)(2,1)S(1)} collective-permute-done((bf16[2,96,640]{2,1,0:T(8,128)(2,1)S(1)}, bf16[2,96,640]{2,1,0:T(8,128)(2,1)S(1)}, u32[]{:S(2)}, u32[]{:S(2)}) %collective-permute-start.14) | collective-permute-done | bytes 245792 | tf_op jit(solution)/shard_map/ppermute | solution.py:15
  116.4 10.0 %collective-permute-start.15 = (bf16[96,640]{1,0:T(8,128)(2,1)S(1)}, bf16[96,640]{1,0:T(8,128)(2,1)S(1)}, u32[]{:S(2)}, u32[]{:S(2)}) collective-permute-start(bf16[96,640]{1,0:T(8,128)(2,1)S(1)} %fusion.5), channel_id=1, source_target_pairs={{0,384},{1,129},{128,256},{129,1},{256,128},{257,385},{384,0},{385... | collective-permute-start | bytes 368648 | tf_op jit(solution)/shard_map/ppermute | solution.py:15
  126.4 0.0 collective-permute-done.13
  126.4 6.0 %collective-permute-done.15 = bf16[96,640]{1,0:T(8,128)(2,1)S(1)} collective-permute-done((bf16[96,640]{1,0:T(8,128)(2,1)S(1)}, bf16[96,640]{1,0:T(8,128)(2,1)S(1)}, u32[]{:S(2)}, u32[]{:S(2)}) %collective-permute-start.15) | collective-permute-done | bytes 122912 | tf_op jit(solution)/shard_map/ppermute | solution.py:15
  132.4 0.1 fusion.3
  132.5 0.7 pad_maximum_fusion.2
  (12 shorter events, 0.3 us)
Async XLA Ops:
  0.0 40.2 %copy-start = (s32[768]{0:T(1024)S(1)}, s32[768]{0:T(1024)}, u32[]{:S(2)}) copy-start(s32[768]{0:T(1024)} %param.6) | copy-start | bytes 9220
  21.2 24.4 %collective-permute-start.6 = (bf16[384,384]{1,0:T(8,128)(2,1)S(1)}, bf16[384,384]{1,0:T(8,128)(2,1)S(1)}, u32[]{:S(2)}, u32[]{:S(2)}) collective-permute-start(bf16[384,384]{1,0:T(8,128)(2,1)S(1)} %slice.71.refs_0_), channel_id=1, source_target_pairs={{0,24},{1,25},{8,0},{9,1},{16,8},{17,9},{24,16},{25,17},{2,26},{3,... | collective-permute-start | bytes 884744 | tf_op jit(solution)/shard_map/ppermute | solution.py:15
  25.9 21.7 %collective-permute-start.7 = (bf16[384,384]{1,0:T(8,128)(2,1)S(1)}, bf16[384,384]{1,0:T(8,128)(2,1)S(1)}, u32[]{:S(2)}, u32[]{:S(2)}) collective-permute-start(bf16[384,384]{1,0:T(8,128)(2,1)S(1)} %slice.71.refs_0_), channel_id=1, source_target_pairs={{0,16},{1,17},{8,24},{9,25},{16,0},{17,1},{24,8},{25,9},{2,18},{3,... | collective-permute-start | bytes 884744 | tf_op jit(solution)/shard_map/ppermute | solution.py:15
  28.6 19.0 %collective-permute-start.8 = (bf16[384,384]{1,0:T(8,128)(2,1)S(1)}, bf16[384,384]{1,0:T(8,128)(2,1)S(1)}, u32[]{:S(2)}, u32[]{:S(2)}) collective-permute-start(bf16[384,384]{1,0:T(8,128)(2,1)S(1)} %slice.71.refs_0_), channel_id=1, source_target_pairs={{0,8},{1,9},{8,16},{9,17},{16,24},{17,25},{24,0},{25,1},{2,10},{3,... | collective-permute-start | bytes 884744 | tf_op jit(solution)/shard_map/ppermute | solution.py:15
  31.5 27.1 %collective-permute-start = (bf16[384,640]{1,0:T(8,128)(2,1)S(1)}, bf16[384,640]{1,0:T(8,128)(2,1)S(1)}, u32[]{:S(2)}, u32[]{:S(2)}) collective-permute-start(bf16[384,640]{1,0:T(8,128)(2,1)S(1)} %slice.66.refs_0_), channel_id=1, source_target_pairs={{0,24},{1,25},{8,0},{9,1},{16,8},{17,9},{24,16},{25,17},{2,26},{3,... | collective-permute-start | bytes 1474568 | tf_op jit(solution)/shard_map/ppermute | solution.py:15
  35.8 26.8 %collective-permute-start.1 = (bf16[384,640]{1,0:T(8,128)(2,1)S(1)}, bf16[384,640]{1,0:T(8,128)(2,1)S(1)}, u32[]{:S(2)}, u32[]{:S(2)}) collective-permute-start(bf16[384,640]{1,0:T(8,128)(2,1)S(1)} %slice.66.refs_0_), channel_id=1, source_target_pairs={{0,16},{1,17},{8,24},{9,25},{16,0},{17,1},{24,8},{25,9},{2,18},{3,... | collective-permute-start | bytes 1474568 | tf_op jit(solution)/shard_map/ppermute | solution.py:15
  45.6 16.9 %collective-permute-start.2 = (bf16[384,640]{1,0:T(8,128)(2,1)S(1)}, bf16[384,640]{1,0:T(8,128)(2,1)S(1)}, u32[]{:S(2)}, u32[]{:S(2)}) collective-permute-start(bf16[384,640]{1,0:T(8,128)(2,1)S(1)} %slice.66.refs_0_), channel_id=1, source_target_pairs={{0,8},{1,9},{8,16},{9,17},{16,24},{17,25},{24,0},{25,1},{2,10},{3,... | collective-permute-start | bytes 1474568 | tf_op jit(solution)/shard_map/ppermute | solution.py:15
  51.6 24.0 %collective-permute-start.10 = (bf16[384,384]{1,0:T(8,128)(2,1)S(1)}, bf16[384,384]{1,0:T(8,128)(2,1)S(1)}, u32[]{:S(2)}, u32[]{:S(2)}) collective-permute-start(bf16[384,384]{1,0:T(8,128)(2,1)S(1)} %get-tuple-element.25), channel_id=1, source_target_pairs={{0,32},{1,33},{32,64},{33,65},{64,96},{65,97},{96,0},{97,1},{2,34}... | collective-permute-start | bytes 884744 | tf_op jit(solution)/shard_map/ppermute | solution.py:15
  55.0 25.0 %collective-permute-start.11 = (bf16[384,384]{1,0:T(8,128)(2,1)S(1)}, bf16[384,384]{1,0:T(8,128)(2,1)S(1)}, u32[]{:S(2)}, u32[]{:S(2)}) collective-permute-start(bf16[384,384]{1,0:T(8,128)(2,1)S(1)} %get-tuple-element.24), channel_id=1, source_target_pairs={{0,96},{1,97},{32,0},{33,1},{64,32},{65,33},{96,64},{97,65},{2,98}... | collective-permute-start | bytes 884744 | tf_op jit(solution)/shard_map/ppermute | solution.py:15
  58.6 21.4 %collective-permute-start.9 = (bf16[384,384]{1,0:T(8,128)(2,1)S(1)}, bf16[384,384]{1,0:T(8,128)(2,1)S(1)}, u32[]{:S(2)}, u32[]{:S(2)}) collective-permute-start(bf16[384,384]{1,0:T(8,128)(2,1)S(1)} %get-tuple-element.23), channel_id=1, source_target_pairs={{0,64},{1,65},{32,96},{33,97},{64,0},{65,1},{96,32},{97,33},{2,66}... | collective-permute-start | bytes 884744 | tf_op jit(solution)/shard_map/ppermute | solution.py:15
  67.9 26.1 %collective-permute-start.3 = (bf16[384,640]{1,0:T(8,128)(2,1)S(1)}, bf16[384,640]{1,0:T(8,128)(2,1)S(1)}, u32[]{:S(2)}, u32[]{:S(2)}) collective-permute-start(bf16[384,640]{1,0:T(8,128)(2,1)S(1)} %get-tuple-element.21), channel_id=1, source_target_pairs={{0,64},{1,65},{32,96},{33,97},{64,0},{65,1},{96,32},{97,33},{2,66}... | collective-permute-start | bytes 1474568 | tf_op jit(solution)/shard_map/ppermute | solution.py:15
  73.0 21.0 %collective-permute-start.4 = (bf16[384,640]{1,0:T(8,128)(2,1)S(1)}, bf16[384,640]{1,0:T(8,128)(2,1)S(1)}, u32[]{:S(2)}, u32[]{:S(2)}) collective-permute-start(bf16[384,640]{1,0:T(8,128)(2,1)S(1)} %get-tuple-element.20), channel_id=1, source_target_pairs={{0,32},{1,33},{32,64},{33,65},{64,96},{65,97},{96,0},{97,1},{2,34}... | collective-permute-start | bytes 1474568 | tf_op jit(solution)/shard_map/ppermute | solution.py:15
  75.6 18.4 %collective-permute-start.5 = (bf16[384,640]{1,0:T(8,128)(2,1)S(1)}, bf16[384,640]{1,0:T(8,128)(2,1)S(1)}, u32[]{:S(2)}, u32[]{:S(2)}) collective-permute-start(bf16[384,640]{1,0:T(8,128)(2,1)S(1)} %get-tuple-element.19), channel_id=1, source_target_pairs={{0,96},{1,97},{32,0},{33,1},{64,32},{65,33},{96,64},{97,65},{2,98}... | collective-permute-start | bytes 1474568 | tf_op jit(solution)/shard_map/ppermute | solution.py:15
  80.3 13.6 %collective-permute-start.12 = (bf16[2,96,384]{2,1,0:T(8,128)(2,1)S(1)}, bf16[2,96,384]{2,1,0:T(8,128)(2,1)S(1)}, u32[]{:S(2)}, u32[]{:S(2)}) collective-permute-start(bf16[2,96,384]{2,1,0:T(8,128)(2,1)S(1)} %pad_maximum_fusion.3), channel_id=1, source_target_pairs={{0,128},{1,385},{128,0},{129,257},{256,384},{257,129},{384,256},{3... | collective-permute-start | bytes 442376 | tf_op jit(solution)/shard_map/ppermute | solution.py:15
  94.3 22.1 %collective-permute-start.14 = (bf16[2,96,640]{2,1,0:T(8,128)(2,1)S(1)}, bf16[2,96,640]{2,1,0:T(8,128)(2,1)S(1)}, u32[]{:S(2)}, u32[]{:S(2)}) collective-permute-start(bf16[2,96,640]{2,1,0:T(8,128)(2,1)S(1)} %pad_maximum_fusion.1), channel_id=1, source_target_pairs={{0,128},{1,385},{128,0},{129,257},{256,384},{257,129},{384,256},{3... | collective-permute-start | bytes 737288 | tf_op jit(solution)/shard_map/ppermute | solution.py:15
  96.8 29.6 %collective-permute-start.13 = (bf16[96,384]{1,0:T(8,128)(2,1)S(1)}, bf16[96,384]{1,0:T(8,128)(2,1)S(1)}, u32[]{:S(2)}, u32[]{:S(2)}) collective-permute-start(bf16[96,384]{1,0:T(8,128)(2,1)S(1)} %fusion.6), channel_id=1, source_target_pairs={{0,384},{1,129},{128,256},{129,1},{256,128},{257,385},{384,0},{385... | collective-permute-start | bytes 221192 | tf_op jit(solution)/shard_map/ppermute | solution.py:15
  116.4 16.0 %collective-permute-start.15 = (bf16[96,640]{1,0:T(8,128)(2,1)S(1)}, bf16[96,640]{1,0:T(8,128)(2,1)S(1)}, u32[]{:S(2)}, u32[]{:S(2)}) collective-permute-start(bf16[96,640]{1,0:T(8,128)(2,1)S(1)} %fusion.5), channel_id=1, source_target_pairs={{0,384},{1,129},{128,256},{129,1},{256,128},{257,385},{384,0},{385... | collective-permute-start | bytes 368648 | tf_op jit(solution)/shard_map/ppermute | solution.py:15

commit v5 on v4

--- a/solution.py
+++ b/solution.py
@@ -123,7 +123,7 @@
     out[...] = jnp.dot(coupled[...], whole[...], preferred_element_type=jnp.float32).astype(out.dtype)[None]
 
 
-def multiply(coupled, blocks, order):
+def multiply(coupled, blocks, order, first):
     rows, depth = coupled.shape
     width = blocks[0].shape[1]
     tile = rows // 4
@@ -132,15 +132,15 @@
         multiply_kernel,
         grid_spec=pltpu.PrefetchScalarGridSpec(
             num_scalar_prefetch=1,
-            grid=(4,),
-            in_specs=[pl.BlockSpec((tile, depth), lambda i, s: (i, 0))] + [one] * 4,
+            grid=(2,),
+            in_specs=[pl.BlockSpec((tile, depth), lambda i, s: ((i + first) % 4, 0))] + [one] * 4,
             out_specs=pl.BlockSpec((1, tile, width), lambda i, s: (i, 0, 0)),
             scratch_shapes=[pltpu.VMEM((depth, width), blocks[0].dtype)],
         ),
-        out_shape=jax.ShapeDtypeStruct((4, tile, width), blocks[0].dtype),
+        out_shape=jax.ShapeDtypeStruct((2, tile, width), blocks[0].dtype),
         compiler_params=pltpu.CompilerParams(vmem_limit_bytes=VMEM * 2**20),
         cost_estimate=pl.CostEstimate(
-            flops=2 * rows * depth * width, bytes_accessed=rows * depth * 2, transcendentals=0
+            flops=rows * depth * width, bytes_accessed=rows * depth, transcendentals=0
         ),
     )(as_ints(order), coupled, *blocks)
 
@@ -168,7 +168,10 @@
         if start:
             part, masked = lax.optimization_barrier((part, masked))
         start += width
-        product.append(multiply(coupled, gather(part, "x"), places("dir", x, core)))
+        blocks, order = gather(part, "x"), places("dir", x, core)
+        up, far = multiply(coupled, blocks, order, 1)
+        down, own = multiply(coupled, blocks, order, 3)
+        product.append((own, up, far, down))
 
     done, earlier = [], None
     for part, kind in zip(product, SCATTER_Z):
@@ -176,7 +179,7 @@
         if earlier is not None:
             arrived, held = lax.optimization_barrier((arrived, earlier[1:]))
             earlier = (earlier[0], *held)
-        over_y = finish("dir", *arrived, "y").reshape(4, -1, part.shape[-1])
+        over_y = finish("dir", *arrived, "y").reshape(4, -1, part[0].shape[-1])
         blocks = pieces(over_y, places(kind, zh, core))
         if earlier is not None:
             done.append(finish(*earlier, "zh"))

time: 134 us -> 136 us (1.015)
  the two profiles are of different devices: /device:TPU:128 before, /device:TPU:18 now
where the time goes in v5:
time: 136 us; the launch traced here: 135 us
  starting transfers between devices  63.4 us (47%)
  waiting for transfers between devices  30.8 us (23%)
  blocking collectives  21.1 us (16%)
  Pallas kernels  15.8 us (12%)
  local copies, waits for them, and re-layouts  1.89 us (1%)
  other arithmetic  1.5 us (1%)
    ppermute x16, starting transfers between devices, permute(): return lax.ppermute(block, (axis, 'core'), moves)  63.4 us
    ppermute x16, waiting for transfers between devices, permute(): return lax.ppermute(block, (axis, 'core'), moves)  30.8 us
    all_gather x1, blocking collectives, body(): near = lax.all_gather(amplitudes, 'zl', axis=0, tiled=True)  21.1 us
    pallas_call x4, Pallas kernels, multiply(): pl.pallas_call(multiply_kernel, grid_spec=pltpu.PrefetchScalarGridSpec(nu...  10.4 us
    pallas_call x1, Pallas kernels, couple(): pl.pallas_call(couple_kernel, grid_spec=pltpu.PrefetchScalarGridSpec(num_...  5.44 us
  transfers between devices with their start and end apart: 16, of which 3 were waited for; matrix products, arithmetic and copies ran while one was open for 1% of the time, Pallas kernels for 12%

profile of v5, /device:TPU:18, one launch (start us, length us, event | category | flops | bytes accessed | tf_op | source)
XLA Modules:
  0.0 135.0 jit_solution(6254641317089793403)
XLA Ops:
  0.0 21.1 %all_gather.3 = bf16[384,1024]{1,0:T(8,128)(2,1)S(1)} all-gather(bf16[96,1024]{1,0:T(8,128)(2,1)} %param.4), channel_id=1, replica_groups=mesh['zh'=4,'y'=4,'x'=4,'zl'=4,'core'=2] {'zl'}, dimensions={0}, use_global_device_ids=true | all-gather | bytes 983040 | tf_op jit(solution)/shard_map/all_gather | solution.py:156
  21.1 3.4 %collective-permute-start.8 = (bf16[384,384]{1,0:T(8,128)(2,1)S(1)}, bf16[384,384]{1,0:T(8,128)(2,1)S(1)}, u32[]{:S(2)}, u32[]{:S(2)}) collective-permute-start(bf16[384,384]{1,0:T(8,128)(2,1)S(1)} %slice.35.refs_0_), channel_id=1, source_target_pairs={{0,8},{1,9},{8,16},{9,17},{16,24},{17,25},{24,0},{25,1},{2,10},{3,... | collective-permute-start | bytes 884744 | tf_op jit(solution)/shard_map/ppermute | solution.py:15
  24.5 3.0 %collective-permute-start.7 = (bf16[384,384]{1,0:T(8,128)(2,1)S(1)}, bf16[384,384]{1,0:T(8,128)(2,1)S(1)}, u32[]{:S(2)}, u32[]{:S(2)}) collective-permute-start(bf16[384,384]{1,0:T(8,128)(2,1)S(1)} %slice.35.refs_0_), channel_id=1, source_target_pairs={{0,16},{1,17},{8,24},{9,25},{16,0},{17,1},{24,8},{25,9},{2,18},{3,... | collective-permute-start | bytes 884744 | tf_op jit(solution)/shard_map/ppermute | solution.py:15
  27.5 4.1 %collective-permute-start.6 = (bf16[384,384]{1,0:T(8,128)(2,1)S(1)}, bf16[384,384]{1,0:T(8,128)(2,1)S(1)}, u32[]{:S(2)}, u32[]{:S(2)}) collective-permute-start(bf16[384,384]{1,0:T(8,128)(2,1)S(1)} %slice.35.refs_0_), channel_id=1, source_target_pairs={{0,24},{1,25},{8,0},{9,1},{16,8},{17,9},{24,16},{25,17},{2,26},{3,... | collective-permute-start | bytes 884744 | tf_op jit(solution)/shard_map/ppermute | solution.py:15
  31.6 0.1 slice.34.refs_0_
  31.7 1.9 %collective-permute-start.2 = (bf16[384,640]{1,0:T(8,128)(2,1)S(1)}, bf16[384,640]{1,0:T(8,128)(2,1)S(1)}, u32[]{:S(2)}, u32[]{:S(2)}) collective-permute-start(bf16[384,640]{1,0:T(8,128)(2,1)S(1)} %slice.34.refs_0_), channel_id=1, source_target_pairs={{0,8},{1,9},{8,16},{9,17},{16,24},{17,25},{24,0},{25,1},{2,10},{3,... | collective-permute-start | bytes 1474568 | tf_op jit(solution)/shard_map/ppermute | solution.py:15
  33.6 5.4 %collective-permute-start.1 = (bf16[384,640]{1,0:T(8,128)(2,1)S(1)}, bf16[384,640]{1,0:T(8,128)(2,1)S(1)}, u32[]{:S(2)}, u32[]{:S(2)}) collective-permute-start(bf16[384,640]{1,0:T(8,128)(2,1)S(1)} %slice.34.refs_0_), channel_id=1, source_target_pairs={{0,16},{1,17},{8,24},{9,25},{16,0},{17,1},{24,8},{25,9},{2,18},{3,... | collective-permute-start | bytes 1474568 | tf_op jit(solution)/shard_map/ppermute | solution.py:15
  39.1 0.7 dynamic-slice_bitcast_fusion.1
  40.0 0.1 pad_add_fusion.2.rows_to
  40.1 0.0 copy-start
  40.1 0.7 copy-done
  40.8 5.4 %shard_map.46 = (bf16[4,4,96,1536]{3,2,1,0:T(8,128)(2,1)S(1)}, f32[8,128]{1,0:T(8,128)}) custom-call(s32[4]{0:T(128)S(1)} %pad_add_fusion.2.rows_to, bf16[1536,1536]{1,0:T(8,128)(2,1)} %block.1, s32[6,128]{1,0:T(8,128)S(1)} %bitcast.53, s32[48,128]{1,0:T(8,128)S(1)} %bitcast.52), custom_call_target="tpu_custom_call" | custom-call | bytes 9437184 | tf_op jit(solution)/shard_map/pallas_call | solution.py:89
  46.2 0.1 pad_add_fusion.1.order
  46.3 0.0 collective-permute-done.8.refs_3_
  46.3 1.9 %collective-permute-start = (bf16[384,640]{1,0:T(8,128)(2,1)S(1)}, bf16[384,640]{1,0:T(8,128)(2,1)S(1)}, u32[]{:S(2)}, u32[]{:S(2)}) collective-permute-start(bf16[384,640]{1,0:T(8,128)(2,1)S(1)} %slice.34.refs_0_), channel_id=1, source_target_pairs={{0,24},{1,25},{8,0},{9,1},{16,8},{17,9},{24,16},{25,17},{2,26},{3,... | collective-permute-start | bytes 1474568 | tf_op jit(solution)/shard_map/ppermute | solution.py:15
  48.2 0.0 collective-permute-done.7.refs_2_
  48.2 0.0 collective-permute-done.6.refs_1_
  48.2 2.3 %shard_map.49 = bf16[2,384,384]{2,1,0:T(8,128)(2,1)S(1)} custom-call(s32[4]{0:T(128)S(1)} %pad_add_fusion.1.order, bf16[1536,1536]{1,0:T(8,128)(2,1)S(1)} %bitcast.48, bf16[384,384]{1,0:T(8,128)(2,1)S(1)} %slice.35.refs_0_, bf16[384,384]{1,0:T(8,128)(2,1)S(1)} %collective-permute-done.6.refs_1_, bf16[384,384]{1,0:T(8,128)(2,1)S(1)} %collective-permute-done.7.refs_2_, ...), custom_call_target="tpu_custom_call" | custom-call | flops 905969664 | bytes 2359296 | tf_op jit(solution)/shard_map/pallas_call | solution.py:131
  50.5 2.4 %collective-permute-start.11 = (bf16[384,384]{1,0:T(8,128)(2,1)S(1)}, bf16[384,384]{1,0:T(8,128)(2,1)S(1)}, u32[]{:S(2)}, u32[]{:S(2)}) collective-permute-start(bf16[384,384]{1,0:T(8,128)(2,1)S(1)} %slice_bitcast_fusion.4), channel_id=1, source_target_pairs={{0,96},{1,97},{32,0},{33,1},{64,32},{65,33},{96,64},{97,65},{2,98}... | collective-permute-start | bytes 884744 | tf_op jit(solution)/shard_map/ppermute | solution.py:15
  52.9 2.3 %shard_map.50 = bf16[2,384,384]{2,1,0:T(8,128)(2,1)S(1)} custom-call(s32[4]{0:T(128)S(1)} %pad_add_fusion.1.order, bf16[1536,1536]{1,0:T(8,128)(2,1)S(1)} %bitcast.49, bf16[384,384]{1,0:T(8,128)(2,1)S(1)} %slice.35.refs_0_, bf16[384,384]{1,0:T(8,128)(2,1)S(1)} %collective-permute-done.6.refs_1_, bf16[384,384]{1,0:T(8,128)(2,1)S(1)} %collective-permute-done.7.refs_2_, ...), custom_call_target="tpu_custom_call" | custom-call | flops 905969664 | bytes 2359296 | tf_op jit(solution)/shard_map/pallas_call | solution.py:131
  55.2 0.1 slice_bitcast_fusion.6
  55.2 4.8 %collective-permute-start.9 = (bf16[384,384]{1,0:T(8,128)(2,1)S(1)}, bf16[384,384]{1,0:T(8,128)(2,1)S(1)}, u32[]{:S(2)}, u32[]{:S(2)}) collective-permute-start(bf16[384,384]{1,0:T(8,128)(2,1)S(1)} %get-tuple-element.23), channel_id=1, source_target_pairs={{0,64},{1,65},{32,96},{33,97},{64,0},{65,1},{96,32},{97,33},{2,66}... | collective-permute-start | bytes 884744 | tf_op jit(solution)/shard_map/ppermute | solution.py:15
  60.0 0.0 collective-permute-done.2.refs_3_
  60.1 2.0 %collective-permute-start.10 = (bf16[384,384]{1,0:T(8,128)(2,1)S(1)}, bf16[384,384]{1,0:T(8,128)(2,1)S(1)}, u32[]{:S(2)}, u32[]{:S(2)}) collective-permute-start(bf16[384,384]{1,0:T(8,128)(2,1)S(1)} %get-tuple-element.24), channel_id=1, source_target_pairs={{0,32},{1,33},{32,64},{33,65},{64,96},{65,97},{96,0},{97,1},{2,34}... | collective-permute-start | bytes 884744 | tf_op jit(solution)/shard_map/ppermute | solution.py:15
  62.1 0.0 collective-permute-done.1.refs_2_
  62.1 0.0 collective-permute-done.refs_1_
  62.1 2.9 %shard_map.48 = bf16[2,384,640]{2,1,0:T(8,128)(2,1)S(1)} custom-call(s32[4]{0:T(128)S(1)} %pad_add_fusion.1.order, bf16[1536,1536]{1,0:T(8,128)(2,1)S(1)} %bitcast.50, bf16[384,640]{1,0:T(8,128)(2,1)S(1)} %slice.34.refs_0_, bf16[384,640]{1,0:T(8,128)(2,1)S(1)} %collective-permute-done.refs_1_, bf16[384,640]{1,0:T(8,128)(2,1)S(1)} %collective-permute-done.1.refs_2_, ...), custom_call_target="tpu_custom_call" | custom-call | flops 1509949440 | bytes 2359296 | tf_op jit(solution)/shard_map/pallas_call | solution.py:131
  65.0 0.1 slice_bitcast_fusion.1
  65.1 3.6 %collective-permute-start.4 = (bf16[384,640]{1,0:T(8,128)(2,1)S(1)}, bf16[384,640]{1,0:T(8,128)(2,1)S(1)}, u32[]{:S(2)}, u32[]{:S(2)}) collective-permute-start(bf16[384,640]{1,0:T(8,128)(2,1)S(1)} %get-tuple-element.21), channel_id=1, source_target_pairs={{0,32},{1,33},{32,64},{33,65},{64,96},{65,97},{96,0},{97,1},{2,34}... | collective-permute-start | bytes 1474568 | tf_op jit(solution)/shard_map/ppermute | solution.py:15
  68.7 3.6 %collective-permute-start.3 = (bf16[384,640]{1,0:T(8,128)(2,1)S(1)}, bf16[384,640]{1,0:T(8,128)(2,1)S(1)}, u32[]{:S(2)}, u32[]{:S(2)}) collective-permute-start(bf16[384,640]{1,0:T(8,128)(2,1)S(1)} %get-tuple-element.22), channel_id=1, source_target_pairs={{0,64},{1,65},{32,96},{33,97},{64,0},{65,1},{96,32},{97,33},{2,66}... | collective-permute-start | bytes 1474568 | tf_op jit(solution)/shard_map/ppermute | solution.py:15
  72.3 2.9 %shard_map.47 = bf16[2,384,640]{2,1,0:T(8,128)(2,1)S(1)} custom-call(s32[4]{0:T(128)S(1)} %pad_add_fusion.1.order, bf16[1536,1536]{1,0:T(8,128)(2,1)S(1)} %bitcast.51, bf16[384,640]{1,0:T(8,128)(2,1)S(1)} %slice.34.refs_0_, bf16[384,640]{1,0:T(8,128)(2,1)S(1)} %collective-permute-done.refs_1_, bf16[384,640]{1,0:T(8,128)(2,1)S(1)} %collective-permute-done.1.refs_2_, ...), custom_call_target="tpu_custom_call" | custom-call | flops 1509949440 | bytes 2359296 | tf_op jit(solution)/shard_map/pallas_call | solution.py:131
  75.3 0.1 slice_bitcast_fusion
  75.4 0.0 collective-permute-done.11
  75.4 2.7 %collective-permute-start.5 = (bf16[384,640]{1,0:T(8,128)(2,1)S(1)}, bf16[384,640]{1,0:T(8,128)(2,1)S(1)}, u32[]{:S(2)}, u32[]{:S(2)}) collective-permute-start(bf16[384,640]{1,0:T(8,128)(2,1)S(1)} %get-tuple-element.19), channel_id=1, source_target_pairs={{0,96},{1,97},{32,0},{33,1},{64,32},{65,33},{96,64},{97,65},{2,98}... | collective-permute-start | bytes 1474568 | tf_op jit(solution)/shard_map/ppermute | solution.py:15
  78.1 0.0 collective-permute-done.9
  78.1 0.2 fusion.2
  78.2 0.1 constant_dynamic-slice_fusion.5
  78.3 9.1 %collective-permute-start.12 = (bf16[2,96,384]{2,1,0:T(8,128)(2,1)S(1)}, bf16[2,96,384]{2,1,0:T(8,128)(2,1)S(1)}, u32[]{:S(2)}, u32[]{:S(2)}) collective-permute-start(bf16[2,96,384]{2,1,0:T(8,128)(2,1)S(1)} %pad_maximum_fusion.3), channel_id=1, source_target_pairs={{0,128},{1,385},{128,0},{129,257},{256,384},{257,129},{384,256},{3... | collective-permute-start | bytes 442376 | tf_op jit(solution)/shard_map/ppermute | solution.py:15
  87.5 7.7 %collective-permute-done.12 = bf16[2,96,384]{2,1,0:T(8,128)(2,1)S(1)} collective-permute-done((bf16[2,96,384]{2,1,0:T(8,128)(2,1)S(1)}, bf16[2,96,384]{2,1,0:T(8,128)(2,1)S(1)}, u32[]{:S(2)}, u32[]{:S(2)}) %collective-permute-start.12) | collective-permute-done | bytes 147488 | tf_op jit(solution)/shard_map/ppermute | solution.py:15
  95.2 0.2 add_convert_fusion
  95.5 4.9 %collective-permute-start.14 = (bf16[2,96,640]{2,1,0:T(8,128)(2,1)S(1)}, bf16[2,96,640]{2,1,0:T(8,128)(2,1)S(1)}, u32[]{:S(2)}, u32[]{:S(2)}) collective-permute-start(bf16[2,96,640]{2,1,0:T(8,128)(2,1)S(1)} %pad_maximum_fusion.1), channel_id=1, source_target_pairs={{0,128},{1,385},{128,0},{129,257},{256,384},{257,129},{384,256},{3... | collective-permute-start | bytes 737288 | tf_op jit(solution)/shard_map/ppermute | solution.py:15
  100.5 8.7 %collective-permute-start.13 = (bf16[96,384]{1,0:T(8,128)(2,1)S(1)}, bf16[96,384]{1,0:T(8,128)(2,1)S(1)}, u32[]{:S(2)}, u32[]{:S(2)}) collective-permute-start(bf16[96,384]{1,0:T(8,128)(2,1)S(1)} %fusion.6), channel_id=1, source_target_pairs={{0,384},{1,129},{128,256},{129,1},{256,128},{257,385},{384,0},{385... | collective-permute-start | bytes 221192 | tf_op jit(solution)/shard_map/ppermute | solution.py:15
  109.2 14.4 %collective-permute-done.14 = bf16[2,96,640]{2,1,0:T(8,128)(2,1)S(1)} collective-permute-done((bf16[2,96,640]{2,1,0:T(8,128)(2,1)S(1)}, bf16[2,96,640]{2,1,0:T(8,128)(2,1)S(1)}, u32[]{:S(2)}, u32[]{:S(2)}) %collective-permute-start.14) | collective-permute-done | bytes 245792 | tf_op jit(solution)/shard_map/ppermute | solution.py:15
  123.6 1.9 %collective-permute-start.15 = (bf16[96,640]{1,0:T(8,128)(2,1)S(1)}, bf16[96,640]{1,0:T(8,128)(2,1)S(1)}, u32[]{:S(2)}, u32[]{:S(2)}) collective-permute-start(bf16[96,640]{1,0:T(8,128)(2,1)S(1)} %fusion.5), channel_id=1, source_target_pairs={{0,384},{1,129},{128,256},{129,1},{256,128},{257,385},{384,0},{385... | collective-permute-start | bytes 368648 | tf_op jit(solution)/shard_map/ppermute | solution.py:15
  125.5 0.0 collective-permute-done.13
  125.6 8.7 %collective-permute-done.15 = bf16[96,640]{1,0:T(8,128)(2,1)S(1)} collective-permute-done((bf16[96,640]{1,0:T(8,128)(2,1)S(1)}, bf16[96,640]{1,0:T(8,128)(2,1)S(1)}, u32[]{:S(2)}, u32[]{:S(2)}) %collective-permute-start.15) | collective-permute-done | bytes 122912 | tf_op jit(solution)/shard_map/ppermute | solution.py:15
  134.3 0.1 fusion.3
  134.3 0.7 pad_maximum_fusion.2
  (16 shorter events, 0.3 us)
Async XLA Ops:
  21.1 25.2 %collective-permute-start.8 = (bf16[384,384]{1,0:T(8,128)(2,1)S(1)}, bf16[384,384]{1,0:T(8,128)(2,1)S(1)}, u32[]{:S(2)}, u32[]{:S(2)}) collective-permute-start(bf16[384,384]{1,0:T(8,128)(2,1)S(1)} %slice.35.refs_0_), channel_id=1, source_target_pairs={{0,8},{1,9},{8,16},{9,17},{16,24},{17,25},{24,0},{25,1},{2,10},{3,... | collective-permute-start | bytes 884744 | tf_op jit(solution)/shard_map/ppermute | solution.py:15
  24.5 23.7 %collective-permute-start.7 = (bf16[384,384]{1,0:T(8,128)(2,1)S(1)}, bf16[384,384]{1,0:T(8,128)(2,1)S(1)}, u32[]{:S(2)}, u32[]{:S(2)}) collective-permute-start(bf16[384,384]{1,0:T(8,128)(2,1)S(1)} %slice.35.refs_0_), channel_id=1, source_target_pairs={{0,16},{1,17},{8,24},{9,25},{16,0},{17,1},{24,8},{25,9},{2,18},{3,... | collective-permute-start | bytes 884744 | tf_op jit(solution)/shard_map/ppermute | solution.py:15
  27.5 20.7 %collective-permute-start.6 = (bf16[384,384]{1,0:T(8,128)(2,1)S(1)}, bf16[384,384]{1,0:T(8,128)(2,1)S(1)}, u32[]{:S(2)}, u32[]{:S(2)}) collective-permute-start(bf16[384,384]{1,0:T(8,128)(2,1)S(1)} %slice.35.refs_0_), channel_id=1, source_target_pairs={{0,24},{1,25},{8,0},{9,1},{16,8},{17,9},{24,16},{25,17},{2,26},{3,... | collective-permute-start | bytes 884744 | tf_op jit(solution)/shard_map/ppermute | solution.py:15
  31.7 28.4 %collective-permute-start.2 = (bf16[384,640]{1,0:T(8,128)(2,1)S(1)}, bf16[384,640]{1,0:T(8,128)(2,1)S(1)}, u32[]{:S(2)}, u32[]{:S(2)}) collective-permute-start(bf16[384,640]{1,0:T(8,128)(2,1)S(1)} %slice.34.refs_0_), channel_id=1, source_target_pairs={{0,8},{1,9},{8,16},{9,17},{16,24},{17,25},{24,0},{25,1},{2,10},{3,... | collective-permute-start | bytes 1474568 | tf_op jit(solution)/shard_map/ppermute | solution.py:15
  33.6 28.5 %collective-permute-start.1 = (bf16[384,640]{1,0:T(8,128)(2,1)S(1)}, bf16[384,640]{1,0:T(8,128)(2,1)S(1)}, u32[]{:S(2)}, u32[]{:S(2)}) collective-permute-start(bf16[384,640]{1,0:T(8,128)(2,1)S(1)} %slice.34.refs_0_), channel_id=1, source_target_pairs={{0,16},{1,17},{8,24},{9,25},{16,0},{17,1},{24,8},{25,9},{2,18},{3,... | collective-permute-start | bytes 1474568 | tf_op jit(solution)/shard_map/ppermute | solution.py:15
  40.1 0.7 copy-start
  46.3 15.8 %collective-permute-start = (bf16[384,640]{1,0:T(8,128)(2,1)S(1)}, bf16[384,640]{1,0:T(8,128)(2,1)S(1)}, u32[]{:S(2)}, u32[]{:S(2)}) collective-permute-start(bf16[384,640]{1,0:T(8,128)(2,1)S(1)} %slice.34.refs_0_), channel_id=1, source_target_pairs={{0,24},{1,25},{8,0},{9,1},{16,8},{17,9},{24,16},{25,17},{2,26},{3,... | collective-permute-start | bytes 1474568 | tf_op jit(solution)/shard_map/ppermute | solution.py:15
  50.5 24.8 %collective-permute-start.11 = (bf16[384,384]{1,0:T(8,128)(2,1)S(1)}, bf16[384,384]{1,0:T(8,128)(2,1)S(1)}, u32[]{:S(2)}, u32[]{:S(2)}) collective-permute-start(bf16[384,384]{1,0:T(8,128)(2,1)S(1)} %slice_bitcast_fusion.4), channel_id=1, source_target_pairs={{0,96},{1,97},{32,0},{33,1},{64,32},{65,33},{96,64},{97,65},{2,98}... | collective-permute-start | bytes 884744 | tf_op jit(solution)/shard_map/ppermute | solution.py:15
  55.2 22.8 %collective-permute-start.9 = (bf16[384,384]{1,0:T(8,128)(2,1)S(1)}, bf16[384,384]{1,0:T(8,128)(2,1)S(1)}, u32[]{:S(2)}, u32[]{:S(2)}) collective-permute-start(bf16[384,384]{1,0:T(8,128)(2,1)S(1)} %get-tuple-element.23), channel_id=1, source_target_pairs={{0,64},{1,65},{32,96},{33,97},{64,0},{65,1},{96,32},{97,33},{2,66}... | collective-permute-start | bytes 884744 | tf_op jit(solution)/shard_map/ppermute | solution.py:15
  60.1 18.0 %collective-permute-start.10 = (bf16[384,384]{1,0:T(8,128)(2,1)S(1)}, bf16[384,384]{1,0:T(8,128)(2,1)S(1)}, u32[]{:S(2)}, u32[]{:S(2)}) collective-permute-start(bf16[384,384]{1,0:T(8,128)(2,1)S(1)} %get-tuple-element.24), channel_id=1, source_target_pairs={{0,32},{1,33},{32,64},{33,65},{64,96},{65,97},{96,0},{97,1},{2,34}... | collective-permute-start | bytes 884744 | tf_op jit(solution)/shard_map/ppermute | solution.py:15
  65.1 30.1 %collective-permute-start.4 = (bf16[384,640]{1,0:T(8,128)(2,1)S(1)}, bf16[384,640]{1,0:T(8,128)(2,1)S(1)}, u32[]{:S(2)}, u32[]{:S(2)}) collective-permute-start(bf16[384,640]{1,0:T(8,128)(2,1)S(1)} %get-tuple-element.21), channel_id=1, source_target_pairs={{0,32},{1,33},{32,64},{33,65},{64,96},{65,97},{96,0},{97,1},{2,34}... | collective-permute-start | bytes 1474568 | tf_op jit(solution)/shard_map/ppermute | solution.py:15
  68.7 26.5 %collective-permute-start.3 = (bf16[384,640]{1,0:T(8,128)(2,1)S(1)}, bf16[384,640]{1,0:T(8,128)(2,1)S(1)}, u32[]{:S(2)}, u32[]{:S(2)}) collective-permute-start(bf16[384,640]{1,0:T(8,128)(2,1)S(1)} %get-tuple-element.22), channel_id=1, source_target_pairs={{0,64},{1,65},{32,96},{33,97},{64,0},{65,1},{96,32},{97,33},{2,66}... | collective-permute-start | bytes 1474568 | tf_op jit(solution)/shard_map/ppermute | solution.py:15
  75.4 19.8 %collective-permute-start.5 = (bf16[384,640]{1,0:T(8,128)(2,1)S(1)}, bf16[384,640]{1,0:T(8,128)(2,1)S(1)}, u32[]{:S(2)}, u32[]{:S(2)}) collective-permute-start(bf16[384,640]{1,0:T(8,128)(2,1)S(1)} %get-tuple-element.19), channel_id=1, source_target_pairs={{0,96},{1,97},{32,0},{33,1},{64,32},{65,33},{96,64},{97,65},{2,98}... | collective-permute-start | bytes 1474568 | tf_op jit(solution)/shard_map/ppermute | solution.py:15
  78.3 16.9 %collective-permute-start.12 = (bf16[2,96,384]{2,1,0:T(8,128)(2,1)S(1)}, bf16[2,96,384]{2,1,0:T(8,128)(2,1)S(1)}, u32[]{:S(2)}, u32[]{:S(2)}) collective-permute-start(bf16[2,96,384]{2,1,0:T(8,128)(2,1)S(1)} %pad_maximum_fusion.3), channel_id=1, source_target_pairs={{0,128},{1,385},{128,0},{129,257},{256,384},{257,129},{384,256},{3... | collective-permute-start | bytes 442376 | tf_op jit(solution)/shard_map/ppermute | solution.py:15
  95.5 28.0 %collective-permute-start.14 = (bf16[2,96,640]{2,1,0:T(8,128)(2,1)S(1)}, bf16[2,96,640]{2,1,0:T(8,128)(2,1)S(1)}, u32[]{:S(2)}, u32[]{:S(2)}) collective-permute-start(bf16[2,96,640]{2,1,0:T(8,128)(2,1)S(1)} %pad_maximum_fusion.1), channel_id=1, source_target_pairs={{0,128},{1,385},{128,0},{129,257},{256,384},{257,129},{384,256},{3... | collective-permute-start | bytes 737288 | tf_op jit(solution)/shard_map/ppermute | solution.py:15
  100.5 25.0 %collective-permute-start.13 = (bf16[96,384]{1,0:T(8,128)(2,1)S(1)}, bf16[96,384]{1,0:T(8,128)(2,1)S(1)}, u32[]{:S(2)}, u32[]{:S(2)}) collective-permute-start(bf16[96,384]{1,0:T(8,128)(2,1)S(1)} %fusion.6), channel_id=1, source_target_pairs={{0,384},{1,129},{128,256},{129,1},{256,128},{257,385},{384,0},{385... | collective-permute-start | bytes 221192 | tf_op jit(solution)/shard_map/ppermute | solution.py:15
  123.6 10.7 %collective-permute-start.15 = (bf16[96,640]{1,0:T(8,128)(2,1)S(1)}, bf16[96,640]{1,0:T(8,128)(2,1)S(1)}, u32[]{:S(2)}, u32[]{:S(2)}) collective-permute-start(bf16[96,640]{1,0:T(8,128)(2,1)S(1)} %fusion.5), channel_id=1, source_target_pairs={{0,384},{1,129},{128,256},{129,1},{256,128},{257,385},{384,0},{385... | collective-permute-start | bytes 368648 | tf_op jit(solution)/shard_map/ppermute | solution.py:15

commit v6 on v5

--- a/solution.py
+++ b/solution.py
@@ -123,7 +123,7 @@
     out[...] = jnp.dot(coupled[...], whole[...], preferred_element_type=jnp.float32).astype(out.dtype)[None]
 
 
-def multiply(coupled, blocks, order, first):
+def multiply(coupled, blocks, order, first, count):
     rows, depth = coupled.shape
     width = blocks[0].shape[1]
     tile = rows // 4
@@ -132,15 +132,15 @@
         multiply_kernel,
         grid_spec=pltpu.PrefetchScalarGridSpec(
             num_scalar_prefetch=1,
-            grid=(2,),
+            grid=(count,),
             in_specs=[pl.BlockSpec((tile, depth), lambda i, s: ((i + first) % 4, 0))] + [one] * 4,
             out_specs=pl.BlockSpec((1, tile, width), lambda i, s: (i, 0, 0)),
             scratch_shapes=[pltpu.VMEM((depth, width), blocks[0].dtype)],
         ),
-        out_shape=jax.ShapeDtypeStruct((2, tile, width), blocks[0].dtype),
+        out_shape=jax.ShapeDtypeStruct((count, tile, width), blocks[0].dtype),
         compiler_params=pltpu.CompilerParams(vmem_limit_bytes=VMEM * 2**20),
         cost_estimate=pl.CostEstimate(
-            flops=rows * depth * width, bytes_accessed=rows * depth, transcendentals=0
+            flops=count * tile * depth * width * 2, bytes_accessed=count * tile * depth * 2, transcendentals=0
         ),
     )(as_ints(order), coupled, *blocks)
 
@@ -169,9 +169,12 @@
             part, masked = lax.optimization_barrier((part, masked))
         start += width
         blocks, order = gather(part, "x"), places("dir", x, core)
-        up, far = multiply(coupled, blocks, order, 1)
-        down, own = multiply(coupled, blocks, order, 3)
-        product.append((own, up, far, down))
+        if product:
+            product.append(tuple(multiply(coupled, blocks, order, 0, 4)))
+        else:
+            up, far = multiply(coupled, blocks, order, 1, 2)
+            down, own = multiply(coupled, blocks, order, 3, 2)
+            product.append((own, up, far, down))
 
     done, earlier = [], None
     for part, kind in zip(product, SCATTER_Z):

time: 136 us -> 136 us (level)
  the two profiles are of different devices: /device:TPU:18 before, /device:TPU:22 now
where the time goes in v6:
time: 136 us; the launch traced here: 135 us
  starting transfers between devices  66.2 us (49%)
  waiting for transfers between devices  29 us (21%)
  blocking collectives  21.1 us (16%)
  Pallas kernels  15.1 us (11%)
  local copies, waits for them, and re-layouts  1.88 us (1%)
  other arithmetic  1.5 us (1%)
    ppermute x16, starting transfers between devices, permute(): return lax.ppermute(block, (axis, 'core'), moves)  66.2 us
    ppermute x16, waiting for transfers between devices, permute(): return lax.ppermute(block, (axis, 'core'), moves)  29 us
    all_gather x1, blocking collectives, body(): near = lax.all_gather(amplitudes, 'zl', axis=0, tiled=True)  21.1 us
    pallas_call x3, Pallas kernels, multiply(): pl.pallas_call(multiply_kernel, grid_spec=pltpu.PrefetchScalarGridSpec(nu...  9.64 us
    pallas_call x1, Pallas kernels, couple(): pl.pallas_call(couple_kernel, grid_spec=pltpu.PrefetchScalarGridSpec(num_...  5.44 us
  transfers between devices with their start and end apart: 16, of which 3 were waited for; matrix products, arithmetic and copies ran while one was open for 1% of the time, Pallas kernels for 11%

profile of v6, /device:TPU:22, one launch (start us, length us, event | category | flops | bytes accessed | tf_op | source)
XLA Modules:
  0.0 135.4 jit_solution(17816513592907608596)
XLA Ops:
  0.0 21.1 %all_gather.3 = bf16[384,1024]{1,0:T(8,128)(2,1)S(1)} all-gather(bf16[96,1024]{1,0:T(8,128)(2,1)} %param.4), channel_id=1, replica_groups=mesh['zh'=4,'y'=4,'x'=4,'zl'=4,'core'=2] {'zl'}, dimensions={0}, use_global_device_ids=true | all-gather | bytes 983040 | tf_op jit(solution)/shard_map/all_gather | solution.py:156
  21.1 2.7 %collective-permute-start.6 = (bf16[384,384]{1,0:T(8,128)(2,1)S(1)}, bf16[384,384]{1,0:T(8,128)(2,1)S(1)}, u32[]{:S(2)}, u32[]{:S(2)}) collective-permute-start(bf16[384,384]{1,0:T(8,128)(2,1)S(1)} %slice.35.refs_0_), channel_id=1, source_target_pairs={{0,24},{1,25},{8,0},{9,1},{16,8},{17,9},{24,16},{25,17},{2,26},{3,... | collective-permute-start | bytes 884744 | tf_op jit(solution)/shard_map/ppermute | solution.py:15
  23.8 3.0 %collective-permute-start.7 = (bf16[384,384]{1,0:T(8,128)(2,1)S(1)}, bf16[384,384]{1,0:T(8,128)(2,1)S(1)}, u32[]{:S(2)}, u32[]{:S(2)}) collective-permute-start(bf16[384,384]{1,0:T(8,128)(2,1)S(1)} %slice.35.refs_0_), channel_id=1, source_target_pairs={{0,16},{1,17},{8,24},{9,25},{16,0},{17,1},{24,8},{25,9},{2,18},{3,... | collective-permute-start | bytes 884744 | tf_op jit(solution)/shard_map/ppermute | solution.py:15
  26.9 4.0 %collective-permute-start.8 = (bf16[384,384]{1,0:T(8,128)(2,1)S(1)}, bf16[384,384]{1,0:T(8,128)(2,1)S(1)}, u32[]{:S(2)}, u32[]{:S(2)}) collective-permute-start(bf16[384,384]{1,0:T(8,128)(2,1)S(1)} %slice.35.refs_0_), channel_id=1, source_target_pairs={{0,8},{1,9},{8,16},{9,17},{16,24},{17,25},{24,0},{25,1},{2,10},{3,... | collective-permute-start | bytes 884744 | tf_op jit(solution)/shard_map/ppermute | solution.py:15
  30.9 0.1 slice.34.refs_0_
  30.9 2.0 %collective-permute-start = (bf16[384,640]{1,0:T(8,128)(2,1)S(1)}, bf16[384,640]{1,0:T(8,128)(2,1)S(1)}, u32[]{:S(2)}, u32[]{:S(2)}) collective-permute-start(bf16[384,640]{1,0:T(8,128)(2,1)S(1)} %slice.34.refs_0_), channel_id=1, source_target_pairs={{0,24},{1,25},{8,0},{9,1},{16,8},{17,9},{24,16},{25,17},{2,26},{3,... | collective-permute-start | bytes 1474568 | tf_op jit(solution)/shard_map/ppermute | solution.py:15
  32.9 4.2 %collective-permute-start.1 = (bf16[384,640]{1,0:T(8,128)(2,1)S(1)}, bf16[384,640]{1,0:T(8,128)(2,1)S(1)}, u32[]{:S(2)}, u32[]{:S(2)}) collective-permute-start(bf16[384,640]{1,0:T(8,128)(2,1)S(1)} %slice.34.refs_0_), channel_id=1, source_target_pairs={{0,16},{1,17},{8,24},{9,25},{16,0},{17,1},{24,8},{25,9},{2,18},{3,... | collective-permute-start | bytes 1474568 | tf_op jit(solution)/shard_map/ppermute | solution.py:15
  37.2 0.7 dynamic-slice_bitcast_fusion.1
  38.1 0.1 pad_add_fusion.2.rows_to
  38.2 0.0 copy-start
  38.2 0.7 copy-done
  38.9 5.4 %shard_map.46 = (bf16[4,4,96,1536]{3,2,1,0:T(8,128)(2,1)S(1)}, f32[8,128]{1,0:T(8,128)}) custom-call(s32[4]{0:T(128)S(1)} %pad_add_fusion.2.rows_to, bf16[1536,1536]{1,0:T(8,128)(2,1)} %block.1, s32[6,128]{1,0:T(8,128)S(1)} %bitcast.52, s32[48,128]{1,0:T(8,128)S(1)} %bitcast.51), custom_call_target="tpu_custom_call" | custom-call | bytes 9437184 | tf_op jit(solution)/shard_map/pallas_call | solution.py:89
  44.3 0.1 pad_add_fusion.1.order
  44.4 0.0 collective-permute-done.6.refs_1_
  44.4 4.3 %collective-permute-start.2 = (bf16[384,640]{1,0:T(8,128)(2,1)S(1)}, bf16[384,640]{1,0:T(8,128)(2,1)S(1)}, u32[]{:S(2)}, u32[]{:S(2)}) collective-permute-start(bf16[384,640]{1,0:T(8,128)(2,1)S(1)} %slice.34.refs_0_), channel_id=1, source_target_pairs={{0,8},{1,9},{8,16},{9,17},{16,24},{17,25},{24,0},{25,1},{2,10},{3,... | collective-permute-start | bytes 1474568 | tf_op jit(solution)/shard_map/ppermute | solution.py:15
  48.7 0.0 collective-permute-done.7.refs_2_
  48.7 0.0 collective-permute-done.8.refs_3_
  48.8 2.3 %shard_map.49 = bf16[2,384,384]{2,1,0:T(8,128)(2,1)S(1)} custom-call(s32[4]{0:T(128)S(1)} %pad_add_fusion.1.order, bf16[1536,1536]{1,0:T(8,128)(2,1)S(1)} %bitcast.48, bf16[384,384]{1,0:T(8,128)(2,1)S(1)} %slice.35.refs_0_, bf16[384,384]{1,0:T(8,128)(2,1)S(1)} %collective-permute-done.6.refs_1_, bf16[384,384]{1,0:T(8,128)(2,1)S(1)} %collective-permute-done.7.refs_2_, ...), custom_call_target="tpu_custom_call" | custom-call | flops 905969664 | bytes 2359296 | tf_op jit(solution)/shard_map/pallas_call | solution.py:131
  51.0 0.1 slice_bitcast_fusion.6
  51.1 3.2 %collective-permute-start.10 = (bf16[384,384]{1,0:T(8,128)(2,1)S(1)}, bf16[384,384]{1,0:T(8,128)(2,1)S(1)}, u32[]{:S(2)}, u32[]{:S(2)}) collective-permute-start(bf16[384,384]{1,0:T(8,128)(2,1)S(1)} %get-tuple-element.24), channel_id=1, source_target_pairs={{0,32},{1,33},{32,64},{33,65},{64,96},{65,97},{96,0},{97,1},{2,34}... | collective-permute-start | bytes 884744 | tf_op jit(solution)/shard_map/ppermute | solution.py:15
  54.3 2.5 %collective-permute-start.9 = (bf16[384,384]{1,0:T(8,128)(2,1)S(1)}, bf16[384,384]{1,0:T(8,128)(2,1)S(1)}, u32[]{:S(2)}, u32[]{:S(2)}) collective-permute-start(bf16[384,384]{1,0:T(8,128)(2,1)S(1)} %get-tuple-element.23), channel_id=1, source_target_pairs={{0,64},{1,65},{32,96},{33,97},{64,0},{65,1},{96,32},{97,33},{2,66}... | collective-permute-start | bytes 884744 | tf_op jit(solution)/shard_map/ppermute | solution.py:15
  56.8 2.3 %shard_map.48 = bf16[2,384,384]{2,1,0:T(8,128)(2,1)S(1)} custom-call(s32[4]{0:T(128)S(1)} %pad_add_fusion.1.order, bf16[1536,1536]{1,0:T(8,128)(2,1)S(1)} %bitcast.49, bf16[384,384]{1,0:T(8,128)(2,1)S(1)} %slice.35.refs_0_, bf16[384,384]{1,0:T(8,128)(2,1)S(1)} %collective-permute-done.6.refs_1_, bf16[384,384]{1,0:T(8,128)(2,1)S(1)} %collective-permute-done.7.refs_2_, ...), custom_call_target="tpu_custom_call" | custom-call | flops 905969664 | bytes 2359296 | tf_op jit(solution)/shard_map/pallas_call | solution.py:131
  59.1 0.0 collective-permute-done.refs_1_
  59.1 3.0 %collective-permute-start.11 = (bf16[384,384]{1,0:T(8,128)(2,1)S(1)}, bf16[384,384]{1,0:T(8,128)(2,1)S(1)}, u32[]{:S(2)}, u32[]{:S(2)}) collective-permute-start(bf16[384,384]{1,0:T(8,128)(2,1)S(1)} %slice_bitcast_fusion.4), channel_id=1, source_target_pairs={{0,96},{1,97},{32,0},{33,1},{64,32},{65,33},{96,64},{97,65},{2,98}... | collective-permute-start | bytes 884744 | tf_op jit(solution)/shard_map/ppermute | solution.py:15
  62.2 0.0 collective-permute-done.1.refs_2_
  62.2 0.0 collective-permute-done.2.refs_3_
  62.2 5.1 %shard_map.47 = bf16[4,384,640]{2,1,0:T(8,128)(2,1)S(1)} custom-call(s32[4]{0:T(128)S(1)} %pad_add_fusion.1.order, bf16[1536,1536]{1,0:T(8,128)(2,1)S(1)} %bitcast.50, bf16[384,640]{1,0:T(8,128)(2,1)S(1)} %slice.34.refs_0_, bf16[384,640]{1,0:T(8,128)(2,1)S(1)} %collective-permute-done.refs_1_, bf16[384,640]{1,0:T(8,128)(2,1)S(1)} %collective-permute-done.1.refs_2_, ...), custom_call_target="tpu_custom_call" | custom-call | flops 3019898880 | bytes 4718592 | tf_op jit(solution)/shard_map/pallas_call | solution.py:131
  67.3 0.2 slice_bitcast_fusion
  67.5 5.0 %collective-permute-start.3 = (bf16[384,640]{1,0:T(8,128)(2,1)S(1)}, bf16[384,640]{1,0:T(8,128)(2,1)S(1)}, u32[]{:S(2)}, u32[]{:S(2)}) collective-permute-start(bf16[384,640]{1,0:T(8,128)(2,1)S(1)} %get-tuple-element.21), channel_id=1, source_target_pairs={{0,64},{1,65},{32,96},{33,97},{64,0},{65,1},{96,32},{97,33},{2,66}... | collective-permute-start | bytes 1474568 | tf_op jit(solution)/shard_map/ppermute | solution.py:15
  72.6 3.2 %collective-permute-start.4 = (bf16[384,640]{1,0:T(8,128)(2,1)S(1)}, bf16[384,640]{1,0:T(8,128)(2,1)S(1)}, u32[]{:S(2)}, u32[]{:S(2)}) collective-permute-start(bf16[384,640]{1,0:T(8,128)(2,1)S(1)} %get-tuple-element.20), channel_id=1, source_target_pairs={{0,32},{1,33},{32,64},{33,65},{64,96},{65,97},{96,0},{97,1},{2,34}... | collective-permute-start | bytes 1474568 | tf_op jit(solution)/shard_map/ppermute | solution.py:15
  75.8 2.6 %collective-permute-start.5 = (bf16[384,640]{1,0:T(8,128)(2,1)S(1)}, bf16[384,640]{1,0:T(8,128)(2,1)S(1)}, u32[]{:S(2)}, u32[]{:S(2)}) collective-permute-start(bf16[384,640]{1,0:T(8,128)(2,1)S(1)} %get-tuple-element.19), channel_id=1, source_target_pairs={{0,96},{1,97},{32,0},{33,1},{64,32},{65,33},{96,64},{97,65},{2,98}... | collective-permute-start | bytes 1474568 | tf_op jit(solution)/shard_map/ppermute | solution.py:15
  78.4 0.0 collective-permute-done.11
  78.4 0.2 fusion.2
  78.6 0.1 constant_dynamic-slice_fusion.5
  78.7 9.1 %collective-permute-start.12 = (bf16[2,96,384]{2,1,0:T(8,128)(2,1)S(1)}, bf16[2,96,384]{2,1,0:T(8,128)(2,1)S(1)}, u32[]{:S(2)}, u32[]{:S(2)}) collective-permute-start(bf16[2,96,384]{2,1,0:T(8,128)(2,1)S(1)} %pad_maximum_fusion.3), channel_id=1, source_target_pairs={{0,128},{1,385},{128,0},{129,257},{256,384},{257,129},{384,256},{3... | collective-permute-start | bytes 442376 | tf_op jit(solution)/shard_map/ppermute | solution.py:15
  87.9 7.5 %collective-permute-done.12 = bf16[2,96,384]{2,1,0:T(8,128)(2,1)S(1)} collective-permute-done((bf16[2,96,384]{2,1,0:T(8,128)(2,1)S(1)}, bf16[2,96,384]{2,1,0:T(8,128)(2,1)S(1)}, u32[]{:S(2)}, u32[]{:S(2)}) %collective-permute-start.12) | collective-permute-done | bytes 147488 | tf_op jit(solution)/shard_map/ppermute | solution.py:15
  95.3 0.0 collective-permute-done.3
  95.3 0.0 collective-permute-done.4
  95.3 0.0 collective-permute-done.5
  95.3 0.2 add_convert_fusion
  95.7 3.9 %collective-permute-start.14 = (bf16[2,96,640]{2,1,0:T(8,128)(2,1)S(1)}, bf16[2,96,640]{2,1,0:T(8,128)(2,1)S(1)}, u32[]{:S(2)}, u32[]{:S(2)}) collective-permute-start(bf16[2,96,640]{2,1,0:T(8,128)(2,1)S(1)} %pad_maximum_fusion.1), channel_id=1, source_target_pairs={{0,128},{1,385},{128,0},{129,257},{256,384},{257,129},{384,256},{3... | collective-permute-start | bytes 737288 | tf_op jit(solution)/shard_map/ppermute | solution.py:15
  99.6 9.9 %collective-permute-start.13 = (bf16[96,384]{1,0:T(8,128)(2,1)S(1)}, bf16[96,384]{1,0:T(8,128)(2,1)S(1)}, u32[]{:S(2)}, u32[]{:S(2)}) collective-permute-start(bf16[96,384]{1,0:T(8,128)(2,1)S(1)} %fusion.6), channel_id=1, source_target_pairs={{0,384},{1,129},{128,256},{129,1},{256,128},{257,385},{384,0},{385... | collective-permute-start | bytes 221192 | tf_op jit(solution)/shard_map/ppermute | solution.py:15
  109.6 14.3 %collective-permute-done.14 = bf16[2,96,640]{2,1,0:T(8,128)(2,1)S(1)} collective-permute-done((bf16[2,96,640]{2,1,0:T(8,128)(2,1)S(1)}, bf16[2,96,640]{2,1,0:T(8,128)(2,1)S(1)}, u32[]{:S(2)}, u32[]{:S(2)}) %collective-permute-start.14) | collective-permute-done | bytes 245792 | tf_op jit(solution)/shard_map/ppermute | solution.py:15
  123.9 3.4 %collective-permute-start.15 = (bf16[96,640]{1,0:T(8,128)(2,1)S(1)}, bf16[96,640]{1,0:T(8,128)(2,1)S(1)}, u32[]{:S(2)}, u32[]{:S(2)}) collective-permute-start(bf16[96,640]{1,0:T(8,128)(2,1)S(1)} %fusion.5), channel_id=1, source_target_pairs={{0,384},{1,129},{128,256},{129,1},{256,128},{257,385},{384,0},{385... | collective-permute-start | bytes 368648 | tf_op jit(solution)/shard_map/ppermute | solution.py:15
  127.4 0.0 collective-permute-done.13
  127.4 7.2 %collective-permute-done.15 = bf16[96,640]{1,0:T(8,128)(2,1)S(1)} collective-permute-done((bf16[96,640]{1,0:T(8,128)(2,1)S(1)}, bf16[96,640]{1,0:T(8,128)(2,1)S(1)}, u32[]{:S(2)}, u32[]{:S(2)}) %collective-permute-start.15) | collective-permute-done | bytes 122912 | tf_op jit(solution)/shard_map/ppermute | solution.py:15
  134.6 0.1 fusion.3
  134.7 0.7 pad_maximum_fusion.2
  (14 shorter events, 0.3 us)
Async XLA Ops:
  21.1 23.3 %collective-permute-start.6 = (bf16[384,384]{1,0:T(8,128)(2,1)S(1)}, bf16[384,384]{1,0:T(8,128)(2,1)S(1)}, u32[]{:S(2)}, u32[]{:S(2)}) collective-permute-start(bf16[384,384]{1,0:T(8,128)(2,1)S(1)} %slice.35.refs_0_), channel_id=1, source_target_pairs={{0,24},{1,25},{8,0},{9,1},{16,8},{17,9},{24,16},{25,17},{2,26},{3,... | collective-permute-start | bytes 884744 | tf_op jit(solution)/shard_map/ppermute | solution.py:15
  23.8 24.9 %collective-permute-start.7 = (bf16[384,384]{1,0:T(8,128)(2,1)S(1)}, bf16[384,384]{1,0:T(8,128)(2,1)S(1)}, u32[]{:S(2)}, u32[]{:S(2)}) collective-permute-start(bf16[384,384]{1,0:T(8,128)(2,1)S(1)} %slice.35.refs_0_), channel_id=1, source_target_pairs={{0,16},{1,17},{8,24},{9,25},{16,0},{17,1},{24,8},{25,9},{2,18},{3,... | collective-permute-start | bytes 884744 | tf_op jit(solution)/shard_map/ppermute | solution.py:15
  26.9 21.9 %collective-permute-start.8 = (bf16[384,384]{1,0:T(8,128)(2,1)S(1)}, bf16[384,384]{1,0:T(8,128)(2,1)S(1)}, u32[]{:S(2)}, u32[]{:S(2)}) collective-permute-start(bf16[384,384]{1,0:T(8,128)(2,1)S(1)} %slice.35.refs_0_), channel_id=1, source_target_pairs={{0,8},{1,9},{8,16},{9,17},{16,24},{17,25},{24,0},{25,1},{2,10},{3,... | collective-permute-start | bytes 884744 | tf_op jit(solution)/shard_map/ppermute | solution.py:15
  30.9 28.2 %collective-permute-start = (bf16[384,640]{1,0:T(8,128)(2,1)S(1)}, bf16[384,640]{1,0:T(8,128)(2,1)S(1)}, u32[]{:S(2)}, u32[]{:S(2)}) collective-permute-start(bf16[384,640]{1,0:T(8,128)(2,1)S(1)} %slice.34.refs_0_), channel_id=1, source_target_pairs={{0,24},{1,25},{8,0},{9,1},{16,8},{17,9},{24,16},{25,17},{2,26},{3,... | collective-permute-start | bytes 1474568 | tf_op jit(solution)/shard_map/ppermute | solution.py:15
  32.9 29.2 %collective-permute-start.1 = (bf16[384,640]{1,0:T(8,128)(2,1)S(1)}, bf16[384,640]{1,0:T(8,128)(2,1)S(1)}, u32[]{:S(2)}, u32[]{:S(2)}) collective-permute-start(bf16[384,640]{1,0:T(8,128)(2,1)S(1)} %slice.34.refs_0_), channel_id=1, source_target_pairs={{0,16},{1,17},{8,24},{9,25},{16,0},{17,1},{24,8},{25,9},{2,18},{3,... | collective-permute-start | bytes 1474568 | tf_op jit(solution)/shard_map/ppermute | solution.py:15
  38.2 0.7 copy-start
  44.4 17.8 %collective-permute-start.2 = (bf16[384,640]{1,0:T(8,128)(2,1)S(1)}, bf16[384,640]{1,0:T(8,128)(2,1)S(1)}, u32[]{:S(2)}, u32[]{:S(2)}) collective-permute-start(bf16[384,640]{1,0:T(8,128)(2,1)S(1)} %slice.34.refs_0_), channel_id=1, source_target_pairs={{0,8},{1,9},{8,16},{9,17},{16,24},{17,25},{24,0},{25,1},{2,10},{3,... | collective-permute-start | bytes 1474568 | tf_op jit(solution)/shard_map/ppermute | solution.py:15
  51.1 24.7 %collective-permute-start.10 = (bf16[384,384]{1,0:T(8,128)(2,1)S(1)}, bf16[384,384]{1,0:T(8,128)(2,1)S(1)}, u32[]{:S(2)}, u32[]{:S(2)}) collective-permute-start(bf16[384,384]{1,0:T(8,128)(2,1)S(1)} %get-tuple-element.24), channel_id=1, source_target_pairs={{0,32},{1,33},{32,64},{33,65},{64,96},{65,97},{96,0},{97,1},{2,34}... | collective-permute-start | bytes 884744 | tf_op jit(solution)/shard_map/ppermute | solution.py:15
  54.3 24.1 %collective-permute-start.9 = (bf16[384,384]{1,0:T(8,128)(2,1)S(1)}, bf16[384,384]{1,0:T(8,128)(2,1)S(1)}, u32[]{:S(2)}, u32[]{:S(2)}) collective-permute-start(bf16[384,384]{1,0:T(8,128)(2,1)S(1)} %get-tuple-element.23), channel_id=1, source_target_pairs={{0,64},{1,65},{32,96},{33,97},{64,0},{65,1},{96,32},{97,33},{2,66}... | collective-permute-start | bytes 884744 | tf_op jit(solution)/shard_map/ppermute | solution.py:15
  59.1 19.3 %collective-permute-start.11 = (bf16[384,384]{1,0:T(8,128)(2,1)S(1)}, bf16[384,384]{1,0:T(8,128)(2,1)S(1)}, u32[]{:S(2)}, u32[]{:S(2)}) collective-permute-start(bf16[384,384]{1,0:T(8,128)(2,1)S(1)} %slice_bitcast_fusion.4), channel_id=1, source_target_pairs={{0,96},{1,97},{32,0},{33,1},{64,32},{65,33},{96,64},{97,65},{2,98}... | collective-permute-start | bytes 884744 | tf_op jit(solution)/shard_map/ppermute | solution.py:15
  67.5 27.8 %collective-permute-start.3 = (bf16[384,640]{1,0:T(8,128)(2,1)S(1)}, bf16[384,640]{1,0:T(8,128)(2,1)S(1)}, u32[]{:S(2)}, u32[]{:S(2)}) collective-permute-start(bf16[384,640]{1,0:T(8,128)(2,1)S(1)} %get-tuple-element.21), channel_id=1, source_target_pairs={{0,64},{1,65},{32,96},{33,97},{64,0},{65,1},{96,32},{97,33},{2,66}... | collective-permute-start | bytes 1474568 | tf_op jit(solution)/shard_map/ppermute | solution.py:15
  72.6 22.8 %collective-permute-start.4 = (bf16[384,640]{1,0:T(8,128)(2,1)S(1)}, bf16[384,640]{1,0:T(8,128)(2,1)S(1)}, u32[]{:S(2)}, u32[]{:S(2)}) collective-permute-start(bf16[384,640]{1,0:T(8,128)(2,1)S(1)} %get-tuple-element.20), channel_id=1, source_target_pairs={{0,32},{1,33},{32,64},{33,65},{64,96},{65,97},{96,0},{97,1},{2,34}... | collective-permute-start | bytes 1474568 | tf_op jit(solution)/shard_map/ppermute | solution.py:15
  75.8 19.6 %collective-permute-start.5 = (bf16[384,640]{1,0:T(8,128)(2,1)S(1)}, bf16[384,640]{1,0:T(8,128)(2,1)S(1)}, u32[]{:S(2)}, u32[]{:S(2)}) collective-permute-start(bf16[384,640]{1,0:T(8,128)(2,1)S(1)} %get-tuple-element.19), channel_id=1, source_target_pairs={{0,96},{1,97},{32,0},{33,1},{64,32},{65,33},{96,64},{97,65},{2,98}... | collective-permute-start | bytes 1474568 | tf_op jit(solution)/shard_map/ppermute | solution.py:15
  78.7 16.6 %collective-permute-start.12 = (bf16[2,96,384]{2,1,0:T(8,128)(2,1)S(1)}, bf16[2,96,384]{2,1,0:T(8,128)(2,1)S(1)}, u32[]{:S(2)}, u32[]{:S(2)}) collective-permute-start(bf16[2,96,384]{2,1,0:T(8,128)(2,1)S(1)} %pad_maximum_fusion.3), channel_id=1, source_target_pairs={{0,128},{1,385},{128,0},{129,257},{256,384},{257,129},{384,256},{3... | collective-permute-start | bytes 442376 | tf_op jit(solution)/shard_map/ppermute | solution.py:15
  95.7 28.2 %collective-permute-start.14 = (bf16[2,96,640]{2,1,0:T(8,128)(2,1)S(1)}, bf16[2,96,640]{2,1,0:T(8,128)(2,1)S(1)}, u32[]{:S(2)}, u32[]{:S(2)}) collective-permute-start(bf16[2,96,640]{2,1,0:T(8,128)(2,1)S(1)} %pad_maximum_fusion.1), channel_id=1, source_target_pairs={{0,128},{1,385},{128,0},{129,257},{256,384},{257,129},{384,256},{3... | collective-permute-start | bytes 737288 | tf_op jit(solution)/shard_map/ppermute | solution.py:15
  99.6 27.7 %collective-permute-start.13 = (bf16[96,384]{1,0:T(8,128)(2,1)S(1)}, bf16[96,384]{1,0:T(8,128)(2,1)S(1)}, u32[]{:S(2)}, u32[]{:S(2)}) collective-permute-start(bf16[96,384]{1,0:T(8,128)(2,1)S(1)} %fusion.6), channel_id=1, source_target_pairs={{0,384},{1,129},{128,256},{129,1},{256,128},{257,385},{384,0},{385... | collective-permute-start | bytes 221192 | tf_op jit(solution)/shard_map/ppermute | solution.py:15
  123.9 10.7 %collective-permute-start.15 = (bf16[96,640]{1,0:T(8,128)(2,1)S(1)}, bf16[96,640]{1,0:T(8,128)(2,1)S(1)}, u32[]{:S(2)}, u32[]{:S(2)}) collective-permute-start(bf16[96,640]{1,0:T(8,128)(2,1)S(1)} %fusion.5), channel_id=1, source_target_pairs={{0,384},{1,129},{128,256},{129,1},{256,128},{257,385},{384,0},{385... | collective-permute-start | bytes 368648 | tf_op jit(solution)/shard_map/ppermute | solution.py:15
